TPU v7x, 32 devices: a whole 2x2x4 slice. The times are simulated.
32 devices in a mesh: seq: 4 (over y, x), row: 8 (over z, core).
Axes of the slice: x: 2, y: 2, z: 4, core: 2. Of those that a mesh axis runs over, the one named last changes fastest.
Arguments:
- tokens: bfloat16 [2, 1024, 3072], P(None, ('seq', 'row')), may hold values from -6 to 6
- w_qkv: bfloat16 [1536, 3072], P('row'), may hold values from -0.109375 to 0.109375
- w_rate: bfloat16 [8, 3072], P('row'), may hold values from -0.109375 to 0.109375
- rate_bias: float32 [8], P('row'), may hold values from -3 to 1
- w_out: bfloat16 [512, 3072], P('row'), may hold values from -0.25 to 0.25
- w_first_init: float32 [8, 64, 256], P('row'), may hold values from -0.75 to 0.75
- b_first_init: float32 [8, 256], P('row'), may hold values from -3 to 3
- w_second_init: float32 [8, 256, 64], P('row'), may hold values from -0.375 to 0.375
- b_second_init: float32 [8, 64], P('row'), may hold values from -3 to 3
- ln_gain: float32 [8, 64], P('row'), may hold values from 0.5 to 1.5
- ln_bias: float32 [8, 64], P('row'), may hold values from -3 to 3
Outputs:
- mixed: bfloat16 [2, 1024, 3072], P(None, ('seq', 'row'))
All inputs are finite; a program needn't handle non-finite values.
Results may differ from a plain program's by a relative error of at most 0.0056.
Values may be sent and summed in bfloat16 or wider, within the bound.
No kernel may reach another device: no remote copies, remote signals or barrier semaphores. Data moves between devices by JAX's collectives and lax.ppermute only.
A program may use at most 64 MiB of HBM per device.

v0:
```python
from functools import partial

import jax
import jax.numpy as jnp
from jax import lax
from jax.sharding import PartitionSpec as P

MINI = 64


gelu_coef = 0.7978845608028654
base_rate = 0.01
ln_eps = 1e-06


def passed_along(array, axis, by):
    size = lax.axis_size(axis)
    pairs = [(i, i + by) for i in range(size) if 0 <= i + by < size]
    return lax.ppermute(array, axis, pairs)


def gelu_tanh(entries):
    tanh_arg = gelu_coef * (entries + 0.044715 * entries * entries * entries)
    return 0.5 * entries * (1.0 + jnp.tanh(tanh_arg))


def gelu_slope(entries):
    tanh_arg = gelu_coef * (entries + 0.044715 * entries * entries * entries)
    tangent = jnp.tanh(tanh_arg)
    return 0.5 * (1.0 + tangent) + 0.5 * entries * (1.0 - tangent * tangent) * gelu_coef * (
        1.0 + 3.0 * 0.044715 * entries * entries
    )


def matmul(left, right):
    return jnp.dot(left, right, precision=lax.Precision.HIGHEST, preferred_element_type=jnp.float32)


def normalize(entries):
    centred = entries - jnp.mean(entries, axis=-1, keepdims=True)
    spread = jnp.sqrt(jnp.mean(centred * centred, axis=-1, keepdims=True) + ln_eps)
    return (centred / spread, spread)


def mini_step(inner_state, batch_block, norm_gain, offset):
    w_first, b_first, w_second, b_second = inner_state
    queries, key_rows, value_rows, lr_rows = batch_block
    mini_len = queries.shape[0]
    hidden_pre = matmul(key_rows, w_first) + b_first
    hidden = gelu_tanh(hidden_pre)
    second = matmul(hidden, w_second) + b_second
    target = value_rows - key_rows
    normed, spread = normalize(second)
    grad_out = norm_gain * (norm_gain * normed + offset - target)
    feat_width = second.shape[-1]
    grad_second = (
        feat_width * grad_out
        - jnp.sum(grad_out, axis=-1, keepdims=True)
        - normed * jnp.sum(grad_out * normed, axis=-1, keepdims=True)
    ) / (feat_width * spread)
    grad_first = matmul(grad_second, w_second.T) * gelu_slope(hidden_pre)
    tri_mask = jnp.tril(jnp.ones((mini_len, mini_len), jnp.float32))
    eta_last = lr_rows / mini_len
    eta_table = tri_mask * eta_last[None, :]
    query_keys = matmul(queries, key_rows.T) * eta_table
    bias_first = b_first - matmul(eta_table, grad_first)
    first_bar = matmul(queries, w_first) - matmul(query_keys, grad_first) + bias_first
    hidden_bar = gelu_tanh(first_bar)
    hidden_pairs = matmul(hidden_bar, hidden.T) * eta_table
    bias_second = b_second - matmul(eta_table, grad_second)
    second_bar = matmul(hidden_bar, w_second) - matmul(hidden_pairs, grad_second) + bias_second
    w_first = w_first - matmul((key_rows * eta_last[:, None]).T, grad_first)
    b_first = b_first - matmul(eta_last[None, :], grad_first)[0]
    w_second = w_second - matmul((hidden * eta_last[:, None]).T, grad_second)
    b_second = b_second - matmul(eta_last[None, :], grad_second)[0]
    normed_bar, spread_bar = normalize(second_bar)
    result = queries + norm_gain * normed_bar + offset
    return ((w_first, b_first, w_second, b_second), result)


def run_blocks(inner_state, queries, key_rows, value_rows, lr_rows, norm_gain, offset, mini_len):
    block_count = queries.shape[0] // mini_len
    blocks = (
        queries.reshape(block_count, mini_len, -1),
        key_rows.reshape(block_count, mini_len, -1),
        value_rows.reshape(block_count, mini_len, -1),
        lr_rows.reshape(block_count, mini_len),
    )

    def advance(loop_carry, batch_block):
        return mini_step(loop_carry, batch_block, norm_gain, offset)

    inner_state, results = lax.scan(advance, inner_state, blocks)
    return (inner_state, results.reshape(queries.shape[0], -1))


def on_device(
    tokens,
    w_qkv,
    w_rate,
    rate_bias,
    w_out,
    w_first_init,
    b_first_init,
    w_second_init,
    b_second_init,
    ln_gain,
    ln_bias,
):
    videos, tok_part, feat_width = tokens.shape
    proj_width = w_qkv.shape[0]
    head_size = proj_width // 3
    full_out = lax.all_gather(w_out, "row", axis=0, tiled=True)
    stacked = jnp.concatenate([w_qkv, w_rate], axis=0)
    combined = jnp.einsum(
        "vkd,cd->vkc",
        lax.all_gather(tokens, "row", axis=1, tiled=True),
        stacked,
        preferred_element_type=jnp.float32,
    )
    projected = lax.optimization_barrier(combined[:, :, :proj_width].astype(jnp.bfloat16)).astype(
        jnp.float32
    )
    queries = projected[:, :, :head_size]
    key_rows = projected[:, :, head_size : 2 * head_size]
    value_rows = projected[:, :, 2 * head_size :]
    lr_rows = base_rate * jax.nn.sigmoid(combined[:, :, proj_width] + rate_bias[0])
    initial = (w_first_init[0], b_first_init[0], w_second_init[0], b_second_init[0])
    norm_gain = ln_gain[0]
    offset = ln_bias[0]

    def segment(inner_state, video_q, video_k, video_v, video_lr):
        return run_blocks(inner_state, video_q, video_k, video_v, video_lr, norm_gain, offset, MINI)

    seq_count = lax.axis_size("seq")
    seq_place = lax.axis_index("seq")
    first_device = seq_place == 0

    def spread_videos(entries):
        return jnp.broadcast_to(entries, (videos,) + entries.shape)

    start_states = jax.tree.map(spread_videos, initial)
    incoming = start_states
    for turn_idx in range(seq_count):
        finals, results = jax.vmap(segment)(incoming, queries, key_rows, value_rows, lr_rows)
        if turn_idx + 1 < seq_count:
            received = passed_along(finals, "seq", 1)
            incoming = jax.tree.map(partial(jnp.where, first_device), start_states, received)
    heads_rows = results.astype(jnp.bfloat16)
    arrived = lax.all_to_all(heads_rows, "row", split_axis=1, concat_axis=2, tiled=True)
    mixed_out = jnp.einsum(
        "vkc,cd->vkd", arrived, full_out, preferred_element_type=jnp.float32
    ).astype(jnp.bfloat16)
    return mixed_out


def solution(mesh):
    in_specs = (
        P(None, ("seq", "row"), None),
        P("row", None),
        P("row", None),
        P("row"),
        P("row", None),
        P("row", None, None),
        P("row", None),
        P("row", None, None),
        P("row", None),
        P("row", None),
        P("row", None),
    )
    out_specs = P(None, ("seq", "row"), None)
    return jax.shard_map(
        on_device, mesh=mesh, in_specs=in_specs, out_specs=out_specs, check_vma=False
    )
```

profile of v0, /device:TPU:0, one launch (start us, length us, event | category | flops | bytes accessed | tf_op | source)
XLA Modules:
  0.0 166.1 jit_solution(2275118484235889921)
XLA Ops:
  6.5 0.7 all-gather.3.cloned.1.call-update
  8.0 42.0 %all-gather.3.cloned.1.call-done = bf16[2,256,3072]{2,1,0:T(8,128)(2,1)} async-done(((bf16[2,32,3072]{2,1,0:T(8,128)(2,1)}), bf16[2,256,3072]{2,1,0:T(8,128)(2,1)}) %all-gather.3.cloned.1.call-update) | async-done | bytes 3145744 | tf_op jit(solution)/shard_map/all_gather | solution.py:117
  50.0 3.4 %fusion.112 = f32[2,256,193]{1,2,0:T(8,128)S(1)} fusion(bf16[2,256,3072]{2,1,0:T(8,128)(2,1)} %all-gather.3.cloned.1.call-done, bf16[1,3072]{1,0:T(2,128)(2,1)} %param.21, bf16[192,3072]{1,0:T(8,128)(2,1)} %param.20), kind=kOutput, calls=%fused_computation.203 | convolution fusion | flops 609497088 | bytes 4726784 | tf_op jit(solution)/shard_map/vkd,cd->vkc/dot_general | solution.py:115
  54.4 10.8 %while.66 = (s32[]{:T(128)}, f32[2,64,256]{2,1,0:T(8,128)S(1)}, f32[2,256]{1,0:T(2,128)S(1)}, f32[2,256,64]{1,2,0:T(8,128)S(1)}, f32[2,64]{1,0:T(2,128)S(1)}, /*...) while((s32[]{:T(128)}, f32[2,64,256]{2,1,0:T(8,128)S(1)}, ...), condition=%wide.region_5.6_spmd, body=%wide.region_0.5_spmd.sunk | while | flops 127755136 | bytes 2386049 | solution.py:93
  56.3 0.4 convolution_subtract_fusion.22
  61.7 0.4 convolution_subtract_fusion.22
  65.2 3.4 %collective-permute-start.3 = (f32[2,64]{1,0:T(2,128)S(1)}, f32[2,64]{1,0:T(2,128)S(1)}, u32[]{:S(2)}, u32[]{:S(2)}) collective-permute-start(f32[2,64]{1,0:T(2,128)S(1)} %get-tuple-element.235), channel_id=1, source_target_pairs={{0,8},{8,16},{16,24},{1,9},{9,17},{17,25},{2,10},{10,18},{18,26},{... | collective-permute-start | bytes 1544 | tf_op jit(solution)/shard_map/ppermute | solution.py:19
  68.6 3.4 %collective-permute-start.2 = (f32[2,256,64]{1,2,0:T(8,128)S(1)}, f32[2,256,64]{1,2,0:T(8,128)S(1)}, u32[]{:S(2)}, u32[]{:S(2)}) collective-permute-start(f32[2,256,64]{1,2,0:T(8,128)S(1)} %get-tuple-element.234), channel_id=1, source_target_pairs={{0,8},{8,16},{16,24},{1,9},{9,17},{17,25},{2,10},{10,18},{18,26},{... | collective-permute-start | bytes 393224 | tf_op jit(solution)/shard_map/ppermute | solution.py:19
  72.0 3.4 %collective-permute-start = (f32[2,64,256]{2,1,0:T(8,128)S(1)}, f32[2,64,256]{2,1,0:T(8,128)S(1)}, u32[]{:S(2)}, u32[]{:S(2)}) collective-permute-start(f32[2,64,256]{2,1,0:T(8,128)S(1)} %get-tuple-element.232), channel_id=1, source_target_pairs={{0,8},{8,16},{16,24},{1,9},{9,17},{17,25},{2,10},{10,18},{18,26},{... | collective-permute-start | bytes 393224 | tf_op jit(solution)/shard_map/ppermute | solution.py:19
  75.4 1.9 %collective-permute-start.1 = (f32[2,256]{1,0:T(2,128)S(1)}, f32[2,256]{1,0:T(2,128)S(1)}, u32[]{:S(2)}, u32[]{:S(2)}) collective-permute-start(f32[2,256]{1,0:T(2,128)S(1)} %get-tuple-element.233), channel_id=1, source_target_pairs={{0,8},{8,16},{16,24},{1,9},{9,17},{17,25},{2,10},{10,18},{18,26},{... | collective-permute-start | bytes 6152 | tf_op jit(solution)/shard_map/ppermute | solution.py:19
  77.3 1.3 collective-permute-done.1
  78.7 10.8 %while.67 = (s32[]{:T(128)}, f32[2,64,256]{2,1,0:T(8,128)S(1)}, f32[2,256]{1,0:T(2,128)S(1)}, f32[2,256,64]{1,2,0:T(8,128)S(1)}, f32[2,64]{1,0:T(2,128)S(1)}, /*...) while((s32[]{:T(128)}, f32[2,64,256]{2,1,0:T(8,128)S(1)}, ...), condition=%wide.region_11.12_spmd, body=%wide.region_6.11_spmd.sunk | while | flops 127755136 | bytes 2386049 | solution.py:93
  80.6 0.4 convolution_subtract_fusion.24
  86.0 0.4 convolution_subtract_fusion.24
  89.5 4.2 %collective-permute-start.7 = (f32[2,64]{1,0:T(2,128)S(1)}, f32[2,64]{1,0:T(2,128)S(1)}, u32[]{:S(2)}, u32[]{:S(2)}) collective-permute-start(f32[2,64]{1,0:T(2,128)S(1)} %get-tuple-element.239), channel_id=1, source_target_pairs={{0,8},{8,16},{16,24},{1,9},{9,17},{17,25},{2,10},{10,18},{18,26},{... | collective-permute-start | bytes 1544 | tf_op jit(solution)/shard_map/ppermute | solution.py:19
  93.7 3.6 %collective-permute-start.6 = (f32[2,256,64]{1,2,0:T(8,128)S(1)}, f32[2,256,64]{1,2,0:T(8,128)S(1)}, u32[]{:S(2)}, u32[]{:S(2)}) collective-permute-start(f32[2,256,64]{1,2,0:T(8,128)S(1)} %get-tuple-element.238), channel_id=1, source_target_pairs={{0,8},{8,16},{16,24},{1,9},{9,17},{17,25},{2,10},{10,18},{18,26},{... | collective-permute-start | bytes 393224 | tf_op jit(solution)/shard_map/ppermute | solution.py:19
  97.3 1.9 %collective-permute-start.4 = (f32[2,64,256]{2,1,0:T(8,128)S(1)}, f32[2,64,256]{2,1,0:T(8,128)S(1)}, u32[]{:S(2)}, u32[]{:S(2)}) collective-permute-start(f32[2,64,256]{2,1,0:T(8,128)S(1)} %get-tuple-element.236), channel_id=1, source_target_pairs={{0,8},{8,16},{16,24},{1,9},{9,17},{17,25},{2,10},{10,18},{18,26},{... | collective-permute-start | bytes 393224 | tf_op jit(solution)/shard_map/ppermute | solution.py:19
  99.2 1.9 %collective-permute-start.5 = (f32[2,256]{1,0:T(2,128)S(1)}, f32[2,256]{1,0:T(2,128)S(1)}, u32[]{:S(2)}, u32[]{:S(2)}) collective-permute-start(f32[2,256]{1,0:T(2,128)S(1)} %get-tuple-element.237), channel_id=1, source_target_pairs={{0,8},{8,16},{16,24},{1,9},{9,17},{17,25},{2,10},{10,18},{18,26},{... | collective-permute-start | bytes 6152 | tf_op jit(solution)/shard_map/ppermute | solution.py:19
  101.2 1.3 collective-permute-done.5
  102.6 10.8 %while.68 = (s32[]{:T(128)}, f32[2,64,256]{2,1,0:T(8,128)S(1)}, f32[2,256]{1,0:T(2,128)S(1)}, f32[2,256,64]{1,2,0:T(8,128)S(1)}, f32[2,64]{1,0:T(2,128)S(1)}, /*...) while((s32[]{:T(128)}, f32[2,64,256]{2,1,0:T(8,128)S(1)}, ...), condition=%wide.region_17.18_spmd, body=%wide.region_12.17_spmd.sunk | while | flops 127755136 | bytes 2386049 | solution.py:93
  104.5 0.4 convolution_subtract_fusion.26
  107.2 0.4 convolution_subtract_fusion.26
  109.9 0.4 convolution_subtract_fusion.26
  112.6 0.4 convolution_subtract_fusion.26
  113.4 4.4 %collective-permute-start.11 = (f32[2,64]{1,0:T(2,128)S(1)}, f32[2,64]{1,0:T(2,128)S(1)}, u32[]{:S(2)}, u32[]{:S(2)}) collective-permute-start(f32[2,64]{1,0:T(2,128)S(1)} %get-tuple-element.243), channel_id=1, source_target_pairs={{0,8},{8,16},{16,24},{1,9},{9,17},{17,25},{2,10},{10,18},{18,26},{... | collective-permute-start | bytes 1544 | tf_op jit(solution)/shard_map/ppermute | solution.py:19
  118.1 2.9 %collective-permute-start.10 = (f32[2,256,64]{1,2,0:T(8,128)S(1)}, f32[2,256,64]{1,2,0:T(8,128)S(1)}, u32[]{:S(2)}, u32[]{:S(2)}) collective-permute-start(f32[2,256,64]{1,2,0:T(8,128)S(1)} %get-tuple-element.242), channel_id=1, source_target_pairs={{0,8},{8,16},{16,24},{1,9},{9,17},{17,25},{2,10},{10,18},{18,26},{... | collective-permute-start | bytes 393224 | tf_op jit(solution)/shard_map/ppermute | solution.py:19
  121.0 1.9 %collective-permute-start.8 = (f32[2,64,256]{2,1,0:T(8,128)S(1)}, f32[2,64,256]{2,1,0:T(8,128)S(1)}, u32[]{:S(2)}, u32[]{:S(2)}) collective-permute-start(f32[2,64,256]{2,1,0:T(8,128)S(1)} %get-tuple-element.240), channel_id=1, source_target_pairs={{0,8},{8,16},{16,24},{1,9},{9,17},{17,25},{2,10},{10,18},{18,26},{... | collective-permute-start | bytes 393224 | tf_op jit(solution)/shard_map/ppermute | solution.py:19
  122.9 1.9 %collective-permute-start.9 = (f32[2,256]{1,0:T(2,128)S(1)}, f32[2,256]{1,0:T(2,128)S(1)}, u32[]{:S(2)}, u32[]{:S(2)}) collective-permute-start(f32[2,256]{1,0:T(2,128)S(1)} %get-tuple-element.241), channel_id=1, source_target_pairs={{0,8},{8,16},{16,24},{1,9},{9,17},{17,25},{2,10},{10,18},{18,26},{... | collective-permute-start | bytes 6152 | tf_op jit(solution)/shard_map/ppermute | solution.py:19
  124.9 1.3 collective-permute-done.9
  126.2 20.8 %while.69 = (s32[]{:T(128)}, f32[2,64,256]{2,1,0:T(8,128)S(1)}, f32[2,256]{1,0:T(2,128)S(1)}, f32[2,256,64]{1,2,0:T(8,128)S(1)}, f32[2,64]{1,0:T(2,128)S(1)}, /*...) while((s32[]{:T(128)}, f32[2,64,256]{2,1,0:T(8,128)S(1)}, ...), condition=%wide.region_25.26_spmd, body=%wide.region_18.25_spmd.sunk | while | flops 273236992 | bytes 4856473 | solution.py:93
  147.3 8.3 %all_to_all.18 = bf16[8,2,2048]{2,1,0:T(2,128)(2,1)S(1)} all-to-all(bf16[8,2,2048]{2,1,0:T(2,128)(2,1)S(1)} %reshape.226), channel_id=1, replica_groups=mesh['seq'=4,'row'=8] {'row'}, dimensions={0} | all-to-all | bytes 131072 | tf_op jit(solution)/shard_map/all_to_all | solution.py:150
  156.0 3.3 %convolution_convert_fusion = bf16[2,32,3072]{2,1,0:T(8,128)(2,1)} fusion(bf16[2,32,512]{2,1,0:T(8,128)(2,1)S(1)} %all_to_all.16, bf16[512,3072]{1,0:T(8,128)(2,1)} %all-gather.5.cloned.1.call-done), kind=kOutput, calls=%fused_computation.197 | convolution fusion | flops 201523200 | bytes 3604480 | tf_op jit(solution)/shard_map/vkc,cd->vkd/dot_general | solution.py:151
  (359 shorter events, 50.5 us)
Async XLA Ops:
  6.5 43.4 %all-gather.3.cloned.1.call-start = ((), (), s32[]{:S(2)}) async-start(), calls=%async_computation.1 | async-start | bytes 3538944 | tf_op jit(solution)/shard_map/all_gather | solution.py:117
  7.3 148.7 %all-gather.5.cloned.1.call-start = ((), (), s32[]{:S(2)}) async-start(), calls=%async_computation.2 | async-start | bytes 3538944 | tf_op jit(solution)/shard_map/all_gather | solution.py:113
  53.4 0.9 copy-start.1
  53.4 0.9 copy-start
  53.4 0.9 copy-start.4
  53.5 0.9 copy-start.5
  53.5 0.9 copy-start.2
  53.5 0.9 copy-start.3
  65.2 12.1 %collective-permute-start.3 = (f32[2,64]{1,0:T(2,128)S(1)}, f32[2,64]{1,0:T(2,128)S(1)}, u32[]{:S(2)}, u32[]{:S(2)}) collective-permute-start(f32[2,64]{1,0:T(2,128)S(1)} %get-tuple-element.235), channel_id=1, source_target_pairs={{0,8},{8,16},{16,24},{1,9},{9,17},{17,25},{2,10},{10,18},{18,26},{... | collective-permute-start | bytes 1544 | tf_op jit(solution)/shard_map/ppermute | solution.py:19
  68.6 10.0 %collective-permute-start.2 = (f32[2,256,64]{1,2,0:T(8,128)S(1)}, f32[2,256,64]{1,2,0:T(8,128)S(1)}, u32[]{:S(2)}, u32[]{:S(2)}) collective-permute-start(f32[2,256,64]{1,2,0:T(8,128)S(1)} %get-tuple-element.234), channel_id=1, source_target_pairs={{0,8},{8,16},{16,24},{1,9},{9,17},{17,25},{2,10},{10,18},{18,26},{... | collective-permute-start | bytes 393224 | tf_op jit(solution)/shard_map/ppermute | solution.py:19
  72.0 6.6 %collective-permute-start = (f32[2,64,256]{2,1,0:T(8,128)S(1)}, f32[2,64,256]{2,1,0:T(8,128)S(1)}, u32[]{:S(2)}, u32[]{:S(2)}) collective-permute-start(f32[2,64,256]{2,1,0:T(8,128)S(1)} %get-tuple-element.232), channel_id=1, source_target_pairs={{0,8},{8,16},{16,24},{1,9},{9,17},{17,25},{2,10},{10,18},{18,26},{... | collective-permute-start | bytes 393224 | tf_op jit(solution)/shard_map/ppermute | solution.py:19
  75.4 3.2 %collective-permute-start.1 = (f32[2,256]{1,0:T(2,128)S(1)}, f32[2,256]{1,0:T(2,128)S(1)}, u32[]{:S(2)}, u32[]{:S(2)}) collective-permute-start(f32[2,256]{1,0:T(2,128)S(1)} %get-tuple-element.233), channel_id=1, source_target_pairs={{0,8},{8,16},{16,24},{1,9},{9,17},{17,25},{2,10},{10,18},{18,26},{... | collective-permute-start | bytes 6152 | tf_op jit(solution)/shard_map/ppermute | solution.py:19
  89.5 11.7 %collective-permute-start.7 = (f32[2,64]{1,0:T(2,128)S(1)}, f32[2,64]{1,0:T(2,128)S(1)}, u32[]{:S(2)}, u32[]{:S(2)}) collective-permute-start(f32[2,64]{1,0:T(2,128)S(1)} %get-tuple-element.239), channel_id=1, source_target_pairs={{0,8},{8,16},{16,24},{1,9},{9,17},{17,25},{2,10},{10,18},{18,26},{... | collective-permute-start | bytes 1544 | tf_op jit(solution)/shard_map/ppermute | solution.py:19
  93.7 8.8 %collective-permute-start.6 = (f32[2,256,64]{1,2,0:T(8,128)S(1)}, f32[2,256,64]{1,2,0:T(8,128)S(1)}, u32[]{:S(2)}, u32[]{:S(2)}) collective-permute-start(f32[2,256,64]{1,2,0:T(8,128)S(1)} %get-tuple-element.238), channel_id=1, source_target_pairs={{0,8},{8,16},{16,24},{1,9},{9,17},{17,25},{2,10},{10,18},{18,26},{... | collective-permute-start | bytes 393224 | tf_op jit(solution)/shard_map/ppermute | solution.py:19
  97.3 5.2 %collective-permute-start.4 = (f32[2,64,256]{2,1,0:T(8,128)S(1)}, f32[2,64,256]{2,1,0:T(8,128)S(1)}, u32[]{:S(2)}, u32[]{:S(2)}) collective-permute-start(f32[2,64,256]{2,1,0:T(8,128)S(1)} %get-tuple-element.236), channel_id=1, source_target_pairs={{0,8},{8,16},{16,24},{1,9},{9,17},{17,25},{2,10},{10,18},{18,26},{... | collective-permute-start | bytes 393224 | tf_op jit(solution)/shard_map/ppermute | solution.py:19
  99.2 3.3 %collective-permute-start.5 = (f32[2,256]{1,0:T(2,128)S(1)}, f32[2,256]{1,0:T(2,128)S(1)}, u32[]{:S(2)}, u32[]{:S(2)}) collective-permute-start(f32[2,256]{1,0:T(2,128)S(1)} %get-tuple-element.237), channel_id=1, source_target_pairs={{0,8},{8,16},{16,24},{1,9},{9,17},{17,25},{2,10},{10,18},{18,26},{... | collective-permute-start | bytes 6152 | tf_op jit(solution)/shard_map/ppermute | solution.py:19
  113.4 11.5 %collective-permute-start.11 = (f32[2,64]{1,0:T(2,128)S(1)}, f32[2,64]{1,0:T(2,128)S(1)}, u32[]{:S(2)}, u32[]{:S(2)}) collective-permute-start(f32[2,64]{1,0:T(2,128)S(1)} %get-tuple-element.243), channel_id=1, source_target_pairs={{0,8},{8,16},{16,24},{1,9},{9,17},{17,25},{2,10},{10,18},{18,26},{... | collective-permute-start | bytes 1544 | tf_op jit(solution)/shard_map/ppermute | solution.py:19
  118.1 8.1 %collective-permute-start.10 = (f32[2,256,64]{1,2,0:T(8,128)S(1)}, f32[2,256,64]{1,2,0:T(8,128)S(1)}, u32[]{:S(2)}, u32[]{:S(2)}) collective-permute-start(f32[2,256,64]{1,2,0:T(8,128)S(1)} %get-tuple-element.242), channel_id=1, source_target_pairs={{0,8},{8,16},{16,24},{1,9},{9,17},{17,25},{2,10},{10,18},{18,26},{... | collective-permute-start | bytes 393224 | tf_op jit(solution)/shard_map/ppermute | solution.py:19
  121.0 5.2 %collective-permute-start.8 = (f32[2,64,256]{2,1,0:T(8,128)S(1)}, f32[2,64,256]{2,1,0:T(8,128)S(1)}, u32[]{:S(2)}, u32[]{:S(2)}) collective-permute-start(f32[2,64,256]{2,1,0:T(8,128)S(1)} %get-tuple-element.240), channel_id=1, source_target_pairs={{0,8},{8,16},{16,24},{1,9},{9,17},{17,25},{2,10},{10,18},{18,26},{... | collective-permute-start | bytes 393224 | tf_op jit(solution)/shard_map/ppermute | solution.py:19
  122.9 3.2 %collective-permute-start.9 = (f32[2,256]{1,0:T(2,128)S(1)}, f32[2,256]{1,0:T(2,128)S(1)}, u32[]{:S(2)}, u32[]{:S(2)}) collective-permute-start(f32[2,256]{1,0:T(2,128)S(1)} %get-tuple-element.241), channel_id=1, source_target_pairs={{0,8},{8,16},{16,24},{1,9},{9,17},{17,25},{2,10},{10,18},{18,26},{... | collective-permute-start | bytes 6152 | tf_op jit(solution)/shard_map/ppermute | solution.py:19
Sparse Core Ops, SparseCore 0:
  9.0 40.9 all-gather.2
  93.8 36.4 all-gather.4
where the time goes:
time: 167 us; the launch traced here: 166 us
  matrix products  47.6 us (29%)
  waiting for transfers between devices  46.7 us (28%)
  starting transfers between devices  34.8 us (21%)
  between operations  14.5 us (9%)
  other arithmetic  11 us (7%)
  blocking collectives  8.3 us (5%)
  local copies, waits for them, and re-layouts  1.75 us (1%)
    all_gather x1, waiting for transfers between devices, on_device(): lax.all_gather(tokens, 'row', axis=1, tiled=True)  42 us
    dot_general x144, matrix products, matmul(): jnp.dot(left, right, precision=lax.Precision.HIGHEST, preferred_element_t...  40.8 us
    ppermute x12, starting transfers between devices, passed_along(): return lax.ppermute(array, axis, pairs)  34.8 us
    all_to_all x1, blocking collectives, on_device(): lax.all_to_all(heads_rows, 'row', split_axis=1, concat_axis=2, tiled=True)  8.3 us
    ppermute x12, waiting for transfers between devices, passed_along(): return lax.ppermute(array, axis, pairs)  3.9 us
    reduce_sum x16, other arithmetic, mini_step(): jnp.sum(grad_out, axis=-1, keepdims=True)  3.46 us
    dot_general x1, matrix products, on_device(): jnp.einsum('vkd,cd->vkc', lax.all_gather(tokens, 'row', axis=1, tiled=Tru...  3.43 us
    reduce_sum x20, other arithmetic, normalize(): jnp.mean(centred * centred, axis=-1, keepdims=True) + ln_eps  3.34 us
  transfers between devices with their start and end apart: 14, of which 4 were waited for; matrix products, arithmetic and copies ran while one was open for 19% of the time, Pallas kernels for 0%

commit v1 on v0

v1 whole, which is shorter than its diff:
```python
from functools import partial

import jax
import jax.numpy as jnp
from jax import lax
from jax.experimental import pallas as pl
from jax.experimental.pallas import tpu as pltpu
from jax.sharding import PartitionSpec as P

MINI = 64
gelu_coef = 0.7978845608028654
gelu_cubic = 0.044715
base_rate = 0.01
ln_eps = 1e-06

f32 = jnp.float32
bf16 = jnp.bfloat16
NN = ((1,), (0,))
NT = ((1,), (1,))
TN = ((0,), (0,))


def dot(left, right, dims=NN):
    return lax.dot_general(
        left.astype(bf16), right.astype(bf16), (dims, ((), ())), preferred_element_type=f32
    )


def lane_low(shape):
    return lax.broadcasted_iota(jnp.int32, shape, len(shape) - 1) < shape[-1] // 2


def blocks(cat):
    low = lane_low(cat.shape)
    zero = jnp.zeros_like(cat)
    return jnp.concatenate([jnp.where(low, cat, zero), jnp.where(low, zero, cat)], axis=0)


def lane_cat(rows):
    half = rows.shape[0] // 2
    return jnp.where(lane_low((half, rows.shape[1])), rows[:half], rows[half:])


def project_kernel(x_ref, w_ref, wr_ref, bias_ref, kv_ref, q_ref):
    d = w_ref.shape[0] // 3
    mini = d
    weights = jnp.concatenate(
        [w_ref[...], jnp.broadcast_to(wr_ref[...], (d, wr_ref.shape[1]))], axis=0
    )
    minis = x_ref.shape[0] // (2 * mini)
    eye = (
        lax.broadcasted_iota(jnp.int32, (2 * mini, 2 * mini), 0)
        == lax.broadcasted_iota(jnp.int32, (2 * mini, 2 * mini), 1)
    ).astype(f32)
    rates = []
    for m in range(minis):
        rows = pl.ds(m * 2 * mini, 2 * mini)
        prod = dot(x_ref[rows, :], weights, NT)
        qk, vr = prod[:, : 2 * d], prod[:, 2 * d :]
        qk_swap, vr_swap = pltpu.roll(qk, d, 1), pltpu.roll(vr, d, 1)
        low = lane_low((mini, 2 * d))
        keys = jnp.where(low, qk_swap[:mini], qk[mini:])
        queries = jnp.where(low, qk[:mini], qk_swap[mini:])
        values = jnp.where(low, vr[:mini], vr_swap[mini:])
        logits = jnp.where(lane_low(vr.shape), vr_swap, vr)
        rate = base_rate * jax.nn.sigmoid(logits + bias_ref[...]) / mini
        rates.append(jnp.sum(rate * eye, axis=0, keepdims=True))
        kv_ref[pl.ds(m * 2 * mini, mini), :] = keys.astype(bf16)
        kv_ref[pl.ds(m * 2 * mini + mini, mini), :] = values.astype(bf16)
        q_ref[pl.ds(m * mini, mini), :] = queries.astype(bf16)
    rates = jnp.concatenate(rates, axis=0)
    high = rates.astype(bf16).astype(f32)
    pad = jnp.zeros((16 - 2 * minis, 2 * d), f32)
    kv_ref[pl.ds(minis * 2 * mini, 16), :] = jnp.concatenate(
        [high, rates - high, pad], axis=0
    ).astype(bf16)


def gelu_both(z):
    square = z * z
    tangent = jnp.tanh(z * (gelu_coef + (gelu_coef * gelu_cubic) * square))
    half = 0.5 * z
    value = half + half * tangent
    slope = (0.5 + 0.5 * tangent) + (half - half * (tangent * tangent)) * (
        gelu_coef + (3.0 * gelu_coef * gelu_cubic) * square
    )
    return value, slope


def gelu(z):
    tangent = jnp.tanh(z * (gelu_coef + (gelu_coef * gelu_cubic) * (z * z)))
    half = 0.5 * z
    return half + half * tangent


def chain_kernel(
    place_ref, kv_ref, q_ref, gain_ref, bias_ref, w1_ref, b1_ref, w2_ref, b2_ref, out_ref,
    w1_s, b1_s, w2_s, b2_s, z1_s,
):
    d = w1_ref.shape[1]
    inner = w1_ref.shape[2]
    mini = d
    minis = q_ref.shape[0] // mini
    both = 2 * d
    gain = jnp.concatenate([gain_ref[...], gain_ref[...]], axis=1)
    bias = jnp.concatenate([bias_ref[...], bias_ref[...]], axis=1)
    gain_sq = gain * gain
    row_id = lax.broadcasted_iota(jnp.int32, (both, both), 0)
    lane_id = lax.broadcasted_iota(jnp.int32, (both, both), 1)
    same = ((row_id < mini) == (lane_id < mini)).astype(f32)
    causal = same * (row_id >= lane_id).astype(f32)
    ones = same.astype(bf16)
    pick = (
        lax.broadcasted_iota(jnp.int32, (mini, both), 0)
        == lax.rem(lax.broadcasted_iota(jnp.int32, (mini, both), 1), mini)
    ).astype(f32)

    def per_row(pair):
        return jnp.concatenate(
            [
                jnp.broadcast_to(pair[:1], (mini, inner)),
                jnp.broadcast_to(pair[1:], (mini, inner)),
            ],
            axis=0,
        )

    def keys_of(j, m):
        return kv_ref[j, pl.ds(m * both, mini), :]

    def step(j, m, state, z1, kb, key_cat, nxt, query):
        w1, b1, w2, b2 = state
        w1h, w2h = w1.astype(bf16), w2.astype(bf16)
        value_cat = kv_ref[j, pl.ds(m * both + mini, mini), :].astype(f32)
        rate_rows = kv_ref[j, pl.ds(minis * both, 16), :].astype(f32)
        e = dot(pick * rate_rows[m : m + 1], ones) + dot(
            pick * rate_rows[minis + m : minis + m + 1], ones
        )
        u = gain * (bias - (value_cat - key_cat.astype(f32)))
        u_mean = dot(u, ones) * (1.0 / d)

        x2, slope = gelu_both(z1)
        x2h = x2.astype(bf16)
        z = lane_cat(dot(x2h, w2h, NT)) + b2
        zz = z * z
        sums = dot(
            jnp.concatenate([zz, gain_sq * z, gain_sq * zz, u * z], axis=0), ones
        ) * (1.0 / d)
        rs = lax.rsqrt(sums[:mini] + ln_eps)
        mean_g = rs * sums[mini : 2 * mini] + u_mean
        mean_gn = rs * (rs * sums[2 * mini : 3 * mini] + sums[3 * mini :])
        h2 = (e * rs) * ((gain_sq * rs - rs * mean_gn) * z + (u - mean_g))
        h2h = blocks(h2).astype(bf16)
        h1 = dot(h2h, w2h) * slope
        h1h = h1.astype(bf16)

        z1_next, kb_next = None, None
        if nxt is not None:
            kb_next = blocks(nxt)
            cross = dot(kb_next, kb, NT) + same
            z1_next = dot(kb_next, w1h) + per_row(b1) - dot(cross, h1h)

        result = None
        if query is not None:
            qb = blocks(query)
            attend = causal * (dot(qb, kb, NT) + 1.0)
            first_bar = dot(qb, w1h) + per_row(b1) - dot(attend, h1h)
            hidden_bar = gelu(first_bar).astype(bf16)
            attend_hidden = causal * (dot(hidden_bar, x2h, NT) + 1.0)
            zb = lane_cat(dot(hidden_bar, w2h, NT) - dot(attend_hidden, h2h)) + b2
            var = dot(zb * zb, ones) * (1.0 / d)
            result = query.astype(f32) + gain * (zb * lax.rsqrt(var + ln_eps)) + bias

        w1 = w1 - dot(kb, h1h, TN)
        b1 = b1 - jnp.concatenate(
            [
                jnp.sum(h1[:mini], axis=0, keepdims=True),
                jnp.sum(h1[mini:], axis=0, keepdims=True),
            ],
            axis=0,
        )
        w2 = w2 - dot(h2h, x2h, TN)
        b2 = b2 - jnp.sum(h2, axis=0, keepdims=True)
        return (w1, b1, w2, b2), z1_next, kb_next, result

    def load():
        return w1_s[...], b1_s[...], w2_s[...], b2_s[...]

    def store(state):
        w1_s[...], b1_s[...], w2_s[...], b2_s[...] = state

    first = w1_ref[0]
    w1 = jnp.concatenate([first, first], axis=0)
    b1 = jnp.concatenate([b1_ref[...], b1_ref[...]], axis=0)
    second = w2_ref[0]
    second = second - jnp.mean(second, axis=1, keepdims=True)
    w2 = jnp.concatenate([second, second], axis=1).T
    b2 = b2_ref[...]
    b2 = b2 - jnp.mean(b2, axis=1, keepdims=True)
    b2 = jnp.concatenate([b2, b2], axis=1)
    store((w1, b1, w2, b2))
    z1_s[...] = dot(blocks(keys_of(0, 0)), w1) + per_row(b1)
    place = place_ref[0]

    def segment(j, carry):
        state, z1 = load(), z1_s[...]
        key_cat = keys_of(j, 0)
        kb = blocks(key_cat)
        for m in range(minis):
            nxt = keys_of(j, m + 1) if m + 1 < minis else keys_of(j + 1, 0)
            state, z1, kb, _ = step(j, m, state, z1, kb, key_cat, nxt, None)
            key_cat = nxt
        store(state)
        z1_s[...] = z1
        return carry

    lax.fori_loop(0, place, segment, 0)

    state, z1 = load(), z1_s[...]
    key_cat = keys_of(place, 0)
    kb = blocks(key_cat)
    for m in range(minis):
        nxt = keys_of(place, m + 1) if m + 1 < minis else None
        query = q_ref[pl.ds(m * mini, mini), :]
        state, z1, kb, result = step(place, m, state, z1, kb, key_cat, nxt, query)
        out_ref[pl.ds(m * mini, mini), :] = result.astype(bf16)
        key_cat = nxt


def out_kernel(heads_ref, w_ref, out_ref):
    heads, rows, both = heads_ref.shape
    d = both // 2
    low = lane_low((rows, both))
    firsts, seconds = [], []
    for h in range(0, heads, 2):
        even, odd = heads_ref[h].astype(f32), heads_ref[h + 1].astype(f32)
        firsts.append(jnp.where(low, even, pltpu.roll(odd, d, 1)))
        seconds.append(jnp.where(low, pltpu.roll(even, d, 1), odd))
    lhs = jnp.concatenate(
        [jnp.concatenate(firsts, axis=1), jnp.concatenate(seconds, axis=1)], axis=0
    )
    prod = dot(lhs, w_ref[...]).astype(bf16)
    out_ref[0] = prod[:rows]
    out_ref[1] = prod[rows:]


VMEM_LIMIT = 56 * 1024 * 1024


def on_device(
    tokens,
    w_qkv,
    w_rate,
    rate_bias,
    w_out,
    w_first_init,
    b_first_init,
    w_second_init,
    b_second_init,
    ln_gain,
    ln_bias,
):
    videos, tok_part, width = tokens.shape
    d = w_qkv.shape[0] // 3
    row_count = lax.axis_size("row")
    seg = tok_part * row_count
    minis = seg // MINI
    full_out = lax.all_gather(w_out, "row", axis=0, tiled=True)
    gathered = lax.all_gather(tokens, "row", axis=1, tiled=True)
    x = gathered.reshape(videos, minis, MINI, width).transpose(1, 0, 2, 3).reshape(-1, width)
    vmem = pl.BlockSpec(memory_space=pltpu.VMEM)
    smem = pl.BlockSpec(memory_space=pltpu.SMEM)
    params = pltpu.CompilerParams(vmem_limit_bytes=VMEM_LIMIT)
    kv, q = pl.pallas_call(
        project_kernel,
        out_shape=(
            jax.ShapeDtypeStruct((minis * 2 * MINI + 16, 2 * d), bf16),
            jax.ShapeDtypeStruct((minis * MINI, 2 * d), bf16),
        ),
        in_specs=[vmem] * 4,
        out_specs=(vmem, vmem),
        compiler_params=params,
        name="project",
    )(x, w_qkv, w_rate, rate_bias.reshape(1, 1))
    kv_all = lax.all_gather(kv, "seq")
    place = lax.axis_index("seq").astype(jnp.int32).reshape(1)
    inner = w_first_init.shape[2]
    heads = pl.pallas_call(
        chain_kernel,
        out_shape=jax.ShapeDtypeStruct((minis * MINI, 2 * d), bf16),
        in_specs=[smem] + [vmem] * 8,
        out_specs=vmem,
        scratch_shapes=[
            pltpu.VMEM((2 * d, inner), f32),
            pltpu.VMEM((2, inner), f32),
            pltpu.VMEM((2 * d, inner), f32),
            pltpu.VMEM((1, 2 * d), f32),
            pltpu.VMEM((2 * MINI, inner), f32),
        ],
        compiler_params=params,
        name="chain",
    )(place, kv_all, q, ln_gain, ln_bias, w_first_init, b_first_init, w_second_init, b_second_init)
    heads = heads.reshape(row_count, tok_part, 2 * d)
    arrived = lax.all_to_all(heads, "row", split_axis=0, concat_axis=0, tiled=True)
    return pl.pallas_call(
        out_kernel,
        out_shape=jax.ShapeDtypeStruct((videos, tok_part, width), bf16),
        in_specs=[vmem, vmem],
        out_specs=vmem,
        compiler_params=params,
        name="mix",
    )(arrived, full_out)


def solution(mesh):
    in_specs = (
        P(None, ("seq", "row"), None),
        P("row", None),
        P("row", None),
        P("row"),
        P("row", None),
        P("row", None, None),
        P("row", None),
        P("row", None, None),
        P("row", None),
        P("row", None),
        P("row", None),
    )
    out_specs = P(None, ("seq", "row"), None)
    return jax.shard_map(
        on_device, mesh=mesh, in_specs=in_specs, out_specs=out_specs, check_vma=False
    )
```

time: 167 us -> 104 us (0.62)
  the two profiles are of different devices: /device:TPU:0 before, /device:TPU:6 now
where the time goes in v1:
time: 104 us
  waiting for transfers between devices  45.5 us (44%)
  Pallas kernels  23 us (22%)
  between operations  14.1 us (14%)
  blocking collectives  11.6 us (11%)
  local copies, waits for them, and re-layouts  6 us (6%)
  starting transfers between devices  3.39 us (3%)
    all_gather x1, waiting for transfers between devices, on_device(): gathered = lax.all_gather(tokens, 'row', axis=1, tiled=True)  38.2 us
    pallas_call x1, Pallas kernels, on_device(): pl.pallas_call(chain_kernel, out_shape=jax.ShapeDtypeStruct((minis * MINI...  14.5 us
    all_gather x1, blocking collectives, on_device(): kv_all = lax.all_gather(kv, 'seq')  11.6 us
    all_to_all x1, waiting for transfers between devices, on_device(): lax.all_to_all(heads, 'row', split_axis=0, concat_axis=0, tiled=True)  5.39 us
    pallas_call x1, Pallas kernels, on_device(): pl.pallas_call(project_kernel, out_shape=(jax.ShapeDtypeStruct((minis * 2...  5.16 us
    reshape x1, local copies, waits for them, and re-layouts, on_device(): gathered.reshape(videos, minis, MINI, width).transpose(1, 0, 2, 3)  3.8 us
    pallas_call x1, Pallas kernels, on_device(): pl.pallas_call(out_kernel, out_shape=jax.ShapeDtypeStruct((videos, tok_pa...  3.38 us
    all_to_all x1, starting transfers between devices, on_device(): lax.all_to_all(heads, 'row', split_axis=0, concat_axis=0, tiled=True)  3.35 us
  transfers between devices with their start and end apart: 3, of which 3 were waited for; matrix products, arithmetic and copies ran while one was open for 5% of the time, Pallas kernels for 19%

profile of v1, /device:TPU:6, one launch (start us, length us, event | category | flops | bytes accessed | tf_op | source)
XLA Modules:
  0.0 103.5 jit_solution(2919542356138811269)
XLA Ops:
  6.5 0.0 all-gather.4.cloned.1.call-start
  6.5 0.7 all-gather.4.cloned.1.call-update
  7.3 0.0 all-gather.6.cloned.1.call-start
  7.3 0.7 all-gather.6.cloned.1.call-update
  8.7 1.6 %copy.13.w2_ref = f32[1,256,64]{2,1,0:T(8,128)} copy(f32[1,256,64]{1,2,0:T(8,128)} %param.18) | data formatting | bytes 131072 | tf_op args[7]
  10.2 38.2 %all-gather.4.cloned.1.call-done = bf16[2,256,3072]{2,1,0:T(8,128)(2,1)} async-done(((bf16[2,32,3072]{2,1,0:T(8,128)(2,1)}), bf16[2,256,3072]{2,1,0:T(8,128)(2,1)}) %all-gather.4.cloned.1.call-update) | async-done | bytes 3145744 | tf_op jit(solution)/shard_map/all_gather | solution.py:268
  48.5 3.8 %copy.12 = bf16[2,4,64,3072]{3,2,0,1:T(8,128)(2,1)} copy(bf16[2,4,64,3072]{3,2,1,0:T(8,128)(2,1)} %bitcast.10) | data formatting | bytes 6291456 | tf_op jit(solution)/shard_map/reshape | solution.py:269
  52.3 5.2 %project.1 = (bf16[528,128]{1,0:T(8,128)(2,1)}, bf16[256,128]{1,0:T(8,128)(2,1)}) custom-call(bf16[512,3072]{1,0:T(8,128)(2,1)} %bitcast.9, bf16[192,3072]{1,0:T(8,128)(2,1)} %w_ref.1, bf16[1,3072]{1,0:T(2,128)(2,1)} %wr_ref.1, f32[1,1]{1,0:T(1,128)} %bitcast.8.bias_ref), custom_call_target="tpu_custom_call" | custom-call | tf_op jit(solution)/shard_map/project/pallas_call | solution.py:273
  57.4 11.6 %all-gather = bf16[2112,128]{1,0:T(8,128)(2,1)} all-gather(bf16[528,128]{1,0:T(8,128)(2,1)} %get-tuple-element.7), channel_id=2, replica_groups=mesh['seq'=4,'row'=8] {'seq'}, dimensions={0}, use_global_device_ids=true | all-gather | bytes 675840 | tf_op jit(solution)/shard_map/all_gather | solution.py:284
  69.0 14.5 %chain.1 = bf16[256,128]{1,0:T(8,128)(2,1)} custom-call(s32[1]{0:T(128)} %bitcast.place_ref, bf16[4,528,128]{2,1,0:T(8,128)(2,1)} %bitcast.11, bf16[256,128]{1,0:T(8,128)(2,1)} %get-tuple-element.8.q_ref, f32[1,64]{1,0:T(1,128)} %gain_ref.1, f32[1,64]{1,0:T(1,128)} %bias_ref.1, f32[1,64,256]{2,1,0:T(8,128)} %w1_ref.1, f32[1,256]{1,0:T(1,128)} %b1_ref.1, ...), custom_call_target="tpu_custom_call" | custom-call | tf_op jit(solution)/shard_map/chain/pallas_call | solution.py:287
  83.5 3.4 %all-to-all-start = ((bf16[8,32,128]{2,1,0:T(8,128)(2,1)}), bf16[8,32,128]{2,1,0:T(8,128)(2,1)S(1)}, u32[]{:S(2)}, u32[]{:S(2)}) async-start(bf16[8,32,128]{2,1,0:T(8,128)(2,1)} %bitcast.12), calls=%async_computation | async-start | bytes 131072 | tf_op jit(solution)/shard_map/all_to_all | solution.py:303
  86.8 0.5 all-gather.6.cloned.1.call-done.w_ref
  87.3 5.4 %all-to-all-done.heads_ref = bf16[8,32,128]{2,1,0:T(8,128)(2,1)S(1)} async-done(((bf16[8,32,128]{2,1,0:T(8,128)(2,1)}), bf16[8,32,128]{2,1,0:T(8,128)(2,1)S(1)}, u32[]{:S(2)}, u32[]{:S(2)}) %all-to-all-start) | async-done | bytes 65568 | tf_op jit(solution)/shard_map/all_to_all | solution.py:303
  92.7 0.0 copy-start
  92.7 0.6 copy-done
  93.3 3.4 %mix.1 = bf16[2,32,3072]{2,1,0:T(8,128)(2,1)} custom-call(bf16[8,32,128]{2,1,0:T(8,128)(2,1)} %copy-done, bf16[512,3072]{1,0:T(8,128)(2,1)} %all-gather.6.cloned.1.call-done.w_ref), custom_call_target="tpu_custom_call" | custom-call | tf_op jit(solution)/shard_map/mix/pallas_call | solution.py:304
Async XLA Ops:
  6.5 41.9 %all-gather.4.cloned.1.call-start = ((), (), s32[]{:S(2)}) async-start(), calls=%async_computation.1 | async-start | bytes 3538944 | tf_op jit(solution)/shard_map/all_gather | solution.py:268
  7.3 80.0 %all-gather.6.cloned.1.call-start = ((), (), s32[]{:S(2)}) async-start(), calls=%async_computation.2 | async-start | bytes 3538944 | tf_op jit(solution)/shard_map/all_gather | solution.py:267
  83.5 9.2 %all-to-all-start = ((bf16[8,32,128]{2,1,0:T(8,128)(2,1)}), bf16[8,32,128]{2,1,0:T(8,128)(2,1)S(1)}, u32[]{:S(2)}, u32[]{:S(2)}) async-start(bf16[8,32,128]{2,1,0:T(8,128)(2,1)} %bitcast.12), calls=%async_computation | async-start | bytes 131072 | tf_op jit(solution)/shard_map/all_to_all | solution.py:303
  92.7 0.6 copy-start
Sparse Core Ops, SparseCore 0:
  9.0 39.4 all-gather.3
  50.1 37.1 all-gather.5

commit v2 on v1

--- a/solution.py
+++ b/solution.py
@@ -20,6 +20,11 @@
 TN = ((0,), (0,))
 
 
+def passed_along(array, axis, by):
+    size = lax.axis_size(axis)
+    return lax.ppermute(array, axis, [(i, i + by) for i in range(size - by)])
+
+
 def dot(left, right, dims=NN):
     return lax.dot_general(
         left.astype(bf16), right.astype(bf16), (dims, ((), ())), preferred_element_type=f32
@@ -41,21 +46,44 @@
     return jnp.where(lane_low((half, rows.shape[1])), rows[:half], rows[half:])
 
 
-def project_kernel(x_ref, w_ref, wr_ref, bias_ref, kv_ref, q_ref):
+def project_kernel(count, *refs):
+    x_refs, (w_ref, wr_ref, prod_ref, stack_ref) = refs[:count], refs[count:]
     d = w_ref.shape[0] // 3
-    mini = d
-    weights = jnp.concatenate(
-        [w_ref[...], jnp.broadcast_to(wr_ref[...], (d, wr_ref.shape[1]))], axis=0
-    )
-    minis = x_ref.shape[0] // (2 * mini)
+    stack_ref[: 3 * d, :] = w_ref[...]
+    stack_ref[3 * d :, :] = jnp.broadcast_to(wr_ref[...], (d, wr_ref.shape[1]))
+    x = jnp.concatenate([x_ref[...].reshape(-1, x_ref.shape[2]) for x_ref in x_refs], axis=0)
+    prod_ref[...] = dot(x, stack_ref[...], NT)
+
+
+def finish_kernel(count, part, spots_ref, early_ref, *refs):
+    x_refs, (stack_ref, bias_ref, kv_ref, q_ref, prod_s) = refs[:count], refs[count:]
+    mini = stack_ref.shape[0] // 4
+    x = jnp.concatenate([x_ref[...].reshape(-1, x_ref.shape[2]) for x_ref in x_refs], axis=0)
+    late = dot(x, stack_ref[...], NT)
+    early_count = early_ref.shape[0] // (2 * part)
+    for i in range(early_count + count):
+        spot = pl.multiple_of(spots_ref[i], part)
+        for video in range(2):
+            row = (2 * i + video) * part
+            if i < early_count:
+                prod = early_ref[pl.ds(row, part), :]
+            else:
+                row -= early_ref.shape[0]
+                prod = late[row : row + part]
+            prod_s[pl.ds(spot + video * mini, part), :] = prod
+    pack(prod_s, bias_ref, kv_ref, q_ref, mini)
+
+
+def pack(prod_s, bias_ref, kv_ref, q_ref, mini):
+    d = prod_s.shape[1] // 4
+    minis = prod_s.shape[0] // (2 * mini)
     eye = (
         lax.broadcasted_iota(jnp.int32, (2 * mini, 2 * mini), 0)
         == lax.broadcasted_iota(jnp.int32, (2 * mini, 2 * mini), 1)
     ).astype(f32)
     rates = []
     for m in range(minis):
-        rows = pl.ds(m * 2 * mini, 2 * mini)
-        prod = dot(x_ref[rows, :], weights, NT)
+        prod = prod_s[pl.ds(m * 2 * mini, 2 * mini), :]
         qk, vr = prod[:, : 2 * d], prod[:, 2 * d :]
         qk_swap, vr_swap = pltpu.roll(qk, d, 1), pltpu.roll(vr, d, 1)
         low = lane_low((mini, 2 * d))
@@ -93,10 +121,17 @@
     return half + half * tangent
 
 
-def chain_kernel(
-    place_ref, kv_ref, q_ref, gain_ref, bias_ref, w1_ref, b1_ref, w2_ref, b2_ref, out_ref,
-    w1_s, b1_s, w2_s, b2_s, z1_s,
-):
+def chain_kernel(seq_count, place_ref, *refs):
+    kv_refs, refs = refs[:seq_count], refs[seq_count:]
+    q_ref, gain_ref, bias_ref, w1_ref, b1_ref, w2_ref, b2_ref, out_ref = refs[:8]
+    kv_ref, w1_s, b1_s, w2_s, b2_s, z1_s = refs[8:]
+    place = place_ref[0]
+    for back in range(seq_count):
+
+        @pl.when(place >= back)
+        def _(back=back):
+            kv_ref[place - back] = kv_refs[back][...]
+
     d = w1_ref.shape[1]
     inner = w1_ref.shape[2]
     mini = d
@@ -199,7 +234,6 @@
     b2 = jnp.concatenate([b2, b2], axis=1)
     store((w1, b1, w2, b2))
     z1_s[...] = dot(blocks(keys_of(0, 0)), w1) + per_row(b1)
-    place = place_ref[0]
 
     def segment(j, carry):
         state, z1 = load(), z1_s[...]
@@ -226,21 +260,29 @@
         key_cat = nxt
 
 
-def out_kernel(heads_ref, w_ref, out_ref):
-    heads, rows, both = heads_ref.shape
+def out_kernel(count, owners_ref, heads_ref, *refs):
+    w_refs, out_ref = refs[:count], refs[count]
+    _, rows, both = heads_ref.shape
     d = both // 2
     low = lane_low((rows, both))
     firsts, seconds = [], []
-    for h in range(0, heads, 2):
-        even, odd = heads_ref[h].astype(f32), heads_ref[h + 1].astype(f32)
+    per = heads_ref.shape[0] // count
+    order = [owners_ref[i] * per + j for i in range(count) for j in range(per)]
+    for h in range(0, len(order), 2):
+        even, odd = heads_ref[order[h]].astype(f32), heads_ref[order[h + 1]].astype(f32)
         firsts.append(jnp.where(low, even, pltpu.roll(odd, d, 1)))
         seconds.append(jnp.where(low, pltpu.roll(even, d, 1), odd))
     lhs = jnp.concatenate(
         [jnp.concatenate(firsts, axis=1), jnp.concatenate(seconds, axis=1)], axis=0
     )
-    prod = dot(lhs, w_ref[...]).astype(bf16)
+    weights = jnp.concatenate([w_ref[...] for w_ref in w_refs], axis=0)
+    prod = dot(lhs, weights).astype(bf16)
     out_ref[0] = prod[:rows]
     out_ref[1] = prod[rows:]
+
+
+def swapped(array, flip):
+    return lax.ppermute(array, "row", [(i, i ^ flip) for i in range(lax.axis_size("row"))])
 
 
 VMEM_LIMIT = 56 * 1024 * 1024
@@ -264,32 +306,77 @@
     row_count = lax.axis_size("row")
     seg = tok_part * row_count
     minis = seg // MINI
-    full_out = lax.all_gather(w_out, "row", axis=0, tiled=True)
-    gathered = lax.all_gather(tokens, "row", axis=1, tiled=True)
-    x = gathered.reshape(videos, minis, MINI, width).transpose(1, 0, 2, 3).reshape(-1, width)
     vmem = pl.BlockSpec(memory_space=pltpu.VMEM)
     smem = pl.BlockSpec(memory_space=pltpu.SMEM)
     params = pltpu.CompilerParams(vmem_limit_bytes=VMEM_LIMIT)
+    row = lax.axis_index("row")
+    if row_count == 8:
+        far, near, own = lax.optimization_barrier(
+            (swapped(tokens, 4), swapped(tokens, 2), swapped(tokens, 1))
+        )
+        last = swapped(far, 2)
+        early = [tokens, own, far, swapped(far, 1), near, swapped(near, 1)]
+        owners = [row ^ flip for flip in (0, 1, 4, 5, 2, 3, 6, 7)]
+        w_owners = jnp.stack(owners).astype(jnp.int32)
+    else:
+        whole = lax.all_gather(tokens, "row", axis=1, tiled=True)
+        whole = whole.reshape(videos, minis, MINI, width)
+        parts = [whole[:, m] for m in range(minis)]
+        early, late = parts[:-1], parts[-1:]
+        owners = [m * (MINI // tok_part) for m in range(minis)]
+        w_parts = [lax.all_gather(w_out, "row", axis=0, tiled=True)]
+        w_owners = jnp.zeros((1,), jnp.int32)
+    per_mini = MINI // tok_part
+    spots = jnp.stack(
+        [
+            jnp.int32((o // per_mini) * (2 * MINI) + (o % per_mini) * tok_part) for o in owners
+        ]
+    )
+    part = early[0].shape[1]
+    early_prod, stack = pl.pallas_call(
+        partial(project_kernel, len(early)),
+        out_shape=(
+            jax.ShapeDtypeStruct((len(early) * 2 * part, 4 * d), f32),
+            jax.ShapeDtypeStruct((4 * d, width), bf16),
+        ),
+        in_specs=[vmem] * (len(early) + 2),
+        out_specs=(vmem, vmem),
+        compiler_params=params,
+        cost_estimate=pl.CostEstimate(
+            flops=len(early) * 4 * part * 4 * d * width, bytes_accessed=3_600_000, transcendentals=0
+        ),
+        name="project",
+    )(*early, w_qkv, w_rate)
+    if row_count == 8:
+        last, early_prod = lax.optimization_barrier((last, early_prod))
+        late = [last, swapped(last, 1)]
+        w_after, _ = lax.optimization_barrier((w_out, last))
+        w_parts = [w_out] + [swapped(w_after, flip) for flip in (4, 2, 6)]
     kv, q = pl.pallas_call(
-        project_kernel,
+        partial(finish_kernel, len(late), part),
         out_shape=(
             jax.ShapeDtypeStruct((minis * 2 * MINI + 16, 2 * d), bf16),
             jax.ShapeDtypeStruct((minis * MINI, 2 * d), bf16),
         ),
-        in_specs=[vmem] * 4,
+        in_specs=[smem] + [vmem] * (len(late) + 3),
         out_specs=(vmem, vmem),
+        scratch_shapes=[pltpu.VMEM((minis * 2 * MINI, 4 * d), f32)],
         compiler_params=params,
-        name="project",
-    )(x, w_qkv, w_rate, rate_bias.reshape(1, 1))
-    kv_all = lax.all_gather(kv, "seq")
+        name="finish",
+    )(spots, early_prod, *late, stack, rate_bias.reshape(1, 1))
+    seq_count = lax.axis_size("seq")
     place = lax.axis_index("seq").astype(jnp.int32).reshape(1)
+    kvs = [kv] + [None] * (seq_count - 1)
+    for back in range(seq_count - 1, 0, -1):
+        kvs[back] = passed_along(kv, "seq", back)
     inner = w_first_init.shape[2]
     heads = pl.pallas_call(
-        chain_kernel,
+        partial(chain_kernel, seq_count),
         out_shape=jax.ShapeDtypeStruct((minis * MINI, 2 * d), bf16),
-        in_specs=[smem] + [vmem] * 8,
+        in_specs=[smem] + [vmem] * (seq_count + 7),
         out_specs=vmem,
         scratch_shapes=[
+            pltpu.VMEM((seq_count,) + kv.shape, bf16),
             pltpu.VMEM((2 * d, inner), f32),
             pltpu.VMEM((2, inner), f32),
             pltpu.VMEM((2 * d, inner), f32),
@@ -298,17 +385,20 @@
         ],
         compiler_params=params,
         name="chain",
-    )(place, kv_all, q, ln_gain, ln_bias, w_first_init, b_first_init, w_second_init, b_second_init)
+    )(place, *kvs, q, ln_gain, ln_bias, w_first_init, b_first_init, w_second_init, b_second_init)
     heads = heads.reshape(row_count, tok_part, 2 * d)
+    if row_count == 8:
+        w_parts = lax.optimization_barrier((heads, *w_parts))[1:]
+        w_parts = [x for w in w_parts for x in (w, swapped(w, 1))]
     arrived = lax.all_to_all(heads, "row", split_axis=0, concat_axis=0, tiled=True)
     return pl.pallas_call(
-        out_kernel,
+        partial(out_kernel, len(w_parts)),
         out_shape=jax.ShapeDtypeStruct((videos, tok_part, width), bf16),
-        in_specs=[vmem, vmem],
+        in_specs=[smem, vmem] + [vmem] * len(w_parts),
         out_specs=vmem,
         compiler_params=params,
         name="mix",
-    )(arrived, full_out)
+    )(w_owners, arrived, *w_parts)
 
 
 def solution(mesh):

time: 104 us -> 89.7 us (0.86)
  starting transfers between devices: 3.39 us -> 20 us
  between operations: 14.1 us -> 0.88 us
  blocking collectives: 11.6 us -> 0 us
  waiting for transfers between devices: 45.5 us -> 36.9 us
  Pallas kernels: 23 us -> 25 us
    all_gather x2 -> x0, waiting for transfers between devices: 38.7 us -> none  [the longest x1 38.2 us: on_device(): gathered = lax.all_gather(tokens, 'row', axis=1, tiled=True)]
    ppermute x0 -> x17, waiting for transfers between devices: none -> 31.7 us  [the longest x14 21.2 us: swapped(): lax.ppermute(array, 'row', [(i, i ^ flip) for i in range(lax.axis_size('r...]
    ppermute x0 -> x17, starting transfers between devices: none -> 15.6 us  [the longest x14 11.7 us: swapped(): lax.ppermute(array, 'row', [(i, i ^ flip) for i in range(lax.axis_size('r...]
    all_gather x1 -> x0, blocking collectives: 11.6 us -> none  [on_device(): kv_all = lax.all_gather(kv, 'seq')]
    reshape x1 -> x0, local copies, waits for them, and re-layouts: 3.8 us -> none  [on_device(): gathered.reshape(videos, minis, MINI, width).transpose(1, 0, 2, 3)]
    unnamed x3 -> x41, local copies, waits for them, and re-layouts: 2.21 us -> 5.12 us
    pallas_call x3 -> x4, Pallas kernels: 23 us -> 25 us  [the longest x1 14.5 us: on_device(): pl.pallas_call(partial(chain_kernel, seq_count), out_shape=jax.ShapeDtype...]
    unnamed x2 -> x0, waiting for transfers between devices: 1.41 us -> none
  transfers between devices with their start and end apart: 3 -> 18, of which waited for: 3 -> 7; matrix products, arithmetic and copies ran while one was open for 5% -> 2% of each run, Pallas kernels for 19% -> 24%
where the time goes in v2:
time: 89.7 us; the launch traced here: 89.3 us
  waiting for transfers between devices  36.9 us (41%)
  Pallas kernels  25 us (28%)
  starting transfers between devices  20 us (22%)
  local copies, waits for them, and re-layouts  6.45 us (7%)
    ppermute x14, waiting for transfers between devices, swapped(): lax.ppermute(array, 'row', [(i, i ^ flip) for i in range(lax.axis_size('r...  21.2 us
    pallas_call x1, Pallas kernels, on_device(): pl.pallas_call(partial(chain_kernel, seq_count), out_shape=jax.ShapeDtype...  14.5 us
    ppermute x14, starting transfers between devices, swapped(): lax.ppermute(array, 'row', [(i, i ^ flip) for i in range(lax.axis_size('r...  11.7 us
    ppermute x3, waiting for transfers between devices, passed_along(): return lax.ppermute(array, axis, [(i, i + by) for i in range(size - by)])  10.5 us
    all_to_all x1, waiting for transfers between devices, on_device(): lax.all_to_all(heads, 'row', split_axis=0, concat_axis=0, tiled=True)  5.24 us
    unnamed x41, local copies, waits for them, and re-layouts  5.12 us
    all_to_all x1, starting transfers between devices, on_device(): lax.all_to_all(heads, 'row', split_axis=0, concat_axis=0, tiled=True)  4.49 us
    ppermute x3, starting transfers between devices, passed_along(): return lax.ppermute(array, axis, [(i, i + by) for i in range(size - by)])  3.85 us
  transfers between devices with their start and end apart: 18, of which 7 were waited for; matrix products, arithmetic and copies ran while one was open for 2% of the time, Pallas kernels for 24%

profile of v2, /device:TPU:6, one launch (start us, length us, event | category | flops | bytes accessed | tf_op | source)
XLA Modules:
  0.0 89.3 jit_solution(5506067472929160084)
XLA Ops:
  0.0 2.6 %collective-permute-start = (bf16[2,32,3072]{2,1,0:T(8,128)(2,1)}, bf16[2,32,3072]{2,1,0:T(8,128)(2,1)S(1)}, u32[]{:S(2)}, u32[]{:S(2)}) collective-permute-start(bf16[2,32,3072]{2,1,0:T(8,128)(2,1)} %refs_0_.1), channel_id=1, source_target_pairs={{0,4},{1,5},{2,6},{3,7},{4,0},{5,1},{6,2},{7,3},{8,12},{9,13},{10,... | collective-permute-start | bytes 1179656 | tf_op jit(solution)/shard_map/ppermute | solution.py:285
  2.6 1.6 %collective-permute-start.1 = (bf16[2,32,3072]{2,1,0:T(8,128)(2,1)}, bf16[2,32,3072]{2,1,0:T(8,128)(2,1)S(1)}, u32[]{:S(2)}, u32[]{:S(2)}) collective-permute-start(bf16[2,32,3072]{2,1,0:T(8,128)(2,1)} %refs_0_.1), channel_id=1, source_target_pairs={{0,2},{1,3},{2,0},{3,1},{4,6},{5,7},{6,4},{7,5},{8,10},{9,11},{10,... | collective-permute-start | bytes 1179656 | tf_op jit(solution)/shard_map/ppermute | solution.py:285
  4.2 16.3 %collective-permute-done.refs_2_ = bf16[2,32,3072]{2,1,0:T(8,128)(2,1)S(1)} collective-permute-done((bf16[2,32,3072]{2,1,0:T(8,128)(2,1)}, bf16[2,32,3072]{2,1,0:T(8,128)(2,1)S(1)}, u32[]{:S(2)}, u32[]{:S(2)}) %collective-permute-start) | collective-permute-done | bytes 393248 | tf_op jit(solution)/shard_map/ppermute | solution.py:285
  20.8 0.5 collective-permute-start.5
  21.3 1.4 %collective-permute-start.3 = (bf16[2,32,3072]{2,1,0:T(8,128)(2,1)S(1)}, bf16[2,32,3072]{2,1,0:T(8,128)(2,1)S(1)}, u32[]{:S(2)}, u32[]{:S(2)}) collective-permute-start(bf16[2,32,3072]{2,1,0:T(8,128)(2,1)S(1)} %collective-permute-done.refs_2_), channel_id=1, source_target_pairs={{0,2},{1,3},{2,0},{3,1},{4,6},{5,7},{6,4},{7,5},{8,10},{9,11},{10,... | collective-permute-start | bytes 1179656 | tf_op jit(solution)/shard_map/ppermute | solution.py:285
  22.7 0.3 collective-permute-done.5.refs_5_
  23.1 0.4 copy-done.13
  23.5 0.8 copy-done.14
  24.2 3.8 %project.1 = (f32[384,256]{1,0:T(8,128)}, bf16[256,3072]{1,0:T(8,128)(2,1)}) custom-call(bf16[2,32,3072]{2,1,0:T(8,128)(2,1)} %refs_0_.1, bf16[2,32,3072]{2,1,0:T(8,128)(2,1)} %copy-done.12, bf16[2,32,3072]{2,1,0:T(8,128)(2,1)} %copy-done.8, bf16[2,32,3072]{2,1,0:T(8,128)(2,1)} %copy-done.13, bf16[2,32,3072]{2,1,0:T(8,128)(2,1)} %copy-done.11, ...), custom_call_target="tpu_custom_call" | custom-call | flops 603979776 | bytes 3600000 | tf_op jit(solution)/shard_map/project/pallas_call | solution.py:336
  28.1 4.3 %collective-permute-done.3.refs_0_ = bf16[2,32,3072]{2,1,0:T(8,128)(2,1)S(1)} collective-permute-done((bf16[2,32,3072]{2,1,0:T(8,128)(2,1)S(1)}, bf16[2,32,3072]{2,1,0:T(8,128)(2,1)S(1)}, u32[]{:S(2)}, u32[]{:S(2)}) %collective-permute-start.3) | collective-permute-done | bytes 393248 | tf_op jit(solution)/shard_map/ppermute | solution.py:285
  32.4 2.1 %collective-permute-start.10 = (bf16[64,3072]{1,0:T(8,128)(2,1)S(1)}, bf16[64,3072]{1,0:T(8,128)(2,1)S(1)}, u32[]{:S(2)}, u32[]{:S(2)}) collective-permute-start(bf16[64,3072]{1,0:T(8,128)(2,1)S(1)} %copy-done.2), channel_id=1, source_target_pairs={{0,4},{1,5},{2,6},{3,7},{4,0},{5,1},{6,2},{7,3},{8,12},{9,13},{10,... | collective-permute-start | bytes 1179656 | tf_op jit(solution)/shard_map/ppermute | solution.py:285
  34.5 1.7 %collective-permute-start.11 = (bf16[64,3072]{1,0:T(8,128)(2,1)S(1)}, bf16[64,3072]{1,0:T(8,128)(2,1)S(1)}, u32[]{:S(2)}, u32[]{:S(2)}) collective-permute-start(bf16[64,3072]{1,0:T(8,128)(2,1)S(1)} %copy-done.2), channel_id=1, source_target_pairs={{0,2},{1,3},{2,0},{3,1},{4,6},{5,7},{6,4},{7,5},{8,10},{9,11},{10,... | collective-permute-start | bytes 1179656 | tf_op jit(solution)/shard_map/ppermute | solution.py:285
  36.2 0.6 collective-permute-start.12
  37.5 0.7 stack.71.spots_ref
  38.2 0.7 copy-done.1
  38.9 3.3 %finish.1 = (bf16[528,128]{1,0:T(8,128)(2,1)}, bf16[256,128]{1,0:T(8,128)(2,1)}) custom-call(s32[8]{0:T(128)} %stack.71.spots_ref, f32[384,256]{1,0:T(8,128)} %get-tuple-element.23.early_ref, bf16[2,32,3072]{2,1,0:T(8,128)(2,1)} %copy-done, bf16[2,32,3072]{2,1,0:T(8,128)(2,1)} %copy-done.1, bf16[256,3072]{1,0:T(8,128)(2,1)} %get-tuple-element.25.refs_2_, ...), custom_call_target="tpu_custom_call" | custom-call | tf_op jit(solution)/shard_map/finish/pallas_call | solution.py:355
  42.2 1.3 %collective-permute-start.7 = (bf16[528,128]{1,0:T(8,128)(2,1)}, bf16[528,128]{1,0:T(8,128)(2,1)S(1)}, u32[]{:S(2)}, u32[]{:S(2)}) collective-permute-start(bf16[528,128]{1,0:T(8,128)(2,1)} %get-tuple-element.26.refs_0_), channel_id=1, source_target_pairs={{0,8},{8,16},{16,24},{1,9},{9,17},{17,25},{2,10},{10,18},{18,26},{... | collective-permute-start | bytes 405512 | tf_op jit(solution)/shard_map/ppermute | solution.py:25
  43.5 1.3 %collective-permute-start.8 = (bf16[528,128]{1,0:T(8,128)(2,1)}, bf16[528,128]{1,0:T(8,128)(2,1)S(1)}, u32[]{:S(2)}, u32[]{:S(2)}) collective-permute-start(bf16[528,128]{1,0:T(8,128)(2,1)} %get-tuple-element.26.refs_0_), channel_id=1, source_target_pairs={{0,16},{8,24},{1,17},{9,25},{2,18},{10,26},{3,19},{11,27},{4,20},{... | collective-permute-start | bytes 405512 | tf_op jit(solution)/shard_map/ppermute | solution.py:25
  44.8 4.6 %collective-permute-done.7.refs_1_ = bf16[528,128]{1,0:T(8,128)(2,1)S(1)} collective-permute-done((bf16[528,128]{1,0:T(8,128)(2,1)}, bf16[528,128]{1,0:T(8,128)(2,1)S(1)}, u32[]{:S(2)}, u32[]{:S(2)}) %collective-permute-start.7) | collective-permute-done | bytes 135200 | tf_op jit(solution)/shard_map/ppermute | solution.py:25
  49.4 1.3 %collective-permute-start.9 = (bf16[528,128]{1,0:T(8,128)(2,1)}, bf16[528,128]{1,0:T(8,128)(2,1)S(1)}, u32[]{:S(2)}, u32[]{:S(2)}) collective-permute-start(bf16[528,128]{1,0:T(8,128)(2,1)} %get-tuple-element.26.refs_0_), channel_id=1, source_target_pairs={{0,24},{1,25},{2,26},{3,27},{4,28},{5,29},{6,30},{7,31}} | collective-permute-start | bytes 405512 | tf_op jit(solution)/shard_map/ppermute | solution.py:25
  50.7 0.8 copy.12.refs_9_
  51.5 5.9 %collective-permute-done.9.refs_3_ = bf16[528,128]{1,0:T(8,128)(2,1)S(1)} collective-permute-done((bf16[528,128]{1,0:T(8,128)(2,1)}, bf16[528,128]{1,0:T(8,128)(2,1)S(1)}, u32[]{:S(2)}, u32[]{:S(2)}) %collective-permute-start.9) | collective-permute-done | bytes 135200 | tf_op jit(solution)/shard_map/ppermute | solution.py:25
  57.4 0.6 copy-done.18
  58.1 14.5 %chain.1 = bf16[256,128]{1,0:T(8,128)(2,1)} custom-call(s32[1]{0:T(128)} %bitcast.8.place_ref, bf16[528,128]{1,0:T(8,128)(2,1)} %get-tuple-element.26.refs_0_, bf16[528,128]{1,0:T(8,128)(2,1)} %copy-done.16, bf16[528,128]{1,0:T(8,128)(2,1)} %copy-done.17, bf16[528,128]{1,0:T(8,128)(2,1)} %copy-done.18, bf16[256,128]{1,0:T(8,128)(2,1)} %get-tuple-element.27.refs_4_, ...), custom_call_target="tpu_custom_call" | custom-call | tf_op jit(solution)/shard_map/chain/pallas_call | solution.py:373
  72.8 0.5 collective-permute-start.14
  73.3 0.4 collective-permute-start.16
  73.8 4.5 %all-to-all-start = ((bf16[8,32,128]{2,1,0:T(8,128)(2,1)}), bf16[8,32,128]{2,1,0:T(8,128)(2,1)S(1)}, u32[]{:S(2)}, u32[]{:S(2)}) async-start(bf16[8,32,128]{2,1,0:T(8,128)(2,1)} %bitcast.20), calls=%async_computation | async-start | bytes 131072 | tf_op jit(solution)/shard_map/all_to_all | solution.py:393
  78.3 0.7 stack.62.owners_ref
  78.9 5.2 %all-to-all-done.heads_ref = bf16[8,32,128]{2,1,0:T(8,128)(2,1)S(1)} async-done(((bf16[8,32,128]{2,1,0:T(8,128)(2,1)}), bf16[8,32,128]{2,1,0:T(8,128)(2,1)S(1)}, u32[]{:S(2)}, u32[]{:S(2)}) %all-to-all-start) | async-done | bytes 65568 | tf_op jit(solution)/shard_map/all_to_all | solution.py:393
  84.3 0.5 copy-done.15
  85.2 0.8 copy-done.10
  86.0 3.3 %mix.1 = bf16[2,32,3072]{2,1,0:T(8,128)(2,1)} custom-call(s32[8]{0:T(128)} %stack.62.owners_ref, bf16[8,32,128]{2,1,0:T(8,128)(2,1)} %copy-done.15, bf16[64,3072]{1,0:T(8,128)(2,1)} %refs_0_.2, bf16[64,3072]{1,0:T(8,128)(2,1)} %copy-done.6, bf16[64,3072]{1,0:T(8,128)(2,1)} %copy-done.3, bf16[64,3072]{1,0:T(8,128)(2,1)} %copy-done.7, ...), custom_call_target="tpu_custom_call" | custom-call | tf_op jit(solution)/shard_map/mix/pallas_call | solution.py:394
  (51 shorter events, 0.9 us)
Async XLA Ops:
  0.0 32.4 %copy-start.2 = (bf16[64,3072]{1,0:T(8,128)(2,1)S(1)}, bf16[64,3072]{1,0:T(8,128)(2,1)}, u32[]{:S(2)}) copy-start(bf16[64,3072]{1,0:T(8,128)(2,1)} %refs_0_.2) | copy-start | bytes 1179652
  0.0 20.5 %collective-permute-start = (bf16[2,32,3072]{2,1,0:T(8,128)(2,1)}, bf16[2,32,3072]{2,1,0:T(8,128)(2,1)S(1)}, u32[]{:S(2)}, u32[]{:S(2)}) collective-permute-start(bf16[2,32,3072]{2,1,0:T(8,128)(2,1)} %refs_0_.1), channel_id=1, source_target_pairs={{0,4},{1,5},{2,6},{3,7},{4,0},{5,1},{6,2},{7,3},{8,12},{9,13},{10,... | collective-permute-start | bytes 1179656 | tf_op jit(solution)/shard_map/ppermute | solution.py:285
  2.6 18.1 %collective-permute-start.1 = (bf16[2,32,3072]{2,1,0:T(8,128)(2,1)}, bf16[2,32,3072]{2,1,0:T(8,128)(2,1)S(1)}, u32[]{:S(2)}, u32[]{:S(2)}) collective-permute-start(bf16[2,32,3072]{2,1,0:T(8,128)(2,1)} %refs_0_.1), channel_id=1, source_target_pairs={{0,2},{1,3},{2,0},{3,1},{4,6},{5,7},{6,4},{7,5},{8,10},{9,11},{10,... | collective-permute-start | bytes 1179656 | tf_op jit(solution)/shard_map/ppermute | solution.py:285
  4.2 16.5 %collective-permute-start.2 = (bf16[2,32,3072]{2,1,0:T(8,128)(2,1)}, bf16[2,32,3072]{2,1,0:T(8,128)(2,1)S(1)}, u32[]{:S(2)}, u32[]{:S(2)}) collective-permute-start(bf16[2,32,3072]{2,1,0:T(8,128)(2,1)} %refs_0_.1), channel_id=1, source_target_pairs={{0,1},{1,0},{2,3},{3,2},{4,5},{5,4},{6,7},{7,6},{8,9},{9,8},{10,11... | collective-permute-start | bytes 1179656 | tf_op jit(solution)/shard_map/ppermute | solution.py:285
  20.5 2.5 %copy-start.8 = (bf16[2,32,3072]{2,1,0:T(8,128)(2,1)}, bf16[2,32,3072]{2,1,0:T(8,128)(2,1)S(1)}, u32[]{:S(2)}) copy-start(bf16[2,32,3072]{2,1,0:T(8,128)(2,1)S(1)} %collective-permute-done.refs_2_) | copy-start | bytes 1179652
  20.7 2.4 %copy-start.11 = (bf16[2,32,3072]{2,1,0:T(8,128)(2,1)}, bf16[2,32,3072]{2,1,0:T(8,128)(2,1)S(1)}, u32[]{:S(2)}) copy-start(bf16[2,32,3072]{2,1,0:T(8,128)(2,1)S(1)} %collective-permute-done.1.refs_4_) | copy-start | bytes 1179652
  20.7 2.4 %copy-start.12 = (bf16[2,32,3072]{2,1,0:T(8,128)(2,1)}, bf16[2,32,3072]{2,1,0:T(8,128)(2,1)S(1)}, u32[]{:S(2)}) copy-start(bf16[2,32,3072]{2,1,0:T(8,128)(2,1)S(1)} %collective-permute-done.2.refs_1_) | copy-start | bytes 1179652
  20.7 2.0 %collective-permute-start.4 = (bf16[2,32,3072]{2,1,0:T(8,128)(2,1)S(1)}, bf16[2,32,3072]{2,1,0:T(8,128)(2,1)S(1)}, u32[]{:S(2)}, u32[]{:S(2)}) collective-permute-start(bf16[2,32,3072]{2,1,0:T(8,128)(2,1)S(1)} %collective-permute-done.refs_2_), channel_id=1, source_target_pairs={{0,1},{1,0},{2,3},{3,2},{4,5},{5,4},{6,7},{7,6},{8,9},{9,8},{10,11... | collective-permute-start | bytes 1179656 | tf_op jit(solution)/shard_map/ppermute | solution.py:285
  20.8 2.3 %collective-permute-start.5 = (bf16[2,32,3072]{2,1,0:T(8,128)(2,1)S(1)}, bf16[2,32,3072]{2,1,0:T(8,128)(2,1)S(1)}, u32[]{:S(2)}, u32[]{:S(2)}) collective-permute-start(bf16[2,32,3072]{2,1,0:T(8,128)(2,1)S(1)} %collective-permute-done.1.refs_4_), channel_id=1, source_target_pairs={{0,1},{1,0},{2,3},{3,2},{4,5},{5,4},{6,7},{7,6},{8,9},{9,8},{10,11... | collective-permute-start | bytes 1179656 | tf_op jit(solution)/shard_map/ppermute | solution.py:285
  21.3 11.1 %collective-permute-start.3 = (bf16[2,32,3072]{2,1,0:T(8,128)(2,1)S(1)}, bf16[2,32,3072]{2,1,0:T(8,128)(2,1)S(1)}, u32[]{:S(2)}, u32[]{:S(2)}) collective-permute-start(bf16[2,32,3072]{2,1,0:T(8,128)(2,1)S(1)} %collective-permute-done.refs_2_), channel_id=1, source_target_pairs={{0,2},{1,3},{2,0},{3,1},{4,6},{5,7},{6,4},{7,5},{8,10},{9,11},{10,... | collective-permute-start | bytes 1179656 | tf_op jit(solution)/shard_map/ppermute | solution.py:285
  22.7 0.8 copy-start.13
  32.4 5.8 %copy-start = (bf16[2,32,3072]{2,1,0:T(8,128)(2,1)}, bf16[2,32,3072]{2,1,0:T(8,128)(2,1)S(1)}, u32[]{:S(2)}) copy-start(bf16[2,32,3072]{2,1,0:T(8,128)(2,1)S(1)} %collective-permute-done.3.refs_0_) | copy-start | bytes 1179652
  32.4 5.8 %collective-permute-start.6 = (bf16[2,32,3072]{2,1,0:T(8,128)(2,1)S(1)}, bf16[2,32,3072]{2,1,0:T(8,128)(2,1)S(1)}, u32[]{:S(2)}, u32[]{:S(2)}) collective-permute-start(bf16[2,32,3072]{2,1,0:T(8,128)(2,1)S(1)} %collective-permute-done.3.refs_0_), channel_id=1, source_target_pairs={{0,1},{1,0},{2,3},{3,2},{4,5},{5,4},{6,7},{7,6},{8,9},{9,8},{10,11... | collective-permute-start | bytes 1179656 | tf_op jit(solution)/shard_map/ppermute | solution.py:285
  32.4 40.2 %collective-permute-start.10 = (bf16[64,3072]{1,0:T(8,128)(2,1)S(1)}, bf16[64,3072]{1,0:T(8,128)(2,1)S(1)}, u32[]{:S(2)}, u32[]{:S(2)}) collective-permute-start(bf16[64,3072]{1,0:T(8,128)(2,1)S(1)} %copy-done.2), channel_id=1, source_target_pairs={{0,4},{1,5},{2,6},{3,7},{4,0},{5,1},{6,2},{7,3},{8,12},{9,13},{10,... | collective-permute-start | bytes 1179656 | tf_op jit(solution)/shard_map/ppermute | solution.py:285
  34.5 38.2 %collective-permute-start.11 = (bf16[64,3072]{1,0:T(8,128)(2,1)S(1)}, bf16[64,3072]{1,0:T(8,128)(2,1)S(1)}, u32[]{:S(2)}, u32[]{:S(2)}) collective-permute-start(bf16[64,3072]{1,0:T(8,128)(2,1)S(1)} %copy-done.2), channel_id=1, source_target_pairs={{0,2},{1,3},{2,0},{3,1},{4,6},{5,7},{6,4},{7,5},{8,10},{9,11},{10,... | collective-permute-start | bytes 1179656 | tf_op jit(solution)/shard_map/ppermute | solution.py:285
  36.2 36.4 %collective-permute-start.12 = (bf16[64,3072]{1,0:T(8,128)(2,1)S(1)}, bf16[64,3072]{1,0:T(8,128)(2,1)S(1)}, u32[]{:S(2)}, u32[]{:S(2)}) collective-permute-start(bf16[64,3072]{1,0:T(8,128)(2,1)S(1)} %copy-done.2), channel_id=1, source_target_pairs={{0,6},{1,7},{2,4},{3,5},{4,2},{5,3},{6,0},{7,1},{8,14},{9,15},{10,... | collective-permute-start | bytes 1179656 | tf_op jit(solution)/shard_map/ppermute | solution.py:285
  36.8 13.9 %copy-start.19 = (f32[1,256,64]{1,2,0:T(8,128)S(1)}, f32[1,256,64]{1,2,0:T(8,128)}, u32[]{:S(2)}) copy-start(f32[1,256,64]{1,2,0:T(8,128)} %param.18) | copy-start | bytes 196612
  42.2 7.2 %collective-permute-start.7 = (bf16[528,128]{1,0:T(8,128)(2,1)}, bf16[528,128]{1,0:T(8,128)(2,1)S(1)}, u32[]{:S(2)}, u32[]{:S(2)}) collective-permute-start(bf16[528,128]{1,0:T(8,128)(2,1)} %get-tuple-element.26.refs_0_), channel_id=1, source_target_pairs={{0,8},{8,16},{16,24},{1,9},{9,17},{17,25},{2,10},{10,18},{18,26},{... | collective-permute-start | bytes 405512 | tf_op jit(solution)/shard_map/ppermute | solution.py:25
  43.5 8.0 %collective-permute-start.8 = (bf16[528,128]{1,0:T(8,128)(2,1)}, bf16[528,128]{1,0:T(8,128)(2,1)S(1)}, u32[]{:S(2)}, u32[]{:S(2)}) collective-permute-start(bf16[528,128]{1,0:T(8,128)(2,1)} %get-tuple-element.26.refs_0_), channel_id=1, source_target_pairs={{0,16},{8,24},{1,17},{9,25},{2,18},{10,26},{3,19},{11,27},{4,20},{... | collective-permute-start | bytes 405512 | tf_op jit(solution)/shard_map/ppermute | solution.py:25
  49.4 8.0 %copy-start.16 = (bf16[528,128]{1,0:T(8,128)(2,1)}, bf16[528,128]{1,0:T(8,128)(2,1)S(1)}, u32[]{:S(2)}) copy-start(bf16[528,128]{1,0:T(8,128)(2,1)S(1)} %collective-permute-done.7.refs_1_) | copy-start | bytes 405508
  49.4 8.0 %collective-permute-start.9 = (bf16[528,128]{1,0:T(8,128)(2,1)}, bf16[528,128]{1,0:T(8,128)(2,1)S(1)}, u32[]{:S(2)}, u32[]{:S(2)}) collective-permute-start(bf16[528,128]{1,0:T(8,128)(2,1)} %get-tuple-element.26.refs_0_), channel_id=1, source_target_pairs={{0,24},{1,25},{2,26},{3,27},{4,28},{5,29},{6,30},{7,31}} | collective-permute-start | bytes 405512 | tf_op jit(solution)/shard_map/ppermute | solution.py:25
  51.5 5.9 %copy-start.17 = (bf16[528,128]{1,0:T(8,128)(2,1)}, bf16[528,128]{1,0:T(8,128)(2,1)S(1)}, u32[]{:S(2)}) copy-start(bf16[528,128]{1,0:T(8,128)(2,1)S(1)} %collective-permute-done.8.refs_2_) | copy-start | bytes 405508
  72.6 11.6 %copy-start.3 = (bf16[64,3072]{1,0:T(8,128)(2,1)}, bf16[64,3072]{1,0:T(8,128)(2,1)S(1)}, u32[]{:S(2)}) copy-start(bf16[64,3072]{1,0:T(8,128)(2,1)S(1)} %collective-permute-done.10.refs_2_) | copy-start | bytes 1179652
  72.6 11.6 %copy-start.4 = (bf16[64,3072]{1,0:T(8,128)(2,1)}, bf16[64,3072]{1,0:T(8,128)(2,1)S(1)}, u32[]{:S(2)}) copy-start(bf16[64,3072]{1,0:T(8,128)(2,1)S(1)} %collective-permute-done.11.refs_4_) | copy-start | bytes 1179652
  72.7 11.6 %copy-start.5 = (bf16[64,3072]{1,0:T(8,128)(2,1)}, bf16[64,3072]{1,0:T(8,128)(2,1)S(1)}, u32[]{:S(2)}) copy-start(bf16[64,3072]{1,0:T(8,128)(2,1)S(1)} %collective-permute-done.12.refs_6_) | copy-start | bytes 1179652
  72.7 11.5 %collective-permute-start.13 = (bf16[64,3072]{1,0:T(8,128)(2,1)S(1)}, bf16[64,3072]{1,0:T(8,128)(2,1)S(1)}, u32[]{:S(2)}, u32[]{:S(2)}) collective-permute-start(bf16[64,3072]{1,0:T(8,128)(2,1)S(1)} %copy-done.2), channel_id=1, source_target_pairs={{0,1},{1,0},{2,3},{3,2},{4,5},{5,4},{6,7},{7,6},{8,9},{9,8},{10,11... | collective-permute-start | bytes 1179656 | tf_op jit(solution)/shard_map/ppermute | solution.py:285
  72.8 11.4 %collective-permute-start.14 = (bf16[64,3072]{1,0:T(8,128)(2,1)S(1)}, bf16[64,3072]{1,0:T(8,128)(2,1)S(1)}, u32[]{:S(2)}, u32[]{:S(2)}) collective-permute-start(bf16[64,3072]{1,0:T(8,128)(2,1)S(1)} %collective-permute-done.10.refs_2_), channel_id=1, source_target_pairs={{0,1},{1,0},{2,3},{3,2},{4,5},{5,4},{6,7},{7,6},{8,9},{9,8},{10,11... | collective-permute-start | bytes 1179656 | tf_op jit(solution)/shard_map/ppermute | solution.py:285
  73.3 10.9 %collective-permute-start.15 = (bf16[64,3072]{1,0:T(8,128)(2,1)S(1)}, bf16[64,3072]{1,0:T(8,128)(2,1)S(1)}, u32[]{:S(2)}, u32[]{:S(2)}) collective-permute-start(bf16[64,3072]{1,0:T(8,128)(2,1)S(1)} %collective-permute-done.11.refs_4_), channel_id=1, source_target_pairs={{0,1},{1,0},{2,3},{3,2},{4,5},{5,4},{6,7},{7,6},{8,9},{9,8},{10,11... | collective-permute-start | bytes 1179656 | tf_op jit(solution)/shard_map/ppermute | solution.py:285
  73.3 10.9 %collective-permute-start.16 = (bf16[64,3072]{1,0:T(8,128)(2,1)S(1)}, bf16[64,3072]{1,0:T(8,128)(2,1)S(1)}, u32[]{:S(2)}, u32[]{:S(2)}) collective-permute-start(bf16[64,3072]{1,0:T(8,128)(2,1)S(1)} %collective-permute-done.12.refs_6_), channel_id=1, source_target_pairs={{0,1},{1,0},{2,3},{3,2},{4,5},{5,4},{6,7},{7,6},{8,9},{9,8},{10,11... | collective-permute-start | bytes 1179656 | tf_op jit(solution)/shard_map/ppermute | solution.py:285
  73.8 10.4 %all-to-all-start = ((bf16[8,32,128]{2,1,0:T(8,128)(2,1)}), bf16[8,32,128]{2,1,0:T(8,128)(2,1)S(1)}, u32[]{:S(2)}, u32[]{:S(2)}) async-start(bf16[8,32,128]{2,1,0:T(8,128)(2,1)} %bitcast.20), calls=%async_computation | async-start | bytes 131072 | tf_op jit(solution)/shard_map/all_to_all | solution.py:393
  84.2 0.9 %copy-start.7 = (bf16[64,3072]{1,0:T(8,128)(2,1)}, bf16[64,3072]{1,0:T(8,128)(2,1)S(1)}, u32[]{:S(2)}) copy-start(bf16[64,3072]{1,0:T(8,128)(2,1)S(1)} %collective-permute-done.14.refs_3_) | copy-start | bytes 1179652
  84.2 1.0 %copy-start.9 = (bf16[64,3072]{1,0:T(8,128)(2,1)}, bf16[64,3072]{1,0:T(8,128)(2,1)S(1)}, u32[]{:S(2)}) copy-start(bf16[64,3072]{1,0:T(8,128)(2,1)S(1)} %collective-permute-done.15.refs_5_) | copy-start | bytes 1179652
  (6 other events, 4.3 us)

commit v3 on v1

v3 whole, which is shorter than its diff:
```python
from functools import partial

import jax
import jax.numpy as jnp
from jax import lax
from jax.experimental import pallas as pl
from jax.experimental.pallas import tpu as pltpu
from jax.sharding import PartitionSpec as P

MINI = 64
gelu_coef = 0.7978845608028654
gelu_cubic = 0.044715
base_rate = 0.01
ln_eps = 1e-06

f32 = jnp.float32
bf16 = jnp.bfloat16
NN = ((1,), (0,))
NT = ((1,), (1,))
TN = ((0,), (0,))


def dot(left, right, dims=NN):
    return lax.dot_general(
        left.astype(bf16), right.astype(bf16), (dims, ((), ())), preferred_element_type=f32
    )


def lane_low(shape):
    return lax.broadcasted_iota(jnp.int32, shape, len(shape) - 1) < shape[-1] // 2


def blocks(cat):
    low = lane_low(cat.shape)
    zero = jnp.zeros_like(cat)
    return jnp.concatenate([jnp.where(low, cat, zero), jnp.where(low, zero, cat)], axis=0)


def lane_cat(rows):
    half = rows.shape[0] // 2
    return jnp.where(lane_low((half, rows.shape[1])), rows[:half], rows[half:])


PACK = 16


def project_kernel(count, pieces, first, ids_ref, *refs):
    x_refs, refs = refs[: count * pieces], refs[count * pieces :]
    if first:
        w_ref, wr_ref, bias_ref, kv_ref, q_ref, stack_ref, prod_s = refs
        d, base = w_ref.shape[0] // 3, 0
        stack_ref[: 3 * d, :] = w_ref[...]
        stack_ref[3 * d :, :] = jnp.broadcast_to(wr_ref[...], (d, wr_ref.shape[1]))
    else:
        stack_ref, bias_ref, early_ref, kv_ref, q_ref, prod_s = refs
        d = stack_ref.shape[0] // 4
        base = early_ref.shape[0]
        kv_ref[:base, :] = early_ref[...]
    mini = d
    both = 2 * mini
    part = x_refs[0].shape[1]
    x = jnp.concatenate([x_ref[...].reshape(-1, x_ref.shape[2]) for x_ref in x_refs], axis=0)
    prod = dot(x, stack_ref[...], NT)
    core = ids_ref[2]
    for i in range(count):
        for j in range(pieces):
            where = (core if j == 0 else 1 - core) * part if pieces > 1 else 0
            for video in range(2):
                row = ((i * pieces + j) * 2 + video) * part
                spot = i * both + video * mini + where
                if pieces > 1:
                    spot = pl.multiple_of(spot, part)
                prod_s[pl.ds(spot, part), :] = prod[row : row + part]
    eye = (
        lax.broadcasted_iota(jnp.int32, (both, both), 0)
        == lax.broadcasted_iota(jnp.int32, (both, both), 1)
    ).astype(f32)
    low = lane_low((mini, 2 * d))
    for i in range(count):
        prod = prod_s[pl.ds(i * both, both), :]
        qk, vr = prod[:, : 2 * d], prod[:, 2 * d :]
        qk_swap, vr_swap = pltpu.roll(qk, d, 1), pltpu.roll(vr, d, 1)
        keys = jnp.where(low, qk_swap[:mini], qk[mini:])
        queries = jnp.where(low, qk[:mini], qk_swap[mini:])
        values = jnp.where(low, vr[:mini], vr_swap[mini:])
        logits = jnp.where(lane_low(vr.shape), vr_swap, vr)
        logits = jnp.sum(logits * eye, axis=0, keepdims=True)
        rate = base_rate * jax.nn.sigmoid(logits + bias_ref[...]) / mini
        high = rate.astype(bf16).astype(f32)
        pad = jnp.zeros((PACK - 2, both), f32)
        at = base + i * (both + PACK)
        kv_ref[pl.ds(at, mini), :] = keys.astype(bf16)
        kv_ref[pl.ds(at + mini, mini), :] = values.astype(bf16)
        kv_ref[pl.ds(at + both, PACK), :] = jnp.concatenate([high, rate - high, pad], axis=0).astype(bf16)
        q_ref[pl.ds(i * mini, mini), :] = queries.astype(bf16)


def gelu_both(z):
    square = z * z
    tangent = jnp.tanh(z * (gelu_coef + (gelu_coef * gelu_cubic) * square))
    half = 0.5 * z
    value = half + half * tangent
    slope = (0.5 + 0.5 * tangent) + (half - half * (tangent * tangent)) * (
        gelu_coef + (3.0 * gelu_coef * gelu_cubic) * square
    )
    return value, slope


def gelu(z):
    tangent = jnp.tanh(z * (gelu_coef + (gelu_coef * gelu_cubic) * (z * z)))
    half = 0.5 * z
    return half + half * tangent


def chain_kernel(seq_count, ids_ref, *refs):
    kv_ref, refs = refs[0], refs[1:]
    q_early, q_late, gain_ref, bias_ref, w1_ref, b1_ref, w2_ref, b2_ref = refs[:8]
    out_ref, kv_s, q_s, w1_s, b1_s, w2_s, b2_s, z1_s = refs[8:]
    inner = w1_ref.shape[-1]
    both = gain_ref.shape[1] * 2
    d = both // 2
    mini = d
    minis = kv_s.shape[1]
    place, flip = ids_ref[0], ids_ref[1]
    gain = jnp.concatenate([gain_ref[...], gain_ref[...]], axis=1)
    bias = jnp.concatenate([bias_ref[...], bias_ref[...]], axis=1)
    gain_sq = gain * gain
    row_id = lax.broadcasted_iota(jnp.int32, (both, both), 0)
    lane_id = lax.broadcasted_iota(jnp.int32, (both, both), 1)
    same = ((row_id < mini) == (lane_id < mini)).astype(f32)
    causal = same * (row_id >= lane_id).astype(f32)
    ones = same.astype(bf16)
    pick = (
        lax.broadcasted_iota(jnp.int32, (mini, both), 0)
        == lax.rem(lax.broadcasted_iota(jnp.int32, (mini, both), 1), mini)
    ).astype(f32)

    def per_row(pair):
        return jnp.concatenate(
            [
                jnp.broadcast_to(pair[:1], (mini, inner)),
                jnp.broadcast_to(pair[1:], (mini, inner)),
            ],
            axis=0,
        )

    def halves(x):
        low = lane_low(x.shape)
        first = jnp.sum(jnp.where(low, x, 0.0), axis=1, keepdims=True)
        second = jnp.sum(jnp.where(low, 0.0, x), axis=1, keepdims=True)
        return jnp.concatenate([first, second], axis=0)

    def spread(col):
        low = lane_low((mini, both))
        return jnp.where(low, col[:mini], col[mini:])

    def keys_of(j, m):
        return kv_s[j, m, pl.ds(0, mini), :]

    def step(j, m, state, z1, kb, key_cat, nxt, query):
        w1, b1, w2, b2 = state
        w1h, w2h = w1.astype(bf16), w2.astype(bf16)
        value_cat = kv_s[j, m, pl.ds(mini, mini), :].astype(f32)
        rate_rows = kv_s[j, m, pl.ds(both, PACK), :].astype(f32)
        e = halves(pick * (rate_rows[:1] + rate_rows[1:2]))
        u = gain * (bias - (value_cat - key_cat.astype(f32)))
        u_mean = halves(u) * (1.0 / d)

        x2h, slope = gelu_both(z1)
        x2h = x2h.astype(bf16)
        z = lane_cat(dot(x2h, w2h)) + b2
        scaled = gain_sq * z
        rs = lax.rsqrt(halves(z * z) * (1.0 / d) + ln_eps)
        mean_g = rs * halves(scaled) * (1.0 / d) + u_mean
        mean_gn = rs * (rs * halves(scaled * z) + halves(u * z)) * (1.0 / d)
        alpha = e * rs
        pulled = dot(blocks(u), w2h, NT)
        back = dot(jnp.concatenate([blocks(scaled), blocks(z)], axis=0), w2h, NT)
        d1 = (alpha * rs) * (back[:both] - mean_gn * back[both:]) + alpha * pulled
        h1h = (d1 * slope).astype(bf16)
        h1 = h1h.astype(f32)
        h2 = spread(alpha) * ((gain_sq - spread(mean_gn)) * (spread(rs) * z) + (u - spread(mean_g)))
        h2h = blocks(h2).astype(bf16)

        z1_next, kb_next, result = None, None, None
        streams = [] if nxt is None else [blocks(nxt)]
        if query is not None:
            streams.append(blocks(query))
        streams = jnp.concatenate(streams, axis=0)
        against_keys = dot(streams, kb, NT)
        against_state = dot(streams, w1h)
        lhs = []
        if nxt is not None:
            kb_next = streams[:both]
            lhs += [(against_keys[:both] + same).astype(bf16)]
        if query is not None:
            lhs.append((causal * (against_keys[-both:] + 1.0)).astype(bf16))
        moved = dot(jnp.concatenate(lhs, axis=0), h1h)
        if nxt is not None:
            z1_next = against_state[:both] + per_row(b1) - moved[:both]
        if query is not None:
            first_bar = against_state[-both:] + per_row(b1) - moved[-both:]
            hidden_bar = gelu(first_bar).astype(bf16)
            attend_hidden = causal * (dot(hidden_bar, x2h, NT) + 1.0)
            zb = lane_cat(dot(hidden_bar, w2h) - dot(attend_hidden, h2h)) + b2
            var = spread(halves(zb * zb)) * (1.0 / d)
            result = query.astype(f32) + gain * (zb * lax.rsqrt(var + ln_eps)) + bias
            if nxt is None:
                return None, None, None, result

        w1 = w1 - dot(kb, h1h, TN)
        b1 = b1 - jnp.concatenate(
            [
                jnp.sum(h1[:mini], axis=0, keepdims=True),
                jnp.sum(h1[mini:], axis=0, keepdims=True),
            ],
            axis=0,
        )
        w2 = w2 - dot(x2h, h2h, TN)
        b2 = b2 - jnp.sum(h2, axis=0, keepdims=True)
        return (w1, b1, w2, b2), z1_next, kb_next, result

    for p in range(minis):
        at = pl.ds((p % (minis - 1)) * mini, mini)
        q_s[p ^ flip] = q_early[at, :] if p + 1 < minis else q_late[...]
    for j in range(seq_count):
        for p in range(minis):
            kv_s[j, p ^ flip] = kv_ref[j, pl.ds(p * (both + PACK), both + PACK), :]

    w2, b2 = w2_ref[0], b2_ref[...]
    w2 = w2 - jnp.mean(w2, axis=0, keepdims=True)
    b2 = b2 - jnp.mean(b2, axis=1, keepdims=True)
    w1_s[...] = jnp.concatenate([w1_ref[0], w1_ref[0]], axis=0)
    b1_s[...] = jnp.concatenate([b1_ref[...], b1_ref[...]], axis=0)
    w2_s[...] = jnp.concatenate([w2, w2], axis=0).T
    b2_s[...] = jnp.concatenate([b2, b2], axis=1)
    z1_s[...] = dot(blocks(keys_of(0, 0)), w1_s[...]) + per_row(b1_s[...])

    def segment(j, queries):
        state, z1 = (w1_s[...], b1_s[...], w2_s[...], b2_s[...]), z1_s[...]
        key_cat = keys_of(j, 0)
        kb = blocks(key_cat)
        for m in range(minis):
            if m + 1 < minis:
                nxt = keys_of(j, m + 1)
            else:
                nxt = None if queries else keys_of(j + 1, 0)
            query = q_s[m] if queries else None
            state, z1, kb, result = step(j, m, state, z1, kb, key_cat, nxt, query)
            if queries:
                out_ref[pl.ds(m * mini, mini), :] = result.astype(bf16)
            key_cat = nxt
        if not queries:
            w1_s[...], b1_s[...], w2_s[...], b2_s[...] = state
            z1_s[...] = z1

    def body(j, carry):
        segment(j, False)
        return carry

    lax.fori_loop(0, place, body, 0)
    segment(place, True)


def out_kernel(count, ids_ref, heads_ref, *refs):
    w_refs, out_ref = refs[:count], refs[count]
    _, rows, both = heads_ref.shape
    d = both // 2
    low = lane_low((rows, both))
    firsts, seconds = [], []
    per = heads_ref.shape[0] // count
    me = 2 * ids_ref[1] + ids_ref[2]
    order = [(me ^ i) * per + j for i in range(count) for j in range(per)]
    for h in range(0, len(order), 2):
        even, odd = heads_ref[order[h]].astype(f32), heads_ref[order[h + 1]].astype(f32)
        firsts.append(jnp.where(low, even, pltpu.roll(odd, d, 1)))
        seconds.append(jnp.where(low, pltpu.roll(even, d, 1), odd))
    lhs = jnp.concatenate(
        [jnp.concatenate(firsts, axis=1), jnp.concatenate(seconds, axis=1)], axis=0
    )
    weights = jnp.concatenate([w_ref[...] for w_ref in w_refs], axis=0)
    prod = dot(lhs, weights).astype(bf16)
    out_ref[0] = prod[:rows]
    out_ref[1] = prod[rows:]


def swapped(array, flip, senders=None):
    senders = range(lax.axis_size("row")) if senders is None else senders
    return lax.ppermute(array, "row", [(i, i ^ flip) for i in senders])


VMEM_LIMIT = 14 * 1024 * 1024


def on_device(
    tokens,
    w_qkv,
    w_rate,
    rate_bias,
    w_out,
    w_first_init,
    b_first_init,
    w_second_init,
    b_second_init,
    ln_gain,
    ln_bias,
):
    videos, tok_part, width = tokens.shape
    d = w_qkv.shape[0] // 3
    both = 2 * d
    row_count, seq_count = lax.axis_size("row"), lax.axis_size("seq")
    minis = tok_part * row_count // MINI
    paired = row_count == 8 and minis == 4
    vmem = pl.BlockSpec(memory_space=pltpu.VMEM)
    smem = pl.BlockSpec(memory_space=pltpu.SMEM)
    params = pltpu.CompilerParams(vmem_limit_bytes=VMEM_LIMIT)
    row = lax.axis_index("row") if paired else 0
    ids = jnp.stack([lax.axis_index("seq"), row // 2, row % 2]).astype(jnp.int32)
    bias = rate_bias.reshape(1, 1)

    def project(count, pieces, first, parts, weights, *before):
        rows = count * MINI
        total = count if first else minis
        out_shape = [
            jax.ShapeDtypeStruct((total * (2 * MINI + PACK), both), bf16),
            jax.ShapeDtypeStruct((rows, both), bf16),
        ]
        if first:
            out_shape.append(jax.ShapeDtypeStruct((4 * d, width), bf16))
        return pl.pallas_call(
            partial(project_kernel, count, pieces, first),
            out_shape=out_shape,
            in_specs=[smem] + [vmem] * (len(parts) + len(weights) + 1 + len(before)),
            out_specs=[vmem] * len(out_shape),
            scratch_shapes=[pltpu.VMEM((2 * rows, 4 * d), f32)],
            compiler_params=params,
            cost_estimate=pl.CostEstimate(
                flops=16 * rows * d * width, bytes_accessed=4_000_000, transcendentals=0
            ),
            name="project" if first else "finish",
        )(ids, *parts, *weights, bias, *before)

    if paired:
        far, near, own, w_own = lax.optimization_barrier(
            (swapped(tokens, 4), swapped(tokens, 2), swapped(tokens, 1), swapped(w_out, 1))
        )
        last = swapped(far, 2)
        w_early, _ = lax.optimization_barrier((w_out, far))
        w_mid = swapped(w_early, 6, (2, 3, 4, 5))
        early = [tokens, own, near, swapped(near, 1), far, swapped(far, 1)]
        kv_early, q_early, stack = project(3, 2, True, early, (w_qkv, w_rate))
        last, kv_early, w_mid = lax.optimization_barrier((last, kv_early, w_mid))
        late = [last, swapped(last, 1)]
        w_after, _ = lax.optimization_barrier((w_out, last))
        w_parts = [w_out, swapped(w_after, 2), swapped(w_after, 4), swapped(w_after, 6, (0, 1, 6, 7))]
        kv, q_late = project(1, 2, False, late, (stack,), kv_early)
    else:
        whole = lax.all_gather(tokens, "row", axis=1, tiled=True)
        whole = whole.reshape(videos, minis, MINI, width)
        parts = [whole[:, m] for m in range(minis)]
        kv_early, q_early, stack = project(minis - 1, 1, True, parts[:-1], (w_qkv, w_rate))
        kv, q_late = project(1, 1, False, parts[-1:], (stack,), kv_early)
        w_parts = [lax.all_gather(w_out, "row", axis=0, tiled=True)]

    inner = w_first_init.shape[2]
    operands = [lax.all_gather(kv, "seq"), q_early, q_late, ln_gain, ln_bias]
    operands += [w_first_init, b_first_init]
    operands += [jnp.swapaxes(w_second_init, 1, 2), b_second_init]
    heads = pl.pallas_call(
        partial(chain_kernel, seq_count),
        out_shape=jax.ShapeDtypeStruct((minis * MINI, both), bf16),
        in_specs=[smem] + [vmem] * len(operands),
        out_specs=vmem,
        scratch_shapes=[
            pltpu.VMEM((seq_count, minis, 2 * MINI + PACK, both), bf16),
            pltpu.VMEM((minis, MINI, both), bf16),
            pltpu.VMEM((both, inner), f32),
            pltpu.VMEM((2, inner), f32),
            pltpu.VMEM((inner, both), f32),
            pltpu.VMEM((1, both), f32),
            pltpu.VMEM((2 * MINI, inner), f32),
        ],
        compiler_params=params,
        name="chain",
    )(ids, *operands)
    if paired:
        w_parts = list(lax.optimization_barrier((heads, *w_parts))[1:])
        w_parts[3] = w_parts[3] + w_mid
        w_parts = [w_parts[0], w_own] + [x for w in w_parts[1:] for x in (w, swapped(w, 1))]
    heads = heads.reshape(row_count, tok_part, both)
    arrived = lax.all_to_all(heads, "row", split_axis=0, concat_axis=0, tiled=True)
    return pl.pallas_call(
        partial(out_kernel, len(w_parts)),
        out_shape=jax.ShapeDtypeStruct((videos, tok_part, width), bf16),
        in_specs=[smem, vmem] + [vmem] * len(w_parts),
        out_specs=vmem,
        compiler_params=params,
        name="mix",
    )(ids, arrived, *w_parts)


def solution(mesh):
    in_specs = (
        P(None, ("seq", "row"), None),
        P("row", None),
        P("row", None),
        P("row"),
        P("row", None),
        P("row", None, None),
        P("row", None),
        P("row", None, None),
        P("row", None),
        P("row", None),
        P("row", None),
    )
    out_specs = P(None, ("seq", "row"), None)
    return jax.shard_map(
        on_device, mesh=mesh, in_specs=in_specs, out_specs=out_specs, check_vma=False
    )
```

time: 104 us -> 80.8 us (0.78)
  the two profiles are of different devices: /device:TPU:6 before, /device:TPU:0 now
where the time goes in v3:
time: 80.8 us; the launch traced here: 80.5 us
  waiting for transfers between devices  30.4 us (38%)
  blocking collectives  19.7 us (24%)
  starting transfers between devices  17.3 us (21%)
  Pallas kernels  9.02 us (11%)
  local copies, waits for them, and re-layouts  3.01 us (4%)
  between operations  0.85 us (1%)
    ppermute x15, waiting for transfers between devices, swapped(): return lax.ppermute(array, 'row', [(i, i ^ flip) for i in senders])  30.4 us
    ppermute x15, starting transfers between devices, swapped(): return lax.ppermute(array, 'row', [(i, i ^ flip) for i in senders])  17.3 us
    all_gather x1, blocking collectives, on_device(): operands = [lax.all_gather(kv, 'seq'), q_early, q_late, ln_gain, ln_bias]  10.3 us
    all_to_all x1, blocking collectives, on_device(): lax.all_to_all(heads, 'row', split_axis=0, concat_axis=0, tiled=True)  9.4 us
    pallas_call x1, Pallas kernels, on_device(): pl.pallas_call(partial(chain_kernel, seq_count), out_shape=jax.ShapeDtype...  4.19 us
    unnamed x20, local copies, waits for them, and re-layouts  3.01 us
    pallas_call x2, Pallas kernels, project(): pl.pallas_call(partial(project_kernel, count, pieces, first), out_shape=o...  2.81 us
    pallas_call x1, Pallas kernels, on_device(): pl.pallas_call(partial(out_kernel, len(w_parts)), out_shape=jax.ShapeDtyp...  2.01 us
  transfers between devices with their start and end apart: 15, of which 5 were waited for; matrix products, arithmetic and copies ran while one was open for 0% of the time, Pallas kernels for 9%

profile of v3, /device:TPU:0, one launch (start us, length us, event | category | flops | bytes accessed | tf_op | source)
XLA Modules:
  0.0 80.5 jit_solution(17002977924972619664)
XLA Ops:
  0.0 4.0 %collective-permute-start = (bf16[2,32,3072]{2,1,0:T(8,128)(2,1)}, bf16[2,32,3072]{2,1,0:T(8,128)(2,1)S(1)}, u32[]{:S(2)}, u32[]{:S(2)}) collective-permute-start(bf16[2,32,3072]{2,1,0:T(8,128)(2,1)} %refs_0_.1), channel_id=1, source_target_pairs={{0,4},{1,5},{2,6},{3,7},{4,0},{5,1},{6,2},{7,3},{8,12},{9,13},{10,... | collective-permute-start | bytes 1179656 | tf_op jit(solution)/shard_map/ppermute | solution.py:289
  4.0 1.6 %collective-permute-start.1 = (bf16[2,32,3072]{2,1,0:T(8,128)(2,1)}, bf16[2,32,3072]{2,1,0:T(8,128)(2,1)S(1)}, u32[]{:S(2)}, u32[]{:S(2)}) collective-permute-start(bf16[2,32,3072]{2,1,0:T(8,128)(2,1)} %refs_0_.1), channel_id=1, source_target_pairs={{0,2},{1,3},{2,0},{3,1},{4,6},{5,7},{6,4},{7,5},{8,10},{9,11},{10,... | collective-permute-start | bytes 1179656 | tf_op jit(solution)/shard_map/ppermute | solution.py:289
  5.6 0.5 collective-permute-start.3
  6.1 15.8 %collective-permute-done.refs_4_ = bf16[2,32,3072]{2,1,0:T(8,128)(2,1)S(1)} collective-permute-done((bf16[2,32,3072]{2,1,0:T(8,128)(2,1)}, bf16[2,32,3072]{2,1,0:T(8,128)(2,1)S(1)}, u32[]{:S(2)}, u32[]{:S(2)}) %collective-permute-start) | collective-permute-done | bytes 393248 | tf_op jit(solution)/shard_map/ppermute | solution.py:289
  21.9 0.2 collective-permute-done.1.refs_2_
  22.1 0.5 collective-permute-start.5
  22.6 0.7 collective-permute-start.7
  23.3 3.2 %collective-permute-start.4 = (bf16[2,32,3072]{2,1,0:T(8,128)(2,1)S(1)}, bf16[2,32,3072]{2,1,0:T(8,128)(2,1)S(1)}, u32[]{:S(2)}, u32[]{:S(2)}) collective-permute-start(bf16[2,32,3072]{2,1,0:T(8,128)(2,1)S(1)} %collective-permute-done.refs_4_), channel_id=1, source_target_pairs={{0,2},{1,3},{2,0},{3,1},{4,6},{5,7},{6,4},{7,5},{8,10},{9,11},{10,... | collective-permute-start | bytes 1179656 | tf_op jit(solution)/shard_map/ppermute | solution.py:289
  27.2 0.1 pad_add_fusion.ids_ref
  27.3 1.3 %copy-done = bf16[192,3072]{1,0:T(8,128)(2,1)S(1)} copy-done((bf16[192,3072]{1,0:T(8,128)(2,1)S(1)}, bf16[192,3072]{1,0:T(8,128)(2,1)}, u32[]{:S(2)}) %copy-start) | copy-done | bytes 1179672
  28.5 1.0 %copy-done.1 = bf16[2,32,3072]{2,1,0:T(8,128)(2,1)S(1)} copy-done((bf16[2,32,3072]{2,1,0:T(8,128)(2,1)S(1)}, bf16[2,32,3072]{2,1,0:T(8,128)(2,1)}, u32[]{:S(2)}) %copy-start.1) | copy-done | bytes 393240
  29.5 0.7 copy-done.5
  30.2 1.5 %project.1 = (bf16[432,128]{1,0:T(8,128)(2,1)S(1)}, bf16[192,128]{1,0:T(8,128)(2,1)S(1)}, bf16[256,3072]{1,0:T(8,128)(2,1)S(1)}) custom-call(s32[3]{0:T(128)S(1)} %pad_add_fusion.ids_ref, bf16[2,32,3072]{2,1,0:T(8,128)(2,1)S(1)} %copy-done.1, bf16[2,32,3072]{2,1,0:T(8,128)(2,1)S(1)} %collective-permute-done.2.refs_1_, ...), custom_call_target="tpu_custom_call" | custom-call | flops 603979776 | bytes 4000000 | tf_op jit(solution)/shard_map/project/pallas_call | solution.py:330
  31.8 3.8 %collective-permute-done.4.refs_0_ = bf16[2,32,3072]{2,1,0:T(8,128)(2,1)S(1)} collective-permute-done((bf16[2,32,3072]{2,1,0:T(8,128)(2,1)S(1)}, bf16[2,32,3072]{2,1,0:T(8,128)(2,1)S(1)}, u32[]{:S(2)}, u32[]{:S(2)}) %collective-permute-start.4) | collective-permute-done | bytes 393248 | tf_op jit(solution)/shard_map/ppermute | solution.py:289
  35.6 2.7 %collective-permute-start.10 = (bf16[64,3072]{1,0:T(8,128)(2,1)S(1)}, bf16[64,3072]{1,0:T(8,128)(2,1)S(1)}, u32[]{:S(2)}, u32[]{:S(2)}) collective-permute-start(bf16[64,3072]{1,0:T(8,128)(2,1)S(1)} %copy-done.2), channel_id=1, source_target_pairs={{0,4},{1,5},{2,6},{3,7},{4,0},{5,1},{6,2},{7,3},{8,12},{9,13},{10,... | collective-permute-start | bytes 1179656 | tf_op jit(solution)/shard_map/ppermute | solution.py:289
  38.3 3.3 %collective-permute-start.11 = (bf16[64,3072]{1,0:T(8,128)(2,1)S(1)}, bf16[64,3072]{1,0:T(8,128)(2,1)S(1)}, u32[]{:S(2)}, u32[]{:S(2)}) collective-permute-start(bf16[64,3072]{1,0:T(8,128)(2,1)S(1)} %copy-done.2), channel_id=1, source_target_pairs={{0,6},{1,7},{6,0},{7,1},{8,14},{9,15},{14,8},{15,9},{16,22},{17,23... | collective-permute-start | bytes 1179656 | tf_op jit(solution)/shard_map/ppermute | solution.py:289
  41.6 0.1 collective-permute-start.9
  41.7 0.0 copy-start.3
  41.7 0.0 copy-start.4
  41.8 0.0 copy-start.8
  41.8 0.0 copy-start.9
  41.8 1.3 %finish.1 = (bf16[576,128]{1,0:T(8,128)(2,1)S(1)}, bf16[64,128]{1,0:T(8,128)(2,1)S(1)}) custom-call(s32[3]{0:T(128)S(1)} %pad_add_fusion.ids_ref, bf16[2,32,3072]{2,1,0:T(8,128)(2,1)S(1)} %collective-permute-done.4.refs_0_, bf16[2,32,3072]{2,1,0:T(8,128)(2,1)S(1)} %collective-permute-done.8.refs_1_, bf16[256,3072]{1,0:T(8,128)(2,1)S(1)} %get-tuple-element.29.refs_2_, ...), custom_call_target="tpu_custom_call" | custom-call | flops 201326592 | bytes 4000000 | tf_op jit(solution)/shard_map/finish/pallas_call | solution.py:330
  43.1 10.3 %all-gather = bf16[2304,128]{1,0:T(8,128)(2,1)S(1)} all-gather(bf16[576,128]{1,0:T(8,128)(2,1)S(1)} %get-tuple-element.31), channel_id=2, replica_groups=mesh['seq'=4,'row'=8] {'seq'}, dimensions={0}, use_global_device_ids=true | all-gather | bytes 737280 | tf_op jit(solution)/shard_map/all_gather | solution.py:366
  53.5 4.2 %chain.1 = bf16[256,128]{1,0:T(8,128)(2,1)S(1)} custom-call(s32[3]{0:T(128)S(1)} %pad_add_fusion.ids_ref, bf16[4,576,128]{2,1,0:T(8,128)(2,1)S(1)} %bitcast.9, bf16[192,128]{1,0:T(8,128)(2,1)S(1)} %get-tuple-element.32.refs_1_, bf16[64,128]{1,0:T(8,128)(2,1)S(1)} %get-tuple-element.33.refs_2_, f32[1,64]{1,0:T(1,128)S(1)} %copy-done.7, ...), custom_call_target="tpu_custom_call" | custom-call | tf_op jit(solution)/shard_map/chain/pallas_call | solution.py:369
  57.7 7.4 %collective-permute-done.10.refs_4_ = bf16[64,3072]{1,0:T(8,128)(2,1)S(1)} collective-permute-done((bf16[64,3072]{1,0:T(8,128)(2,1)S(1)}, bf16[64,3072]{1,0:T(8,128)(2,1)S(1)}, u32[]{:S(2)}, u32[]{:S(2)}) %collective-permute-start.10) | collective-permute-done | bytes 393248 | tf_op jit(solution)/shard_map/ppermute | solution.py:289
  65.1 3.2 %collective-permute-done.9.refs_2_ = bf16[64,3072]{1,0:T(8,128)(2,1)S(1)} collective-permute-done((bf16[64,3072]{1,0:T(8,128)(2,1)S(1)}, bf16[64,3072]{1,0:T(8,128)(2,1)S(1)}, u32[]{:S(2)}, u32[]{:S(2)}) %collective-permute-start.9) | collective-permute-done | bytes 393248 | tf_op jit(solution)/shard_map/ppermute | solution.py:289
  68.3 0.1 add.9.refs_6_
  68.4 0.1 collective-permute-start.14
  68.5 0.5 collective-permute-start.12
  69.0 0.1 collective-permute-start.13
  69.1 9.4 %all_to_all.5.heads_ref = bf16[8,32,128]{2,1,0:T(8,128)(2,1)S(1)} all-to-all(bf16[8,32,128]{2,1,0:T(8,128)(2,1)S(1)} %bitcast.10), channel_id=1, replica_groups=mesh['seq'=4,'row'=8] {'row'}, dimensions={0} | all-to-all | bytes 131072 | tf_op jit(solution)/shard_map/all_to_all | solution.py:391
  78.5 2.0 %mix.1 = bf16[2,32,3072]{2,1,0:T(8,128)(2,1)} custom-call(s32[3]{0:T(128)S(1)} %pad_add_fusion.ids_ref, bf16[8,32,128]{2,1,0:T(8,128)(2,1)S(1)} %all_to_all.5.heads_ref, bf16[64,3072]{1,0:T(8,128)(2,1)S(1)} %copy-done.2, bf16[64,3072]{1,0:T(8,128)(2,1)S(1)} %collective-permute-done.3.refs_1_, bf16[64,3072]{1,0:T(8,128)(2,1)S(1)} %collective-permute-done.9.refs_2_, ...), custom_call_target="tpu_custom_call" | custom-call | tf_op jit(solution)/shard_map/mix/pallas_call | solution.py:392
  (26 shorter events, 0.1 us)
Async XLA Ops:
  0.0 21.9 %collective-permute-start = (bf16[2,32,3072]{2,1,0:T(8,128)(2,1)}, bf16[2,32,3072]{2,1,0:T(8,128)(2,1)S(1)}, u32[]{:S(2)}, u32[]{:S(2)}) collective-permute-start(bf16[2,32,3072]{2,1,0:T(8,128)(2,1)} %refs_0_.1), channel_id=1, source_target_pairs={{0,4},{1,5},{2,6},{3,7},{4,0},{5,1},{6,2},{7,3},{8,12},{9,13},{10,... | collective-permute-start | bytes 1179656 | tf_op jit(solution)/shard_map/ppermute | solution.py:289
  4.0 18.0 %collective-permute-start.1 = (bf16[2,32,3072]{2,1,0:T(8,128)(2,1)}, bf16[2,32,3072]{2,1,0:T(8,128)(2,1)S(1)}, u32[]{:S(2)}, u32[]{:S(2)}) collective-permute-start(bf16[2,32,3072]{2,1,0:T(8,128)(2,1)} %refs_0_.1), channel_id=1, source_target_pairs={{0,2},{1,3},{2,0},{3,1},{4,6},{5,7},{6,4},{7,5},{8,10},{9,11},{10,... | collective-permute-start | bytes 1179656 | tf_op jit(solution)/shard_map/ppermute | solution.py:289
  5.6 16.5 %collective-permute-start.2 = (bf16[2,32,3072]{2,1,0:T(8,128)(2,1)}, bf16[2,32,3072]{2,1,0:T(8,128)(2,1)S(1)}, u32[]{:S(2)}, u32[]{:S(2)}) collective-permute-start(bf16[2,32,3072]{2,1,0:T(8,128)(2,1)} %refs_0_.1), channel_id=1, source_target_pairs={{0,1},{1,0},{2,3},{3,2},{4,5},{5,4},{6,7},{7,6},{8,9},{9,8},{10,11... | collective-permute-start | bytes 1179656 | tf_op jit(solution)/shard_map/ppermute | solution.py:289
  5.6 16.5 %collective-permute-start.3 = (bf16[64,3072]{1,0:T(8,128)(2,1)}, bf16[64,3072]{1,0:T(8,128)(2,1)S(1)}, u32[]{:S(2)}, u32[]{:S(2)}) collective-permute-start(bf16[64,3072]{1,0:T(8,128)(2,1)} %refs_0_.2), channel_id=1, source_target_pairs={{0,1},{1,0},{2,3},{3,2},{4,5},{5,4},{6,7},{7,6},{8,9},{9,8},{10,11... | collective-permute-start | bytes 1179656 | tf_op jit(solution)/shard_map/ppermute | solution.py:289
  22.1 5.2 %collective-permute-start.6 = (bf16[2,32,3072]{2,1,0:T(8,128)(2,1)S(1)}, bf16[2,32,3072]{2,1,0:T(8,128)(2,1)S(1)}, u32[]{:S(2)}, u32[]{:S(2)}) collective-permute-start(bf16[2,32,3072]{2,1,0:T(8,128)(2,1)S(1)} %collective-permute-done.refs_4_), channel_id=1, source_target_pairs={{0,1},{1,0},{2,3},{3,2},{4,5},{5,4},{6,7},{7,6},{8,9},{9,8},{10,11... | collective-permute-start | bytes 1179656 | tf_op jit(solution)/shard_map/ppermute | solution.py:289
  22.1 5.2 %collective-permute-start.5 = (bf16[2,32,3072]{2,1,0:T(8,128)(2,1)S(1)}, bf16[2,32,3072]{2,1,0:T(8,128)(2,1)S(1)}, u32[]{:S(2)}, u32[]{:S(2)}) collective-permute-start(bf16[2,32,3072]{2,1,0:T(8,128)(2,1)S(1)} %collective-permute-done.1.refs_2_), channel_id=1, source_target_pairs={{0,1},{1,0},{2,3},{3,2},{4,5},{5,4},{6,7},{7,6},{8,9},{9,8},{10,11... | collective-permute-start | bytes 1179656 | tf_op jit(solution)/shard_map/ppermute | solution.py:289
  22.6 9.1 %collective-permute-start.7 = (bf16[64,3072]{1,0:T(8,128)(2,1)}, bf16[64,3072]{1,0:T(8,128)(2,1)S(1)}, u32[]{:S(2)}, u32[]{:S(2)}) collective-permute-start(bf16[64,3072]{1,0:T(8,128)(2,1)} %refs_0_.2), channel_id=1, source_target_pairs={{2,4},{3,5},{4,2},{5,3},{10,12},{11,13},{12,10},{13,11},{18,20},{1... | collective-permute-start | bytes 1179656 | tf_op jit(solution)/shard_map/ppermute | solution.py:289
  23.3 12.3 %collective-permute-start.4 = (bf16[2,32,3072]{2,1,0:T(8,128)(2,1)S(1)}, bf16[2,32,3072]{2,1,0:T(8,128)(2,1)S(1)}, u32[]{:S(2)}, u32[]{:S(2)}) collective-permute-start(bf16[2,32,3072]{2,1,0:T(8,128)(2,1)S(1)} %collective-permute-done.refs_4_), channel_id=1, source_target_pairs={{0,2},{1,3},{2,0},{3,1},{4,6},{5,7},{6,4},{7,5},{8,10},{9,11},{10,... | collective-permute-start | bytes 1179656 | tf_op jit(solution)/shard_map/ppermute | solution.py:289
  27.3 1.3 %copy-start = (bf16[192,3072]{1,0:T(8,128)(2,1)S(1)}, bf16[192,3072]{1,0:T(8,128)(2,1)}, u32[]{:S(2)}) copy-start(bf16[192,3072]{1,0:T(8,128)(2,1)} %refs_6_.2) | copy-start | bytes 3538948
  28.5 1.0 %copy-start.1 = (bf16[2,32,3072]{2,1,0:T(8,128)(2,1)S(1)}, bf16[2,32,3072]{2,1,0:T(8,128)(2,1)}, u32[]{:S(2)}) copy-start(bf16[2,32,3072]{2,1,0:T(8,128)(2,1)} %refs_0_.1) | copy-start | bytes 1179652
  29.5 0.7 copy-start.5
  30.2 5.4 %copy-start.2 = (bf16[64,3072]{1,0:T(8,128)(2,1)S(1)}, bf16[64,3072]{1,0:T(8,128)(2,1)}, u32[]{:S(2)}) copy-start(bf16[64,3072]{1,0:T(8,128)(2,1)} %refs_0_.2) | copy-start | bytes 1179652
  35.6 6.1 %collective-permute-start.8 = (bf16[2,32,3072]{2,1,0:T(8,128)(2,1)S(1)}, bf16[2,32,3072]{2,1,0:T(8,128)(2,1)S(1)}, u32[]{:S(2)}, u32[]{:S(2)}) collective-permute-start(bf16[2,32,3072]{2,1,0:T(8,128)(2,1)S(1)} %collective-permute-done.4.refs_0_), channel_id=1, source_target_pairs={{0,1},{1,0},{2,3},{3,2},{4,5},{5,4},{6,7},{7,6},{8,9},{9,8},{10,11... | collective-permute-start | bytes 1179656 | tf_op jit(solution)/shard_map/ppermute | solution.py:289
  35.6 29.5 %collective-permute-start.10 = (bf16[64,3072]{1,0:T(8,128)(2,1)S(1)}, bf16[64,3072]{1,0:T(8,128)(2,1)S(1)}, u32[]{:S(2)}, u32[]{:S(2)}) collective-permute-start(bf16[64,3072]{1,0:T(8,128)(2,1)S(1)} %copy-done.2), channel_id=1, source_target_pairs={{0,4},{1,5},{2,6},{3,7},{4,0},{5,1},{6,2},{7,3},{8,12},{9,13},{10,... | collective-permute-start | bytes 1179656 | tf_op jit(solution)/shard_map/ppermute | solution.py:289
  38.3 26.7 %collective-permute-start.11 = (bf16[64,3072]{1,0:T(8,128)(2,1)S(1)}, bf16[64,3072]{1,0:T(8,128)(2,1)S(1)}, u32[]{:S(2)}, u32[]{:S(2)}) collective-permute-start(bf16[64,3072]{1,0:T(8,128)(2,1)S(1)} %copy-done.2), channel_id=1, source_target_pairs={{0,6},{1,7},{6,0},{7,1},{8,14},{9,15},{14,8},{15,9},{16,22},{17,23... | collective-permute-start | bytes 1179656 | tf_op jit(solution)/shard_map/ppermute | solution.py:289
  41.6 26.7 %collective-permute-start.9 = (bf16[64,3072]{1,0:T(8,128)(2,1)S(1)}, bf16[64,3072]{1,0:T(8,128)(2,1)S(1)}, u32[]{:S(2)}, u32[]{:S(2)}) collective-permute-start(bf16[64,3072]{1,0:T(8,128)(2,1)S(1)} %copy-done.2), channel_id=1, source_target_pairs={{0,2},{1,3},{2,0},{3,1},{4,6},{5,7},{6,4},{7,5},{8,10},{9,11},{10,... | collective-permute-start | bytes 1179656 | tf_op jit(solution)/shard_map/ppermute | solution.py:289
  41.7 11.7 %copy-start.3 = (f32[1,64,256]{2,1,0:T(8,128)S(1)}, f32[1,64,256]{2,1,0:T(8,128)}, u32[]{:S(2)}) copy-start(f32[1,64,256]{2,1,0:T(8,128)} %refs_5_.1) | copy-start | bytes 196612
  41.7 11.7 %copy-start.4 = (f32[1,256,64]{1,2,0:T(8,128)S(1)}, f32[1,256,64]{1,2,0:T(8,128)}, u32[]{:S(2)}) copy-start(f32[1,256,64]{1,2,0:T(8,128)} %param.18) | copy-start | bytes 196612
  41.7 11.7 %copy-start.6 = (f32[1,256]{1,0:T(1,128)S(1)}, f32[1,256]{1,0:T(1,128)}, u32[]{:S(2)}) copy-start(f32[1,256]{1,0:T(1,128)} %refs_6_.3) | copy-start | bytes 3076
  41.8 11.7 %copy-start.7 = (f32[1,64]{1,0:T(1,128)S(1)}, f32[1,64]{1,0:T(1,128)}, u32[]{:S(2)}) copy-start(f32[1,64]{1,0:T(1,128)} %refs_3_.1) | copy-start | bytes 772
  41.8 11.7 %copy-start.8 = (f32[1,64]{1,0:T(1,128)S(1)}, f32[1,64]{1,0:T(1,128)}, u32[]{:S(2)}) copy-start(f32[1,64]{1,0:T(1,128)} %refs_4_.1) | copy-start | bytes 772
  41.8 11.7 %copy-start.9 = (f32[1,64]{1,0:T(1,128)S(1)}, f32[1,64]{1,0:T(1,128)}, u32[]{:S(2)}) copy-start(f32[1,64]{1,0:T(1,128)} %refs_8_.1) | copy-start | bytes 772
  68.4 10.1 %collective-permute-start.14 = (bf16[64,3072]{1,0:T(8,128)(2,1)S(1)}, bf16[64,3072]{1,0:T(8,128)(2,1)S(1)}, u32[]{:S(2)}, u32[]{:S(2)}) collective-permute-start(bf16[64,3072]{1,0:T(8,128)(2,1)S(1)} %add.9.refs_6_), channel_id=1, source_target_pairs={{0,1},{1,0},{2,3},{3,2},{4,5},{5,4},{6,7},{7,6},{8,9},{9,8},{10,11... | collective-permute-start | bytes 1179656 | tf_op jit(solution)/shard_map/ppermute | solution.py:289
  68.5 10.0 %collective-permute-start.12 = (bf16[64,3072]{1,0:T(8,128)(2,1)S(1)}, bf16[64,3072]{1,0:T(8,128)(2,1)S(1)}, u32[]{:S(2)}, u32[]{:S(2)}) collective-permute-start(bf16[64,3072]{1,0:T(8,128)(2,1)S(1)} %collective-permute-done.9.refs_2_), channel_id=1, source_target_pairs={{0,1},{1,0},{2,3},{3,2},{4,5},{5,4},{6,7},{7,6},{8,9},{9,8},{10,11... | collective-permute-start | bytes 1179656 | tf_op jit(solution)/shard_map/ppermute | solution.py:289
  69.0 9.5 %collective-permute-start.13 = (bf16[64,3072]{1,0:T(8,128)(2,1)S(1)}, bf16[64,3072]{1,0:T(8,128)(2,1)S(1)}, u32[]{:S(2)}, u32[]{:S(2)}) collective-permute-start(bf16[64,3072]{1,0:T(8,128)(2,1)S(1)} %collective-permute-done.10.refs_4_), channel_id=1, source_target_pairs={{0,1},{1,0},{2,3},{3,2},{4,5},{5,4},{6,7},{7,6},{8,9},{9,8},{10,11... | collective-permute-start | bytes 1179656 | tf_op jit(solution)/shard_map/ppermute | solution.py:289

commit v4 on v3

--- a/solution.py
+++ b/solution.py
@@ -263,30 +263,37 @@
 
 
 def out_kernel(count, ids_ref, heads_ref, *refs):
-    w_refs, out_ref = refs[:count], refs[count]
-    _, rows, both = heads_ref.shape
+    w_refs, refs = refs[:count], refs[count:]
+    out_ref = refs[0]
+    heads, rows, both = heads_ref.shape
     d = both // 2
     low = lane_low((rows, both))
+    me = 2 * ids_ref[1] + ids_ref[2]
+    order = list(range(heads)) if count == 1 else [me ^ i for i in range(heads)]
     firsts, seconds = [], []
-    per = heads_ref.shape[0] // count
-    me = 2 * ids_ref[1] + ids_ref[2]
-    order = [(me ^ i) * per + j for i in range(count) for j in range(per)]
-    for h in range(0, len(order), 2):
+    for h in range(0, heads, 2):
         even, odd = heads_ref[order[h]].astype(f32), heads_ref[order[h + 1]].astype(f32)
         firsts.append(jnp.where(low, even, pltpu.roll(odd, d, 1)))
         seconds.append(jnp.where(low, pltpu.roll(even, d, 1), odd))
     lhs = jnp.concatenate(
         [jnp.concatenate(firsts, axis=1), jnp.concatenate(seconds, axis=1)], axis=0
     )
-    weights = jnp.concatenate([w_ref[...] for w_ref in w_refs], axis=0)
-    prod = dot(lhs, weights).astype(bf16)
+    weights = [w_ref[...] for w_ref in w_refs]
+    if count > 1:
+        w_s = refs[1]
+        share = d // 4
+        for i in range(2):
+            for flip in range(4):
+                at = pl.multiple_of(i * d + (ids_ref[0] ^ flip) * share, share)
+                w_s[pl.ds(at, share), :] = w_refs[count - 2 + i][pl.ds(flip * share, share), :]
+        weights = weights[:-2] + [w_s[...]]
+    prod = dot(lhs, jnp.concatenate(weights, axis=0)).astype(bf16)
     out_ref[0] = prod[:rows]
     out_ref[1] = prod[rows:]
 
 
-def swapped(array, flip, senders=None):
-    senders = range(lax.axis_size("row")) if senders is None else senders
-    return lax.ppermute(array, "row", [(i, i ^ flip) for i in senders])
+def swapped(array, flip, axis="row"):
+    return lax.ppermute(array, axis, [(i, i ^ flip) for i in range(lax.axis_size(axis))])
 
 
 VMEM_LIMIT = 14 * 1024 * 1024
@@ -310,7 +317,7 @@
     both = 2 * d
     row_count, seq_count = lax.axis_size("row"), lax.axis_size("seq")
     minis = tok_part * row_count // MINI
-    paired = row_count == 8 and minis == 4
+    paired = row_count == 8 and minis == 4 and seq_count == 4 and d == 64
     vmem = pl.BlockSpec(memory_space=pltpu.VMEM)
     smem = pl.BlockSpec(memory_space=pltpu.SMEM)
     params = pltpu.CompilerParams(vmem_limit_bytes=VMEM_LIMIT)
@@ -341,18 +348,24 @@
         )(ids, *parts, *weights, bias, *before)
 
     if paired:
-        far, near, own, w_own = lax.optimization_barrier(
-            (swapped(tokens, 4), swapped(tokens, 2), swapped(tokens, 1), swapped(w_out, 1))
+        share = w_out.shape[0] // seq_count
+        place = lax.axis_index("seq")
+        far, near = swapped(tokens, 4), swapped(tokens, 2)
+        own, w_own = swapped(tokens, 1), swapped(w_out, 1)
+        w_share = swapped(lax.dynamic_slice_in_dim(w_out, place * share, share, 0), 6)
+        w_end = [w_share] + [swapped(w_share, flip, "seq") for flip in range(1, seq_count)]
+        w_end = jnp.concatenate(w_end, axis=0)
+        w_end_other = swapped(w_end, 1)
+        far, near, own, w_own, w_end, w_end_other = lax.optimization_barrier(
+            (far, near, own, w_own, w_end, w_end_other)
         )
         last = swapped(far, 2)
-        w_early, _ = lax.optimization_barrier((w_out, far))
-        w_mid = swapped(w_early, 6, (2, 3, 4, 5))
         early = [tokens, own, near, swapped(near, 1), far, swapped(far, 1)]
         kv_early, q_early, stack = project(3, 2, True, early, (w_qkv, w_rate))
-        last, kv_early, w_mid = lax.optimization_barrier((last, kv_early, w_mid))
+        last, kv_early = lax.optimization_barrier((last, kv_early))
         late = [last, swapped(last, 1)]
         w_after, _ = lax.optimization_barrier((w_out, last))
-        w_parts = [w_out, swapped(w_after, 2), swapped(w_after, 4), swapped(w_after, 6, (0, 1, 6, 7))]
+        w_far, w_near = swapped(w_after, 4), swapped(w_after, 2)
         kv, q_late = project(1, 2, False, late, (stack,), kv_early)
     else:
         whole = lax.all_gather(tokens, "row", axis=1, tiled=True)
@@ -384,9 +397,9 @@
         name="chain",
     )(ids, *operands)
     if paired:
-        w_parts = list(lax.optimization_barrier((heads, *w_parts))[1:])
-        w_parts[3] = w_parts[3] + w_mid
-        w_parts = [w_parts[0], w_own] + [x for w in w_parts[1:] for x in (w, swapped(w, 1))]
+        w_far, w_near, _ = lax.optimization_barrier((w_far, w_near, heads))
+        w_parts = [w_out, w_own, w_near, swapped(w_near, 1), w_far, swapped(w_far, 1)]
+        w_parts += [w_end, w_end_other]
     heads = heads.reshape(row_count, tok_part, both)
     arrived = lax.all_to_all(heads, "row", split_axis=0, concat_axis=0, tiled=True)
     return pl.pallas_call(
@@ -394,6 +407,7 @@
         out_shape=jax.ShapeDtypeStruct((videos, tok_part, width), bf16),
         in_specs=[smem, vmem] + [vmem] * len(w_parts),
         out_specs=vmem,
+        scratch_shapes=[pltpu.VMEM((2 * d, width), bf16)] if paired else [],
         compiler_params=params,
         name="mix",
     )(ids, arrived, *w_parts)

time: 80.8 us -> 75.3 us (0.932)
  the two profiles are of different devices: /device:TPU:0 before, /device:TPU:6 now
where the time goes in v4:
time: 75.3 us; the launch traced here: 75 us
  waiting for transfers between devices  23.8 us (32%)
  blocking collectives  17.6 us (23%)
  Pallas kernels  16.3 us (22%)
  starting transfers between devices  12.5 us (17%)
  local copies, waits for them, and re-layouts  3.93 us (5%)
  between operations  0.82 us (1%)
    ppermute x17, waiting for transfers between devices, swapped(): lax.ppermute(array, axis, [(i, i ^ flip) for i in range(lax.axis_size(axi...  23.8 us
    ppermute x17, starting transfers between devices, swapped(): lax.ppermute(array, axis, [(i, i ^ flip) for i in range(lax.axis_size(axi...  12.5 us
    pallas_call x1, Pallas kernels, on_device(): pl.pallas_call(partial(chain_kernel, seq_count), out_shape=jax.ShapeDtype...  11.5 us
    all_gather x1, blocking collectives, on_device(): operands = [lax.all_gather(kv, 'seq'), q_early, q_late, ln_gain, ln_bias]  9.33 us
    all_to_all x1, blocking collectives, on_device(): lax.all_to_all(heads, 'row', split_axis=0, concat_axis=0, tiled=True)  8.28 us
    unnamed x23, local copies, waits for them, and re-layouts  3.03 us
    pallas_call x2, Pallas kernels, project(): pl.pallas_call(partial(project_kernel, count, pieces, first), out_shape=o...  2.81 us
    pallas_call x1, Pallas kernels, on_device(): pl.pallas_call(partial(out_kernel, len(w_parts)), out_shape=jax.ShapeDtyp...  2.01 us
  transfers between devices with their start and end apart: 17, of which 7 were waited for; matrix products, arithmetic and copies ran while one was open for 0% of the time, Pallas kernels for 19%

profile of v4, /device:TPU:6, one launch (start us, length us, event | category | flops | bytes accessed | tf_op | source)
XLA Modules:
  0.0 75.0 jit_solution(9875941683312225731)
XLA Ops:
  0.0 0.9 %constant_dynamic-slice_fusion = bf16[16,3072]{1,0:T(8,128)(2,1)S(1)} fusion(bf16[64,3072]{1,0:T(8,128)(2,1)} %refs_0_.3, s32[]{:T(128)S(6)} %select_n.16), kind=kLoop, calls=%fused_computation.5 | loop fusion | bytes 196612 | tf_op jit(solution)/shard_map/dynamic_slice | solution.py:355
  0.9 3.6 %collective-permute-start.4 = (bf16[16,3072]{1,0:T(8,128)(2,1)S(1)}, bf16[16,3072]{1,0:T(8,128)(2,1)S(1)}, u32[]{:S(2)}, u32[]{:S(2)}) collective-permute-start(bf16[16,3072]{1,0:T(8,128)(2,1)S(1)} %constant_dynamic-slice_fusion), channel_id=1, source_target_pairs={{0,6},{1,7},{2,4},{3,5},{4,2},{5,3},{6,0},{7,1},{8,14},{9,15},{10,... | collective-permute-start | bytes 294920 | tf_op jit(solution)/shard_map/ppermute | solution.py:296
  4.5 0.8 %collective-permute-start = (bf16[2,32,3072]{2,1,0:T(8,128)(2,1)}, bf16[2,32,3072]{2,1,0:T(8,128)(2,1)S(1)}, u32[]{:S(2)}, u32[]{:S(2)}) collective-permute-start(bf16[2,32,3072]{2,1,0:T(8,128)(2,1)} %refs_0_.2), channel_id=1, source_target_pairs={{0,4},{1,5},{2,6},{3,7},{4,0},{5,1},{6,2},{7,3},{8,12},{9,13},{10,... | collective-permute-start | bytes 1179656 | tf_op jit(solution)/shard_map/ppermute | solution.py:296
  5.3 0.5 collective-permute-start.3
  5.8 2.6 %collective-permute-done.4 = bf16[16,3072]{1,0:T(8,128)(2,1)S(1)} collective-permute-done((bf16[16,3072]{1,0:T(8,128)(2,1)S(1)}, bf16[16,3072]{1,0:T(8,128)(2,1)S(1)}, u32[]{:S(2)}, u32[]{:S(2)}) %collective-permute-start.4) | collective-permute-done | bytes 98336 | tf_op jit(solution)/shard_map/ppermute | solution.py:296
  8.4 0.5 collective-permute-start.5
  8.9 4.1 %collective-permute-done.5 = bf16[16,3072]{1,0:T(8,128)(2,1)S(1)} collective-permute-done((bf16[16,3072]{1,0:T(8,128)(2,1)S(1)}, bf16[16,3072]{1,0:T(8,128)(2,1)S(1)}, u32[]{:S(2)}, u32[]{:S(2)}) %collective-permute-start.5) | collective-permute-done | bytes 98336 | tf_op jit(solution)/shard_map/ppermute | solution.py:296
  13.0 0.5 collective-permute-start.6
  13.5 5.2 %collective-permute-done.6 = bf16[16,3072]{1,0:T(8,128)(2,1)S(1)} collective-permute-done((bf16[16,3072]{1,0:T(8,128)(2,1)S(1)}, bf16[16,3072]{1,0:T(8,128)(2,1)S(1)}, u32[]{:S(2)}, u32[]{:S(2)}) %collective-permute-start.6) | collective-permute-done | bytes 98336 | tf_op jit(solution)/shard_map/ppermute | solution.py:296
  18.7 5.5 %collective-permute-done.7 = bf16[16,3072]{1,0:T(8,128)(2,1)S(1)} collective-permute-done((bf16[16,3072]{1,0:T(8,128)(2,1)S(1)}, bf16[16,3072]{1,0:T(8,128)(2,1)S(1)}, u32[]{:S(2)}, u32[]{:S(2)}) %collective-permute-start.7) | collective-permute-done | bytes 98336 | tf_op jit(solution)/shard_map/ppermute | solution.py:296
  24.2 0.1 collective-permute-start.8
  24.3 1.1 %collective-permute-done.refs_4_ = bf16[2,32,3072]{2,1,0:T(8,128)(2,1)S(1)} collective-permute-done((bf16[2,32,3072]{2,1,0:T(8,128)(2,1)}, bf16[2,32,3072]{2,1,0:T(8,128)(2,1)S(1)}, u32[]{:S(2)}, u32[]{:S(2)}) %collective-permute-start) | collective-permute-done | bytes 393248 | tf_op jit(solution)/shard_map/ppermute | solution.py:296
  25.4 0.6 collective-permute-done.8.refs_7_
  26.0 0.1 collective-permute-start.10
  26.1 0.4 collective-permute-start.11
  26.5 1.1 %collective-permute-start.9 = (bf16[2,32,3072]{2,1,0:T(8,128)(2,1)S(1)}, bf16[2,32,3072]{2,1,0:T(8,128)(2,1)S(1)}, u32[]{:S(2)}, u32[]{:S(2)}) collective-permute-start(bf16[2,32,3072]{2,1,0:T(8,128)(2,1)S(1)} %collective-permute-done.refs_4_), channel_id=1, source_target_pairs={{0,2},{1,3},{2,0},{3,1},{4,6},{5,7},{6,4},{7,5},{8,10},{9,11},{10,... | collective-permute-start | bytes 1179656 | tf_op jit(solution)/shard_map/ppermute | solution.py:296
  28.3 0.1 pad_add_fusion.ids_ref
  28.4 1.3 %copy-done = bf16[192,3072]{1,0:T(8,128)(2,1)S(1)} copy-done((bf16[192,3072]{1,0:T(8,128)(2,1)S(1)}, bf16[192,3072]{1,0:T(8,128)(2,1)}, u32[]{:S(2)}) %copy-start) | copy-done | bytes 1179672
  29.7 1.0 %copy-done.2 = bf16[2,32,3072]{2,1,0:T(8,128)(2,1)S(1)} copy-done((bf16[2,32,3072]{2,1,0:T(8,128)(2,1)S(1)}, bf16[2,32,3072]{2,1,0:T(8,128)(2,1)}, u32[]{:S(2)}) %copy-start.2) | copy-done | bytes 393240
  30.7 0.7 copy-done.5
  31.4 1.5 %project.1 = (bf16[432,128]{1,0:T(8,128)(2,1)S(1)}, bf16[192,128]{1,0:T(8,128)(2,1)S(1)}, bf16[256,3072]{1,0:T(8,128)(2,1)S(1)}) custom-call(s32[3]{0:T(128)S(1)} %pad_add_fusion.ids_ref, bf16[2,32,3072]{2,1,0:T(8,128)(2,1)S(1)} %copy-done.2, bf16[2,32,3072]{2,1,0:T(8,128)(2,1)S(1)} %collective-permute-done.2.refs_1_, ...), custom_call_target="tpu_custom_call" | custom-call | flops 603979776 | bytes 4000000 | tf_op jit(solution)/shard_map/project/pallas_call | solution.py:337
  32.9 4.8 %collective-permute-done.9.refs_0_ = bf16[2,32,3072]{2,1,0:T(8,128)(2,1)S(1)} collective-permute-done((bf16[2,32,3072]{2,1,0:T(8,128)(2,1)S(1)}, bf16[2,32,3072]{2,1,0:T(8,128)(2,1)S(1)}, u32[]{:S(2)}, u32[]{:S(2)}) %collective-permute-start.9) | collective-permute-done | bytes 393248 | tf_op jit(solution)/shard_map/ppermute | solution.py:296
  37.7 1.1 %collective-permute-start.14 = (bf16[64,3072]{1,0:T(8,128)(2,1)S(1)}, bf16[64,3072]{1,0:T(8,128)(2,1)S(1)}, u32[]{:S(2)}, u32[]{:S(2)}) collective-permute-start(bf16[64,3072]{1,0:T(8,128)(2,1)S(1)} %copy-done.1), channel_id=1, source_target_pairs={{0,2},{1,3},{2,0},{3,1},{4,6},{5,7},{6,4},{7,5},{8,10},{9,11},{10,... | collective-permute-start | bytes 1179656 | tf_op jit(solution)/shard_map/ppermute | solution.py:296
  38.8 3.1 %collective-permute-start.13 = (bf16[64,3072]{1,0:T(8,128)(2,1)S(1)}, bf16[64,3072]{1,0:T(8,128)(2,1)S(1)}, u32[]{:S(2)}, u32[]{:S(2)}) collective-permute-start(bf16[64,3072]{1,0:T(8,128)(2,1)S(1)} %copy-done.1), channel_id=1, source_target_pairs={{0,4},{1,5},{2,6},{3,7},{4,0},{5,1},{6,2},{7,3},{8,12},{9,13},{10,... | collective-permute-start | bytes 1179656 | tf_op jit(solution)/shard_map/ppermute | solution.py:296
  41.9 0.0 copy-start.9
  41.9 1.3 %finish.1 = (bf16[576,128]{1,0:T(8,128)(2,1)S(1)}, bf16[64,128]{1,0:T(8,128)(2,1)S(1)}) custom-call(s32[3]{0:T(128)S(1)} %pad_add_fusion.ids_ref, bf16[2,32,3072]{2,1,0:T(8,128)(2,1)S(1)} %collective-permute-done.9.refs_0_, bf16[2,32,3072]{2,1,0:T(8,128)(2,1)S(1)} %collective-permute-done.12.refs_1_, bf16[256,3072]{1,0:T(8,128)(2,1)S(1)} %get-tuple-element.26.refs_2_, ...), custom_call_target="tpu_custom_call" | custom-call | flops 201326592 | bytes 4000000 | tf_op jit(solution)/shard_map/finish/pallas_call | solution.py:337
  43.2 9.3 %all-gather = bf16[2304,128]{1,0:T(8,128)(2,1)S(1)} all-gather(bf16[576,128]{1,0:T(8,128)(2,1)S(1)} %get-tuple-element.28), channel_id=2, replica_groups=mesh['seq'=4,'row'=8] {'seq'}, dimensions={0}, use_global_device_ids=true | all-gather | bytes 737280 | tf_op jit(solution)/shard_map/all_gather | solution.py:379
  52.6 11.5 %chain.1 = bf16[256,128]{1,0:T(8,128)(2,1)S(1)} custom-call(s32[3]{0:T(128)S(1)} %pad_add_fusion.ids_ref, bf16[4,576,128]{2,1,0:T(8,128)(2,1)S(1)} %bitcast.9, bf16[192,128]{1,0:T(8,128)(2,1)S(1)} %get-tuple-element.29.refs_1_, bf16[64,128]{1,0:T(8,128)(2,1)S(1)} %get-tuple-element.30.refs_2_, f32[1,64]{1,0:T(1,128)S(1)} %copy-done.7, ...), custom_call_target="tpu_custom_call" | custom-call | tf_op jit(solution)/shard_map/chain/pallas_call | solution.py:382
  64.1 0.1 collective-permute-start.15
  64.2 0.5 collective-permute-start.16
  64.7 8.3 %all_to_all.5.heads_ref = bf16[8,32,128]{2,1,0:T(8,128)(2,1)S(1)} all-to-all(bf16[8,32,128]{2,1,0:T(8,128)(2,1)S(1)} %bitcast.10), channel_id=1, replica_groups=mesh['seq'=4,'row'=8] {'row'}, dimensions={0} | all-to-all | bytes 131072 | tf_op jit(solution)/shard_map/all_to_all | solution.py:404
  73.0 2.0 %mix.1 = bf16[2,32,3072]{2,1,0:T(8,128)(2,1)} custom-call(s32[3]{0:T(128)S(1)} %pad_add_fusion.ids_ref, bf16[8,32,128]{2,1,0:T(8,128)(2,1)S(1)} %all_to_all.5.heads_ref, bf16[64,3072]{1,0:T(8,128)(2,1)S(1)} %copy-done.1, bf16[64,3072]{1,0:T(8,128)(2,1)S(1)} %collective-permute-done.3.refs_1_, bf16[64,3072]{1,0:T(8,128)(2,1)S(1)} %collective-permute-done.14.refs_2_, ...), custom_call_target="tpu_custom_call" | custom-call | tf_op jit(solution)/shard_map/mix/pallas_call | solution.py:405
  (34 shorter events, 0.1 us)
Async XLA Ops:
  0.9 7.5 %collective-permute-start.4 = (bf16[16,3072]{1,0:T(8,128)(2,1)S(1)}, bf16[16,3072]{1,0:T(8,128)(2,1)S(1)}, u32[]{:S(2)}, u32[]{:S(2)}) collective-permute-start(bf16[16,3072]{1,0:T(8,128)(2,1)S(1)} %constant_dynamic-slice_fusion), channel_id=1, source_target_pairs={{0,6},{1,7},{2,4},{3,5},{4,2},{5,3},{6,0},{7,1},{8,14},{9,15},{10,... | collective-permute-start | bytes 294920 | tf_op jit(solution)/shard_map/ppermute | solution.py:296
  4.5 19.8 %collective-permute-start.1 = (bf16[2,32,3072]{2,1,0:T(8,128)(2,1)}, bf16[2,32,3072]{2,1,0:T(8,128)(2,1)S(1)}, u32[]{:S(2)}, u32[]{:S(2)}) collective-permute-start(bf16[2,32,3072]{2,1,0:T(8,128)(2,1)} %refs_0_.2), channel_id=1, source_target_pairs={{0,2},{1,3},{2,0},{3,1},{4,6},{5,7},{6,4},{7,5},{8,10},{9,11},{10,... | collective-permute-start | bytes 1179656 | tf_op jit(solution)/shard_map/ppermute | solution.py:296
  4.5 20.9 %collective-permute-start = (bf16[2,32,3072]{2,1,0:T(8,128)(2,1)}, bf16[2,32,3072]{2,1,0:T(8,128)(2,1)S(1)}, u32[]{:S(2)}, u32[]{:S(2)}) collective-permute-start(bf16[2,32,3072]{2,1,0:T(8,128)(2,1)} %refs_0_.2), channel_id=1, source_target_pairs={{0,4},{1,5},{2,6},{3,7},{4,0},{5,1},{6,2},{7,3},{8,12},{9,13},{10,... | collective-permute-start | bytes 1179656 | tf_op jit(solution)/shard_map/ppermute | solution.py:296
  5.3 20.1 %collective-permute-start.2 = (bf16[2,32,3072]{2,1,0:T(8,128)(2,1)}, bf16[2,32,3072]{2,1,0:T(8,128)(2,1)S(1)}, u32[]{:S(2)}, u32[]{:S(2)}) collective-permute-start(bf16[2,32,3072]{2,1,0:T(8,128)(2,1)} %refs_0_.2), channel_id=1, source_target_pairs={{0,1},{1,0},{2,3},{3,2},{4,5},{5,4},{6,7},{7,6},{8,9},{9,8},{10,11... | collective-permute-start | bytes 1179656 | tf_op jit(solution)/shard_map/ppermute | solution.py:296
  5.3 20.1 %collective-permute-start.3 = (bf16[64,3072]{1,0:T(8,128)(2,1)}, bf16[64,3072]{1,0:T(8,128)(2,1)S(1)}, u32[]{:S(2)}, u32[]{:S(2)}) collective-permute-start(bf16[64,3072]{1,0:T(8,128)(2,1)} %refs_0_.3), channel_id=1, source_target_pairs={{0,1},{1,0},{2,3},{3,2},{4,5},{5,4},{6,7},{7,6},{8,9},{9,8},{10,11... | collective-permute-start | bytes 1179656 | tf_op jit(solution)/shard_map/ppermute | solution.py:296
  8.4 4.6 %collective-permute-start.5 = (bf16[16,3072]{1,0:T(8,128)(2,1)S(1)}, bf16[16,3072]{1,0:T(8,128)(2,1)S(1)}, u32[]{:S(2)}, u32[]{:S(2)}) collective-permute-start(bf16[16,3072]{1,0:T(8,128)(2,1)S(1)} %collective-permute-done.4), channel_id=1, source_target_pairs={{0,8},{8,0},{16,24},{24,16},{1,9},{9,1},{17,25},{25,17},{2,10},{10... | collective-permute-start | bytes 294920 | tf_op jit(solution)/shard_map/ppermute | solution.py:296
  13.0 5.7 %collective-permute-start.6 = (bf16[16,3072]{1,0:T(8,128)(2,1)S(1)}, bf16[16,3072]{1,0:T(8,128)(2,1)S(1)}, u32[]{:S(2)}, u32[]{:S(2)}) collective-permute-start(bf16[16,3072]{1,0:T(8,128)(2,1)S(1)} %collective-permute-done.4), channel_id=1, source_target_pairs={{0,16},{8,24},{16,0},{24,8},{1,17},{9,25},{17,1},{25,9},{2,18},{10... | collective-permute-start | bytes 294920 | tf_op jit(solution)/shard_map/ppermute | solution.py:296
  18.7 5.5 %collective-permute-start.7 = (bf16[16,3072]{1,0:T(8,128)(2,1)S(1)}, bf16[16,3072]{1,0:T(8,128)(2,1)S(1)}, u32[]{:S(2)}, u32[]{:S(2)}) collective-permute-start(bf16[16,3072]{1,0:T(8,128)(2,1)S(1)} %collective-permute-done.4), channel_id=1, source_target_pairs={{0,24},{8,16},{16,8},{24,0},{1,25},{9,17},{17,9},{25,1},{2,26},{10... | collective-permute-start | bytes 294920 | tf_op jit(solution)/shard_map/ppermute | solution.py:296
  24.2 1.8 %collective-permute-start.8 = (bf16[64,3072]{1,0:T(8,128)(2,1)S(1)}, bf16[64,3072]{1,0:T(8,128)(2,1)S(1)}, u32[]{:S(2)}, u32[]{:S(2)}) collective-permute-start(bf16[64,3072]{1,0:T(8,128)(2,1)S(1)} %constant_dynamic-update-slice_fusion.refs_6_), channel_id=1, source_target_pairs={{0,1},{1,0},{2,3},{3,2},{4,5},{5,4},{6,7},{7,6},{8,9},{9,8},{10,11... | collective-permute-start | bytes 1179656 | tf_op jit(solution)/shard_map/ppermute | solution.py:296
  26.0 2.4 %collective-permute-start.10 = (bf16[2,32,3072]{2,1,0:T(8,128)(2,1)S(1)}, bf16[2,32,3072]{2,1,0:T(8,128)(2,1)S(1)}, u32[]{:S(2)}, u32[]{:S(2)}) collective-permute-start(bf16[2,32,3072]{2,1,0:T(8,128)(2,1)S(1)} %collective-permute-done.1.refs_2_), channel_id=1, source_target_pairs={{0,1},{1,0},{2,3},{3,2},{4,5},{5,4},{6,7},{7,6},{8,9},{9,8},{10,11... | collective-permute-start | bytes 1179656 | tf_op jit(solution)/shard_map/ppermute | solution.py:296
  26.1 2.3 %collective-permute-start.11 = (bf16[2,32,3072]{2,1,0:T(8,128)(2,1)S(1)}, bf16[2,32,3072]{2,1,0:T(8,128)(2,1)S(1)}, u32[]{:S(2)}, u32[]{:S(2)}) collective-permute-start(bf16[2,32,3072]{2,1,0:T(8,128)(2,1)S(1)} %collective-permute-done.refs_4_), channel_id=1, source_target_pairs={{0,1},{1,0},{2,3},{3,2},{4,5},{5,4},{6,7},{7,6},{8,9},{9,8},{10,11... | collective-permute-start | bytes 1179656 | tf_op jit(solution)/shard_map/ppermute | solution.py:296
  26.5 11.2 %collective-permute-start.9 = (bf16[2,32,3072]{2,1,0:T(8,128)(2,1)S(1)}, bf16[2,32,3072]{2,1,0:T(8,128)(2,1)S(1)}, u32[]{:S(2)}, u32[]{:S(2)}) collective-permute-start(bf16[2,32,3072]{2,1,0:T(8,128)(2,1)S(1)} %collective-permute-done.refs_4_), channel_id=1, source_target_pairs={{0,2},{1,3},{2,0},{3,1},{4,6},{5,7},{6,4},{7,5},{8,10},{9,11},{10,... | collective-permute-start | bytes 1179656 | tf_op jit(solution)/shard_map/ppermute | solution.py:296
  28.4 1.3 %copy-start = (bf16[192,3072]{1,0:T(8,128)(2,1)S(1)}, bf16[192,3072]{1,0:T(8,128)(2,1)}, u32[]{:S(2)}) copy-start(bf16[192,3072]{1,0:T(8,128)(2,1)} %refs_6_.2) | copy-start | bytes 3538948
  29.7 1.0 %copy-start.2 = (bf16[2,32,3072]{2,1,0:T(8,128)(2,1)S(1)}, bf16[2,32,3072]{2,1,0:T(8,128)(2,1)}, u32[]{:S(2)}) copy-start(bf16[2,32,3072]{2,1,0:T(8,128)(2,1)} %refs_0_.2) | copy-start | bytes 1179652
  30.7 0.7 copy-start.5
  31.4 6.3 %copy-start.1 = (bf16[64,3072]{1,0:T(8,128)(2,1)S(1)}, bf16[64,3072]{1,0:T(8,128)(2,1)}, u32[]{:S(2)}) copy-start(bf16[64,3072]{1,0:T(8,128)(2,1)} %refs_0_.3) | copy-start | bytes 1179652
  37.7 4.2 %collective-permute-start.12 = (bf16[2,32,3072]{2,1,0:T(8,128)(2,1)S(1)}, bf16[2,32,3072]{2,1,0:T(8,128)(2,1)S(1)}, u32[]{:S(2)}, u32[]{:S(2)}) collective-permute-start(bf16[2,32,3072]{2,1,0:T(8,128)(2,1)S(1)} %collective-permute-done.9.refs_0_), channel_id=1, source_target_pairs={{0,1},{1,0},{2,3},{3,2},{4,5},{5,4},{6,7},{7,6},{8,9},{9,8},{10,11... | collective-permute-start | bytes 1179656 | tf_op jit(solution)/shard_map/ppermute | solution.py:296
  37.7 26.5 %collective-permute-start.14 = (bf16[64,3072]{1,0:T(8,128)(2,1)S(1)}, bf16[64,3072]{1,0:T(8,128)(2,1)S(1)}, u32[]{:S(2)}, u32[]{:S(2)}) collective-permute-start(bf16[64,3072]{1,0:T(8,128)(2,1)S(1)} %copy-done.1), channel_id=1, source_target_pairs={{0,2},{1,3},{2,0},{3,1},{4,6},{5,7},{6,4},{7,5},{8,10},{9,11},{10,... | collective-permute-start | bytes 1179656 | tf_op jit(solution)/shard_map/ppermute | solution.py:296
  38.8 25.3 %collective-permute-start.13 = (bf16[64,3072]{1,0:T(8,128)(2,1)S(1)}, bf16[64,3072]{1,0:T(8,128)(2,1)S(1)}, u32[]{:S(2)}, u32[]{:S(2)}) collective-permute-start(bf16[64,3072]{1,0:T(8,128)(2,1)S(1)} %copy-done.1), channel_id=1, source_target_pairs={{0,4},{1,5},{2,6},{3,7},{4,0},{5,1},{6,2},{7,3},{8,12},{9,13},{10,... | collective-permute-start | bytes 1179656 | tf_op jit(solution)/shard_map/ppermute | solution.py:296
  41.9 10.7 %copy-start.3 = (f32[1,64,256]{2,1,0:T(8,128)S(1)}, f32[1,64,256]{2,1,0:T(8,128)}, u32[]{:S(2)}) copy-start(f32[1,64,256]{2,1,0:T(8,128)} %refs_5_.1) | copy-start | bytes 196612
  41.9 10.7 %copy-start.4 = (f32[1,256,64]{1,2,0:T(8,128)S(1)}, f32[1,256,64]{1,2,0:T(8,128)}, u32[]{:S(2)}) copy-start(f32[1,256,64]{1,2,0:T(8,128)} %param.18) | copy-start | bytes 196612
  41.9 10.7 %copy-start.6 = (f32[1,256]{1,0:T(1,128)S(1)}, f32[1,256]{1,0:T(1,128)}, u32[]{:S(2)}) copy-start(f32[1,256]{1,0:T(1,128)} %refs_6_.3) | copy-start | bytes 3076
  41.9 10.7 %copy-start.7 = (f32[1,64]{1,0:T(1,128)S(1)}, f32[1,64]{1,0:T(1,128)}, u32[]{:S(2)}) copy-start(f32[1,64]{1,0:T(1,128)} %refs_3_.1) | copy-start | bytes 772
  41.9 10.7 %copy-start.8 = (f32[1,64]{1,0:T(1,128)S(1)}, f32[1,64]{1,0:T(1,128)}, u32[]{:S(2)}) copy-start(f32[1,64]{1,0:T(1,128)} %refs_4_.1) | copy-start | bytes 772
  41.9 10.7 %copy-start.9 = (f32[1,64]{1,0:T(1,128)S(1)}, f32[1,64]{1,0:T(1,128)}, u32[]{:S(2)}) copy-start(f32[1,64]{1,0:T(1,128)} %refs_8_.1) | copy-start | bytes 772
  64.1 8.9 %collective-permute-start.15 = (bf16[64,3072]{1,0:T(8,128)(2,1)S(1)}, bf16[64,3072]{1,0:T(8,128)(2,1)S(1)}, u32[]{:S(2)}, u32[]{:S(2)}) collective-permute-start(bf16[64,3072]{1,0:T(8,128)(2,1)S(1)} %collective-permute-done.14.refs_2_), channel_id=1, source_target_pairs={{0,1},{1,0},{2,3},{3,2},{4,5},{5,4},{6,7},{7,6},{8,9},{9,8},{10,11... | collective-permute-start | bytes 1179656 | tf_op jit(solution)/shard_map/ppermute | solution.py:296
  64.2 8.8 %collective-permute-start.16 = (bf16[64,3072]{1,0:T(8,128)(2,1)S(1)}, bf16[64,3072]{1,0:T(8,128)(2,1)S(1)}, u32[]{:S(2)}, u32[]{:S(2)}) collective-permute-start(bf16[64,3072]{1,0:T(8,128)(2,1)S(1)} %collective-permute-done.13.refs_4_), channel_id=1, source_target_pairs={{0,1},{1,0},{2,3},{3,2},{4,5},{5,4},{6,7},{7,6},{8,9},{9,8},{10,11... | collective-permute-start | bytes 1179656 | tf_op jit(solution)/shard_map/ppermute | solution.py:296

commit v5 on v4

--- a/solution.py
+++ b/solution.py
@@ -263,8 +263,7 @@
 
 
 def out_kernel(count, ids_ref, heads_ref, *refs):
-    w_refs, refs = refs[:count], refs[count:]
-    out_ref = refs[0]
+    w_refs, out_ref, w_s = refs[:count], refs[count], refs[-1]
     heads, rows, both = heads_ref.shape
     d = both // 2
     low = lane_low((rows, both))
@@ -280,7 +279,6 @@
     )
     weights = [w_ref[...] for w_ref in w_refs]
     if count > 1:
-        w_s = refs[1]
         share = d // 4
         for i in range(2):
             for flip in range(4):
@@ -317,7 +315,7 @@
     both = 2 * d
     row_count, seq_count = lax.axis_size("row"), lax.axis_size("seq")
     minis = tok_part * row_count // MINI
-    paired = row_count == 8 and minis == 4 and seq_count == 4 and d == 64
+    paired = row_count == 8 and minis == 4 and seq_count == 4
     vmem = pl.BlockSpec(memory_space=pltpu.VMEM)
     smem = pl.BlockSpec(memory_space=pltpu.SMEM)
     params = pltpu.CompilerParams(vmem_limit_bytes=VMEM_LIMIT)
@@ -352,17 +350,16 @@
         place = lax.axis_index("seq")
         far, near = swapped(tokens, 4), swapped(tokens, 2)
         own, w_own = swapped(tokens, 1), swapped(w_out, 1)
-        w_share = swapped(lax.dynamic_slice_in_dim(w_out, place * share, share, 0), 6)
+        w_share = lax.dynamic_slice_in_dim(w_out, place * share, share, 0)
+        w_share = swapped(w_share, 6)
+        far, near, own, w_own, w_share = lax.optimization_barrier((far, near, own, w_own, w_share))
+        last = swapped(far, 2)
+        near_other, far_other = swapped(near, 1), swapped(far, 1)
         w_end = [w_share] + [swapped(w_share, flip, "seq") for flip in range(1, seq_count)]
+        early = [tokens, own, near, near_other, far, far_other]
+        kv_early, q_early, stack = project(3, 2, True, early, (w_qkv, w_rate))
+        last, kv_early, *w_end = lax.optimization_barrier((last, kv_early, *w_end))
         w_end = jnp.concatenate(w_end, axis=0)
-        w_end_other = swapped(w_end, 1)
-        far, near, own, w_own, w_end, w_end_other = lax.optimization_barrier(
-            (far, near, own, w_own, w_end, w_end_other)
-        )
-        last = swapped(far, 2)
-        early = [tokens, own, near, swapped(near, 1), far, swapped(far, 1)]
-        kv_early, q_early, stack = project(3, 2, True, early, (w_qkv, w_rate))
-        last, kv_early = lax.optimization_barrier((last, kv_early))
         late = [last, swapped(last, 1)]
         w_after, _ = lax.optimization_barrier((w_out, last))
         w_far, w_near = swapped(w_after, 4), swapped(w_after, 2)
@@ -397,9 +394,8 @@
         name="chain",
     )(ids, *operands)
     if paired:
-        w_far, w_near, _ = lax.optimization_barrier((w_far, w_near, heads))
-        w_parts = [w_out, w_own, w_near, swapped(w_near, 1), w_far, swapped(w_far, 1)]
-        w_parts += [w_end, w_end_other]
+        w_near, w_far, w_end, _ = lax.optimization_barrier((w_near, w_far, w_end, heads))
+        w_parts = [w_out, w_own] + [x for w in (w_near, w_far, w_end) for x in (w, swapped(w, 1))]
     heads = heads.reshape(row_count, tok_part, both)
     arrived = lax.all_to_all(heads, "row", split_axis=0, concat_axis=0, tiled=True)
     return pl.pallas_call(
@@ -407,7 +403,7 @@
         out_shape=jax.ShapeDtypeStruct((videos, tok_part, width), bf16),
         in_specs=[smem, vmem] + [vmem] * len(w_parts),
         out_specs=vmem,
-        scratch_shapes=[pltpu.VMEM((2 * d, width), bf16)] if paired else [],
+        scratch_shapes=[pltpu.VMEM((2 * d, width), bf16)],
         compiler_params=params,
         name="mix",
     )(ids, arrived, *w_parts)

time: 75.3 us -> 73.3 us (0.973)
  waiting for transfers between devices: 23.8 us -> 18.6 us
  starting transfers between devices: 12.5 us -> 15 us
    ppermute x17, waiting for transfers between devices: 23.8 us -> 18.6 us  [swapped(): lax.ppermute(array, axis, [(i, i ^ flip) for i in range(lax.axis_size(axi...]
    ppermute x17, starting transfers between devices: 12.5 us -> 15 us  [swapped(): lax.ppermute(array, axis, [(i, i ^ flip) for i in range(lax.axis_size(axi...]
    unnamed x23 -> x20, local copies, waits for them, and re-layouts: 3.03 us -> 3.01 us
  transfers between devices with their start and end apart: 17 -> 17, of which waited for: 7 -> 2; matrix products, arithmetic and copies ran while one was open for 0% -> 1% of each run, Pallas kernels for 19% -> 20%
where the time goes in v5:
time: 73.3 us; the launch traced here: 73 us
  waiting for transfers between devices  18.6 us (25%)
  blocking collectives  18.1 us (25%)
  Pallas kernels  16.3 us (22%)
  starting transfers between devices  15 us (20%)
  local copies, waits for them, and re-layouts  3.91 us (5%)
  between operations  0.88 us (1%)
    ppermute x17, waiting for transfers between devices, swapped(): lax.ppermute(array, axis, [(i, i ^ flip) for i in range(lax.axis_size(axi...  18.6 us
    ppermute x17, starting transfers between devices, swapped(): lax.ppermute(array, axis, [(i, i ^ flip) for i in range(lax.axis_size(axi...  15 us
    pallas_call x1, Pallas kernels, on_device(): pl.pallas_call(partial(chain_kernel, seq_count), out_shape=jax.ShapeDtype...  11.5 us
    all_gather x1, blocking collectives, on_device(): operands = [lax.all_gather(kv, 'seq'), q_early, q_late, ln_gain, ln_bias]  9.33 us
    all_to_all x1, blocking collectives, on_device(): lax.all_to_all(heads, 'row', split_axis=0, concat_axis=0, tiled=True)  8.77 us
    unnamed x20, local copies, waits for them, and re-layouts  3.01 us
    pallas_call x2, Pallas kernels, project(): pl.pallas_call(partial(project_kernel, count, pieces, first), out_shape=o...  2.81 us
    pallas_call x1, Pallas kernels, on_device(): pl.pallas_call(partial(out_kernel, len(w_parts)), out_shape=jax.ShapeDtyp...  2.01 us
  transfers between devices with their start and end apart: 17, of which 2 were waited for; matrix products, arithmetic and copies ran while one was open for 1% of the time, Pallas kernels for 20%

profile of v5, /device:TPU:6, one launch (start us, length us, event | category | flops | bytes accessed | tf_op | source)
XLA Modules:
  0.0 73.0 jit_solution(14728093324080906678)
XLA Ops:
  0.0 2.6 %collective-permute-start = (bf16[2,32,3072]{2,1,0:T(8,128)(2,1)}, bf16[2,32,3072]{2,1,0:T(8,128)(2,1)S(1)}, u32[]{:S(2)}, u32[]{:S(2)}) collective-permute-start(bf16[2,32,3072]{2,1,0:T(8,128)(2,1)} %refs_0_.2), channel_id=1, source_target_pairs={{0,4},{1,5},{2,6},{3,7},{4,0},{5,1},{6,2},{7,3},{8,12},{9,13},{10,... | collective-permute-start | bytes 1179656 | tf_op jit(solution)/shard_map/ppermute | solution.py:294
  2.6 1.6 %collective-permute-start.1 = (bf16[2,32,3072]{2,1,0:T(8,128)(2,1)}, bf16[2,32,3072]{2,1,0:T(8,128)(2,1)S(1)}, u32[]{:S(2)}, u32[]{:S(2)}) collective-permute-start(bf16[2,32,3072]{2,1,0:T(8,128)(2,1)} %refs_0_.2), channel_id=1, source_target_pairs={{0,2},{1,3},{2,0},{3,1},{4,6},{5,7},{6,4},{7,5},{8,10},{9,11},{10,... | collective-permute-start | bytes 1179656 | tf_op jit(solution)/shard_map/ppermute | solution.py:294
  4.2 0.5 collective-permute-start.3
  4.7 0.9 %constant_dynamic-slice_fusion = bf16[16,3072]{1,0:T(8,128)(2,1)S(1)} fusion(bf16[64,3072]{1,0:T(8,128)(2,1)} %refs_0_.3, s32[]{:T(128)S(6)} %select_n.16), kind=kLoop, calls=%fused_computation.2 | loop fusion | bytes 196612 | tf_op jit(solution)/shard_map/dynamic_slice | solution.py:353
  5.6 0.2 collective-permute-start.4
  5.8 17.9 %collective-permute-done.4 = bf16[16,3072]{1,0:T(8,128)(2,1)S(1)} collective-permute-done((bf16[16,3072]{1,0:T(8,128)(2,1)S(1)}, bf16[16,3072]{1,0:T(8,128)(2,1)S(1)}, u32[]{:S(2)}, u32[]{:S(2)}) %collective-permute-start.4) | collective-permute-done | bytes 98336 | tf_op jit(solution)/shard_map/ppermute | solution.py:294
  23.7 0.1 collective-permute-start.7
  23.8 0.5 collective-permute-start.6
  24.3 1.6 %collective-permute-start.5 = (bf16[2,32,3072]{2,1,0:T(8,128)(2,1)S(1)}, bf16[2,32,3072]{2,1,0:T(8,128)(2,1)S(1)}, u32[]{:S(2)}, u32[]{:S(2)}) collective-permute-start(bf16[2,32,3072]{2,1,0:T(8,128)(2,1)S(1)} %collective-permute-done.refs_4_), channel_id=1, source_target_pairs={{0,2},{1,3},{2,0},{3,1},{4,6},{5,7},{6,4},{7,5},{8,10},{9,11},{10,... | collective-permute-start | bytes 1179656 | tf_op jit(solution)/shard_map/ppermute | solution.py:294
  25.9 0.5 collective-permute-start.10
  26.4 1.5 %collective-permute-start.8 = (bf16[16,3072]{1,0:T(8,128)(2,1)S(1)}, bf16[16,3072]{1,0:T(8,128)(2,1)S(1)}, u32[]{:S(2)}, u32[]{:S(2)}) collective-permute-start(bf16[16,3072]{1,0:T(8,128)(2,1)S(1)} %collective-permute-done.4), channel_id=1, source_target_pairs={{0,8},{8,0},{16,24},{24,16},{1,9},{9,1},{17,25},{25,17},{2,10},{10... | collective-permute-start | bytes 294920 | tf_op jit(solution)/shard_map/ppermute | solution.py:294
  27.8 1.5 %collective-permute-start.9 = (bf16[16,3072]{1,0:T(8,128)(2,1)S(1)}, bf16[16,3072]{1,0:T(8,128)(2,1)S(1)}, u32[]{:S(2)}, u32[]{:S(2)}) collective-permute-start(bf16[16,3072]{1,0:T(8,128)(2,1)S(1)} %collective-permute-done.4), channel_id=1, source_target_pairs={{0,16},{8,24},{16,0},{24,8},{1,17},{9,25},{17,1},{25,9},{2,18},{10... | collective-permute-start | bytes 294920 | tf_op jit(solution)/shard_map/ppermute | solution.py:294
  29.4 0.1 pad_add_fusion.ids_ref
  30.1 1.3 %copy-done = bf16[192,3072]{1,0:T(8,128)(2,1)S(1)} copy-done((bf16[192,3072]{1,0:T(8,128)(2,1)S(1)}, bf16[192,3072]{1,0:T(8,128)(2,1)}, u32[]{:S(2)}) %copy-start) | copy-done | bytes 1179672
  31.4 1.0 %copy-done.2 = bf16[2,32,3072]{2,1,0:T(8,128)(2,1)S(1)} copy-done((bf16[2,32,3072]{2,1,0:T(8,128)(2,1)S(1)}, bf16[2,32,3072]{2,1,0:T(8,128)(2,1)}, u32[]{:S(2)}) %copy-start.2) | copy-done | bytes 393240
  32.4 0.7 copy-done.5
  33.1 1.5 %project.1 = (bf16[432,128]{1,0:T(8,128)(2,1)S(1)}, bf16[192,128]{1,0:T(8,128)(2,1)S(1)}, bf16[256,3072]{1,0:T(8,128)(2,1)S(1)}) custom-call(s32[3]{0:T(128)S(1)} %pad_add_fusion.ids_ref, bf16[2,32,3072]{2,1,0:T(8,128)(2,1)S(1)} %copy-done.2, bf16[2,32,3072]{2,1,0:T(8,128)(2,1)S(1)} %collective-permute-done.2.refs_1_, ...), custom_call_target="tpu_custom_call" | custom-call | flops 603979776 | bytes 4000000 | tf_op jit(solution)/shard_map/project/pallas_call | solution.py:335
  34.6 0.7 %collective-permute-done.5.refs_0_ = bf16[2,32,3072]{2,1,0:T(8,128)(2,1)S(1)} collective-permute-done((bf16[2,32,3072]{2,1,0:T(8,128)(2,1)S(1)}, bf16[2,32,3072]{2,1,0:T(8,128)(2,1)S(1)}, u32[]{:S(2)}, u32[]{:S(2)}) %collective-permute-start.5) | collective-permute-done | bytes 393248 | tf_op jit(solution)/shard_map/ppermute | solution.py:294
  35.4 1.6 %collective-permute-start.12 = (bf16[64,3072]{1,0:T(8,128)(2,1)S(1)}, bf16[64,3072]{1,0:T(8,128)(2,1)S(1)}, u32[]{:S(2)}, u32[]{:S(2)}) collective-permute-start(bf16[64,3072]{1,0:T(8,128)(2,1)S(1)} %copy-done.1), channel_id=1, source_target_pairs={{0,2},{1,3},{2,0},{3,1},{4,6},{5,7},{6,4},{7,5},{8,10},{9,11},{10,... | collective-permute-start | bytes 1179656 | tf_op jit(solution)/shard_map/ppermute | solution.py:294
  37.0 2.2 %collective-permute-start.13 = (bf16[64,3072]{1,0:T(8,128)(2,1)S(1)}, bf16[64,3072]{1,0:T(8,128)(2,1)S(1)}, u32[]{:S(2)}, u32[]{:S(2)}) collective-permute-start(bf16[64,3072]{1,0:T(8,128)(2,1)S(1)} %copy-done.1), channel_id=1, source_target_pairs={{0,4},{1,5},{2,6},{3,7},{4,0},{5,1},{6,2},{7,3},{8,12},{9,13},{10,... | collective-permute-start | bytes 1179656 | tf_op jit(solution)/shard_map/ppermute | solution.py:294
  39.2 0.0 copy-start.3
  39.2 0.0 copy-start.4
  39.3 0.0 copy-start.8
  39.3 0.0 copy-start.9
  39.3 1.3 %finish.1 = (bf16[576,128]{1,0:T(8,128)(2,1)S(1)}, bf16[64,128]{1,0:T(8,128)(2,1)S(1)}) custom-call(s32[3]{0:T(128)S(1)} %pad_add_fusion.ids_ref, bf16[2,32,3072]{2,1,0:T(8,128)(2,1)S(1)} %collective-permute-done.5.refs_0_, bf16[2,32,3072]{2,1,0:T(8,128)(2,1)S(1)} %collective-permute-done.11.refs_1_, bf16[256,3072]{1,0:T(8,128)(2,1)S(1)} %get-tuple-element.31.refs_2_, ...), custom_call_target="tpu_custom_call" | custom-call | flops 201326592 | bytes 4000000 | tf_op jit(solution)/shard_map/finish/pallas_call | solution.py:335
  40.6 9.3 %all-gather = bf16[2304,128]{1,0:T(8,128)(2,1)S(1)} all-gather(bf16[576,128]{1,0:T(8,128)(2,1)S(1)} %get-tuple-element.33), channel_id=2, replica_groups=mesh['seq'=4,'row'=8] {'seq'}, dimensions={0}, use_global_device_ids=true | all-gather | bytes 737280 | tf_op jit(solution)/shard_map/all_gather | solution.py:376
  50.0 11.5 %chain.1 = bf16[256,128]{1,0:T(8,128)(2,1)S(1)} custom-call(s32[3]{0:T(128)S(1)} %pad_add_fusion.ids_ref, bf16[4,576,128]{2,1,0:T(8,128)(2,1)S(1)} %bitcast.9, bf16[192,128]{1,0:T(8,128)(2,1)S(1)} %get-tuple-element.34.refs_1_, bf16[64,128]{1,0:T(8,128)(2,1)S(1)} %get-tuple-element.35.refs_2_, f32[1,64]{1,0:T(1,128)S(1)} %copy-done.7, ...), custom_call_target="tpu_custom_call" | custom-call | tf_op jit(solution)/shard_map/chain/pallas_call | solution.py:379
  61.5 0.1 collective-permute-start.14
  61.6 0.5 collective-permute-start.15
  62.1 0.1 collective-permute-start.16
  62.2 8.8 %all_to_all.5.heads_ref = bf16[8,32,128]{2,1,0:T(8,128)(2,1)S(1)} all-to-all(bf16[8,32,128]{2,1,0:T(8,128)(2,1)S(1)} %bitcast.10), channel_id=1, replica_groups=mesh['seq'=4,'row'=8] {'row'}, dimensions={0} | all-to-all | bytes 131072 | tf_op jit(solution)/shard_map/all_to_all | solution.py:400
  71.0 2.0 %mix.1 = bf16[2,32,3072]{2,1,0:T(8,128)(2,1)} custom-call(s32[3]{0:T(128)S(1)} %pad_add_fusion.ids_ref, bf16[8,32,128]{2,1,0:T(8,128)(2,1)S(1)} %all_to_all.5.heads_ref, bf16[64,3072]{1,0:T(8,128)(2,1)S(1)} %copy-done.1, bf16[64,3072]{1,0:T(8,128)(2,1)S(1)} %collective-permute-done.3.refs_1_, bf16[64,3072]{1,0:T(8,128)(2,1)S(1)} %collective-permute-done.12.refs_2_, ...), custom_call_target="tpu_custom_call" | custom-call | tf_op jit(solution)/shard_map/mix/pallas_call | solution.py:401
  (31 shorter events, 0.1 us)
Async XLA Ops:
  0.0 23.7 %collective-permute-start = (bf16[2,32,3072]{2,1,0:T(8,128)(2,1)}, bf16[2,32,3072]{2,1,0:T(8,128)(2,1)S(1)}, u32[]{:S(2)}, u32[]{:S(2)}) collective-permute-start(bf16[2,32,3072]{2,1,0:T(8,128)(2,1)} %refs_0_.2), channel_id=1, source_target_pairs={{0,4},{1,5},{2,6},{3,7},{4,0},{5,1},{6,2},{7,3},{8,12},{9,13},{10,... | collective-permute-start | bytes 1179656 | tf_op jit(solution)/shard_map/ppermute | solution.py:294
  2.6 21.1 %collective-permute-start.1 = (bf16[2,32,3072]{2,1,0:T(8,128)(2,1)}, bf16[2,32,3072]{2,1,0:T(8,128)(2,1)S(1)}, u32[]{:S(2)}, u32[]{:S(2)}) collective-permute-start(bf16[2,32,3072]{2,1,0:T(8,128)(2,1)} %refs_0_.2), channel_id=1, source_target_pairs={{0,2},{1,3},{2,0},{3,1},{4,6},{5,7},{6,4},{7,5},{8,10},{9,11},{10,... | collective-permute-start | bytes 1179656 | tf_op jit(solution)/shard_map/ppermute | solution.py:294
  4.2 19.5 %collective-permute-start.2 = (bf16[2,32,3072]{2,1,0:T(8,128)(2,1)}, bf16[2,32,3072]{2,1,0:T(8,128)(2,1)S(1)}, u32[]{:S(2)}, u32[]{:S(2)}) collective-permute-start(bf16[2,32,3072]{2,1,0:T(8,128)(2,1)} %refs_0_.2), channel_id=1, source_target_pairs={{0,1},{1,0},{2,3},{3,2},{4,5},{5,4},{6,7},{7,6},{8,9},{9,8},{10,11... | collective-permute-start | bytes 1179656 | tf_op jit(solution)/shard_map/ppermute | solution.py:294
  4.2 19.5 %collective-permute-start.3 = (bf16[64,3072]{1,0:T(8,128)(2,1)}, bf16[64,3072]{1,0:T(8,128)(2,1)S(1)}, u32[]{:S(2)}, u32[]{:S(2)}) collective-permute-start(bf16[64,3072]{1,0:T(8,128)(2,1)} %refs_0_.3), channel_id=1, source_target_pairs={{0,1},{1,0},{2,3},{3,2},{4,5},{5,4},{6,7},{7,6},{8,9},{9,8},{10,11... | collective-permute-start | bytes 1179656 | tf_op jit(solution)/shard_map/ppermute | solution.py:294
  5.6 18.1 %collective-permute-start.4 = (bf16[16,3072]{1,0:T(8,128)(2,1)S(1)}, bf16[16,3072]{1,0:T(8,128)(2,1)S(1)}, u32[]{:S(2)}, u32[]{:S(2)}) collective-permute-start(bf16[16,3072]{1,0:T(8,128)(2,1)S(1)} %constant_dynamic-slice_fusion), channel_id=1, source_target_pairs={{0,6},{1,7},{2,4},{3,5},{4,2},{5,3},{6,0},{7,1},{8,14},{9,15},{10,... | collective-permute-start | bytes 294920 | tf_op jit(solution)/shard_map/ppermute | solution.py:294
  23.7 4.2 %collective-permute-start.7 = (bf16[2,32,3072]{2,1,0:T(8,128)(2,1)S(1)}, bf16[2,32,3072]{2,1,0:T(8,128)(2,1)S(1)}, u32[]{:S(2)}, u32[]{:S(2)}) collective-permute-start(bf16[2,32,3072]{2,1,0:T(8,128)(2,1)S(1)} %collective-permute-done.refs_4_), channel_id=1, source_target_pairs={{0,1},{1,0},{2,3},{3,2},{4,5},{5,4},{6,7},{7,6},{8,9},{9,8},{10,11... | collective-permute-start | bytes 1179656 | tf_op jit(solution)/shard_map/ppermute | solution.py:294
  23.8 6.3 %collective-permute-start.6 = (bf16[2,32,3072]{2,1,0:T(8,128)(2,1)S(1)}, bf16[2,32,3072]{2,1,0:T(8,128)(2,1)S(1)}, u32[]{:S(2)}, u32[]{:S(2)}) collective-permute-start(bf16[2,32,3072]{2,1,0:T(8,128)(2,1)S(1)} %collective-permute-done.1.refs_2_), channel_id=1, source_target_pairs={{0,1},{1,0},{2,3},{3,2},{4,5},{5,4},{6,7},{7,6},{8,9},{9,8},{10,11... | collective-permute-start | bytes 1179656 | tf_op jit(solution)/shard_map/ppermute | solution.py:294
  24.3 11.1 %collective-permute-start.5 = (bf16[2,32,3072]{2,1,0:T(8,128)(2,1)S(1)}, bf16[2,32,3072]{2,1,0:T(8,128)(2,1)S(1)}, u32[]{:S(2)}, u32[]{:S(2)}) collective-permute-start(bf16[2,32,3072]{2,1,0:T(8,128)(2,1)S(1)} %collective-permute-done.refs_4_), channel_id=1, source_target_pairs={{0,2},{1,3},{2,0},{3,1},{4,6},{5,7},{6,4},{7,5},{8,10},{9,11},{10,... | collective-permute-start | bytes 1179656 | tf_op jit(solution)/shard_map/ppermute | solution.py:294
  25.9 8.7 %collective-permute-start.10 = (bf16[16,3072]{1,0:T(8,128)(2,1)S(1)}, bf16[16,3072]{1,0:T(8,128)(2,1)S(1)}, u32[]{:S(2)}, u32[]{:S(2)}) collective-permute-start(bf16[16,3072]{1,0:T(8,128)(2,1)S(1)} %collective-permute-done.4), channel_id=1, source_target_pairs={{0,24},{8,16},{16,8},{24,0},{1,25},{9,17},{17,9},{25,1},{2,26},{10... | collective-permute-start | bytes 294920 | tf_op jit(solution)/shard_map/ppermute | solution.py:294
  26.4 8.3 %collective-permute-start.8 = (bf16[16,3072]{1,0:T(8,128)(2,1)S(1)}, bf16[16,3072]{1,0:T(8,128)(2,1)S(1)}, u32[]{:S(2)}, u32[]{:S(2)}) collective-permute-start(bf16[16,3072]{1,0:T(8,128)(2,1)S(1)} %collective-permute-done.4), channel_id=1, source_target_pairs={{0,8},{8,0},{16,24},{24,16},{1,9},{9,1},{17,25},{25,17},{2,10},{10... | collective-permute-start | bytes 294920 | tf_op jit(solution)/shard_map/ppermute | solution.py:294
  27.8 6.8 %collective-permute-start.9 = (bf16[16,3072]{1,0:T(8,128)(2,1)S(1)}, bf16[16,3072]{1,0:T(8,128)(2,1)S(1)}, u32[]{:S(2)}, u32[]{:S(2)}) collective-permute-start(bf16[16,3072]{1,0:T(8,128)(2,1)S(1)} %collective-permute-done.4), channel_id=1, source_target_pairs={{0,16},{8,24},{16,0},{24,8},{1,17},{9,25},{17,1},{25,9},{2,18},{10... | collective-permute-start | bytes 294920 | tf_op jit(solution)/shard_map/ppermute | solution.py:294
  30.1 1.3 %copy-start = (bf16[192,3072]{1,0:T(8,128)(2,1)S(1)}, bf16[192,3072]{1,0:T(8,128)(2,1)}, u32[]{:S(2)}) copy-start(bf16[192,3072]{1,0:T(8,128)(2,1)} %refs_6_.2) | copy-start | bytes 3538948
  31.4 1.0 %copy-start.2 = (bf16[2,32,3072]{2,1,0:T(8,128)(2,1)S(1)}, bf16[2,32,3072]{2,1,0:T(8,128)(2,1)}, u32[]{:S(2)}) copy-start(bf16[2,32,3072]{2,1,0:T(8,128)(2,1)} %refs_0_.2) | copy-start | bytes 1179652
  32.4 0.7 copy-start.5
  33.1 2.3 %copy-start.1 = (bf16[64,3072]{1,0:T(8,128)(2,1)S(1)}, bf16[64,3072]{1,0:T(8,128)(2,1)}, u32[]{:S(2)}) copy-start(bf16[64,3072]{1,0:T(8,128)(2,1)} %refs_0_.3) | copy-start | bytes 1179652
  35.4 3.9 %collective-permute-start.11 = (bf16[2,32,3072]{2,1,0:T(8,128)(2,1)S(1)}, bf16[2,32,3072]{2,1,0:T(8,128)(2,1)S(1)}, u32[]{:S(2)}, u32[]{:S(2)}) collective-permute-start(bf16[2,32,3072]{2,1,0:T(8,128)(2,1)S(1)} %collective-permute-done.5.refs_0_), channel_id=1, source_target_pairs={{0,1},{1,0},{2,3},{3,2},{4,5},{5,4},{6,7},{7,6},{8,9},{9,8},{10,11... | collective-permute-start | bytes 1179656 | tf_op jit(solution)/shard_map/ppermute | solution.py:294
  35.4 26.1 %collective-permute-start.12 = (bf16[64,3072]{1,0:T(8,128)(2,1)S(1)}, bf16[64,3072]{1,0:T(8,128)(2,1)S(1)}, u32[]{:S(2)}, u32[]{:S(2)}) collective-permute-start(bf16[64,3072]{1,0:T(8,128)(2,1)S(1)} %copy-done.1), channel_id=1, source_target_pairs={{0,2},{1,3},{2,0},{3,1},{4,6},{5,7},{6,4},{7,5},{8,10},{9,11},{10,... | collective-permute-start | bytes 1179656 | tf_op jit(solution)/shard_map/ppermute | solution.py:294
  37.0 24.5 %collective-permute-start.13 = (bf16[64,3072]{1,0:T(8,128)(2,1)S(1)}, bf16[64,3072]{1,0:T(8,128)(2,1)S(1)}, u32[]{:S(2)}, u32[]{:S(2)}) collective-permute-start(bf16[64,3072]{1,0:T(8,128)(2,1)S(1)} %copy-done.1), channel_id=1, source_target_pairs={{0,4},{1,5},{2,6},{3,7},{4,0},{5,1},{6,2},{7,3},{8,12},{9,13},{10,... | collective-permute-start | bytes 1179656 | tf_op jit(solution)/shard_map/ppermute | solution.py:294
  39.2 10.7 %copy-start.3 = (f32[1,64,256]{2,1,0:T(8,128)S(1)}, f32[1,64,256]{2,1,0:T(8,128)}, u32[]{:S(2)}) copy-start(f32[1,64,256]{2,1,0:T(8,128)} %refs_5_.1) | copy-start | bytes 196612
  39.2 10.7 %copy-start.4 = (f32[1,256,64]{1,2,0:T(8,128)S(1)}, f32[1,256,64]{1,2,0:T(8,128)}, u32[]{:S(2)}) copy-start(f32[1,256,64]{1,2,0:T(8,128)} %param.18) | copy-start | bytes 196612
  39.2 10.7 %copy-start.6 = (f32[1,256]{1,0:T(1,128)S(1)}, f32[1,256]{1,0:T(1,128)}, u32[]{:S(2)}) copy-start(f32[1,256]{1,0:T(1,128)} %refs_6_.3) | copy-start | bytes 3076
  39.3 10.7 %copy-start.7 = (f32[1,64]{1,0:T(1,128)S(1)}, f32[1,64]{1,0:T(1,128)}, u32[]{:S(2)}) copy-start(f32[1,64]{1,0:T(1,128)} %refs_3_.1) | copy-start | bytes 772
  39.3 10.7 %copy-start.8 = (f32[1,64]{1,0:T(1,128)S(1)}, f32[1,64]{1,0:T(1,128)}, u32[]{:S(2)}) copy-start(f32[1,64]{1,0:T(1,128)} %refs_4_.1) | copy-start | bytes 772
  39.3 10.7 %copy-start.9 = (f32[1,64]{1,0:T(1,128)S(1)}, f32[1,64]{1,0:T(1,128)}, u32[]{:S(2)}) copy-start(f32[1,64]{1,0:T(1,128)} %refs_8_.1) | copy-start | bytes 772
  61.5 9.4 %collective-permute-start.14 = (bf16[64,3072]{1,0:T(8,128)(2,1)S(1)}, bf16[64,3072]{1,0:T(8,128)(2,1)S(1)}, u32[]{:S(2)}, u32[]{:S(2)}) collective-permute-start(bf16[64,3072]{1,0:T(8,128)(2,1)S(1)} %collective-permute-done.12.refs_2_), channel_id=1, source_target_pairs={{0,1},{1,0},{2,3},{3,2},{4,5},{5,4},{6,7},{7,6},{8,9},{9,8},{10,11... | collective-permute-start | bytes 1179656 | tf_op jit(solution)/shard_map/ppermute | solution.py:294
  61.6 9.4 %collective-permute-start.15 = (bf16[64,3072]{1,0:T(8,128)(2,1)S(1)}, bf16[64,3072]{1,0:T(8,128)(2,1)S(1)}, u32[]{:S(2)}, u32[]{:S(2)}) collective-permute-start(bf16[64,3072]{1,0:T(8,128)(2,1)S(1)} %collective-permute-done.13.refs_4_), channel_id=1, source_target_pairs={{0,1},{1,0},{2,3},{3,2},{4,5},{5,4},{6,7},{7,6},{8,9},{9,8},{10,11... | collective-permute-start | bytes 1179656 | tf_op jit(solution)/shard_map/ppermute | solution.py:294
  62.1 8.9 %collective-permute-start.16 = (bf16[64,3072]{1,0:T(8,128)(2,1)S(1)}, bf16[64,3072]{1,0:T(8,128)(2,1)S(1)}, u32[]{:S(2)}, u32[]{:S(2)}) collective-permute-start(bf16[64,3072]{1,0:T(8,128)(2,1)S(1)} %pad_maximum_fusion.refs_6_), channel_id=1, source_target_pairs={{0,1},{1,0},{2,3},{3,2},{4,5},{5,4},{6,7},{7,6},{8,9},{9,8},{10,11... | collective-permute-start | bytes 1179656 | tf_op jit(solution)/shard_map/ppermute | solution.py:294

commit v6 on v5

--- a/solution.py
+++ b/solution.py
@@ -26,6 +26,11 @@
     )
 
 
+def halved(x):
+    high = x.astype(bf16)
+    return high, (x - high.astype(f32)).astype(bf16)
+
+
 def lane_low(shape):
     return lax.broadcasted_iota(jnp.int32, shape, len(shape) - 1) < shape[-1] // 2
 
@@ -42,6 +47,7 @@
 
 
 PACK = 16
+MIX_CHUNKS = 4
 
 
 def project_kernel(count, pieces, first, ids_ref, *refs):
@@ -159,16 +165,17 @@
 
     def step(j, m, state, z1, kb, key_cat, nxt, query):
         w1, b1, w2, b2 = state
-        w1h, w2h = w1.astype(bf16), w2.astype(bf16)
+        w1h, (w2h, w2l) = w1.astype(bf16), halved(w2)
         value_cat = kv_s[j, m, pl.ds(mini, mini), :].astype(f32)
         rate_rows = kv_s[j, m, pl.ds(both, PACK), :].astype(f32)
         e = halves(pick * (rate_rows[:1] + rate_rows[1:2]))
         u = gain * (bias - (value_cat - key_cat.astype(f32)))
         u_mean = halves(u) * (1.0 / d)
 
-        x2h, slope = gelu_both(z1)
-        x2h = x2h.astype(bf16)
-        z = lane_cat(dot(x2h, w2h)) + b2
+        x2, slope = gelu_both(z1)
+        x2h, x2l = halved(x2)
+        pieces = dot(x2h, jnp.concatenate([w2h, w2l], axis=1))
+        z = lane_cat(pieces[:, :both] + (pieces[:, both:] + dot(x2l, w2h))) + b2
         scaled = gain_sq * z
         rs = lax.rsqrt(halves(z * z) * (1.0 / d) + ln_eps)
         mean_g = rs * halves(scaled) * (1.0 / d) + u_mean
@@ -180,7 +187,7 @@
         h1h = (d1 * slope).astype(bf16)
         h1 = h1h.astype(f32)
         h2 = spread(alpha) * ((gain_sq - spread(mean_gn)) * (spread(rs) * z) + (u - spread(mean_g)))
-        h2h = blocks(h2).astype(bf16)
+        h2h, h2l = (blocks(x) for x in halved(h2))
 
         z1_next, kb_next, result = None, None, None
         streams = [] if nxt is None else [blocks(nxt)]
@@ -216,7 +223,9 @@
             ],
             axis=0,
         )
-        w2 = w2 - dot(x2h, h2h, TN)
+        w2 = w2 - dot(
+            jnp.concatenate([x2h, x2l, x2h], axis=0), jnp.concatenate([h2h, h2h, h2l], axis=0), TN
+        )
         b2 = b2 - jnp.sum(h2, axis=0, keepdims=True)
         return (w1, b1, w2, b2), z1_next, kb_next, result
 
@@ -263,7 +272,7 @@
 
 
 def out_kernel(count, ids_ref, heads_ref, *refs):
-    w_refs, out_ref, w_s = refs[:count], refs[count], refs[-1]
+    w_refs, (out_ref, w_s, out_s, sems) = refs[:count], refs[count:]
     heads, rows, both = heads_ref.shape
     d = both // 2
     low = lane_low((rows, both))
@@ -277,17 +286,23 @@
     lhs = jnp.concatenate(
         [jnp.concatenate(firsts, axis=1), jnp.concatenate(seconds, axis=1)], axis=0
     )
-    weights = [w_ref[...] for w_ref in w_refs]
-    if count > 1:
-        share = d // 4
-        for i in range(2):
-            for flip in range(4):
-                at = pl.multiple_of(i * d + (ids_ref[0] ^ flip) * share, share)
-                w_s[pl.ds(at, share), :] = w_refs[count - 2 + i][pl.ds(flip * share, share), :]
-        weights = weights[:-2] + [w_s[...]]
-    prod = dot(lhs, jnp.concatenate(weights, axis=0)).astype(bf16)
-    out_ref[0] = prod[:rows]
-    out_ref[1] = prod[rows:]
+    share = d // 4
+    for i in range(2 if count > 1 else 0):
+        for flip in range(4):
+            at = pl.multiple_of(i * d + (ids_ref[0] ^ flip) * share, share)
+            w_s[pl.ds(at, share), :] = w_refs[count - 2 + i][pl.ds(flip * share, share), :]
+    whole = w_refs if count == 1 else [*w_refs[:-2], w_s]
+    cols = out_s.shape[3]
+    copies = []
+    for c in range(out_s.shape[0]):
+        lanes = slice(c * cols, (c + 1) * cols)
+        prod = dot(lhs, jnp.concatenate([w[:, lanes] for w in whole], axis=0)).astype(bf16)
+        out_s[c, 0] = prod[:rows]
+        out_s[c, 1] = prod[rows:]
+        copies.append(pltpu.make_async_copy(out_s.at[c], out_ref.at[:, :, lanes], sems.at[c]))
+        copies[-1].start()
+    for copy in copies:
+        copy.wait()
 
 
 def swapped(array, flip, axis="row"):
@@ -402,8 +417,12 @@
         partial(out_kernel, len(w_parts)),
         out_shape=jax.ShapeDtypeStruct((videos, tok_part, width), bf16),
         in_specs=[smem, vmem] + [vmem] * len(w_parts),
-        out_specs=vmem,
-        scratch_shapes=[pltpu.VMEM((2 * d, width), bf16)],
+        out_specs=pl.BlockSpec(memory_space=pl.ANY),
+        scratch_shapes=[
+            pltpu.VMEM((2 * d, width), bf16),
+            pltpu.VMEM((MIX_CHUNKS, videos, tok_part, width // MIX_CHUNKS), bf16),
+            pltpu.SemaphoreType.DMA((MIX_CHUNKS,)),
+        ],
         compiler_params=params,
         name="mix",
     )(ids, arrived, *w_parts)

time: 73.3 us -> 74.7 us (1.019)
  Pallas kernels: 16.3 us -> 17.7 us
    pallas_call x1, Pallas kernels: 11.5 us -> 13 us  [on_device(): pl.pallas_call(partial(chain_kernel, seq_count), out_shape=jax.ShapeDtype...]
  transfers between devices with their start and end apart: 17 -> 17, of which waited for: 2 -> 2; matrix products, arithmetic and copies ran while one was open for 1% -> 1% of each run, Pallas kernels for 20% -> 21%
where the time goes in v6:
time: 74.7 us; the launch traced here: 74.4 us
  waiting for transfers between devices  18.6 us (25%)
  blocking collectives  18.1 us (24%)
  Pallas kernels  17.7 us (24%)
  starting transfers between devices  15 us (20%)
  local copies, waits for them, and re-layouts  3.91 us (5%)
  between operations  0.88 us (1%)
    ppermute x17, waiting for transfers between devices, swapped(): lax.ppermute(array, axis, [(i, i ^ flip) for i in range(lax.axis_size(axi...  18.6 us
    ppermute x17, starting transfers between devices, swapped(): lax.ppermute(array, axis, [(i, i ^ flip) for i in range(lax.axis_size(axi...  15 us
    pallas_call x1, Pallas kernels, on_device(): pl.pallas_call(partial(chain_kernel, seq_count), out_shape=jax.ShapeDtype...  13 us
    all_gather x1, blocking collectives, on_device(): operands = [lax.all_gather(kv, 'seq'), q_early, q_late, ln_gain, ln_bias]  9.33 us
    all_to_all x1, blocking collectives, on_device(): lax.all_to_all(heads, 'row', split_axis=0, concat_axis=0, tiled=True)  8.8 us
    unnamed x20, local copies, waits for them, and re-layouts  3.01 us
    pallas_call x2, Pallas kernels, project(): pl.pallas_call(partial(project_kernel, count, pieces, first), out_shape=o...  2.81 us
    pallas_call x1, Pallas kernels, on_device(): pl.pallas_call(partial(out_kernel, len(w_parts)), out_shape=jax.ShapeDtyp...  1.94 us
  transfers between devices with their start and end apart: 17, of which 2 were waited for; matrix products, arithmetic and copies ran while one was open for 1% of the time, Pallas kernels for 21%

profile of v6, /device:TPU:6, one launch (start us, length us, event | category | flops | bytes accessed | tf_op | source)
XLA Modules:
  0.0 74.4 jit_solution(16852859096754637850)
XLA Ops:
  0.0 2.6 %collective-permute-start = (bf16[2,32,3072]{2,1,0:T(8,128)(2,1)}, bf16[2,32,3072]{2,1,0:T(8,128)(2,1)S(1)}, u32[]{:S(2)}, u32[]{:S(2)}) collective-permute-start(bf16[2,32,3072]{2,1,0:T(8,128)(2,1)} %refs_0_.2), channel_id=1, source_target_pairs={{0,4},{1,5},{2,6},{3,7},{4,0},{5,1},{6,2},{7,3},{8,12},{9,13},{10,... | collective-permute-start | bytes 1179656 | tf_op jit(solution)/shard_map/ppermute | solution.py:309
  2.6 1.6 %collective-permute-start.1 = (bf16[2,32,3072]{2,1,0:T(8,128)(2,1)}, bf16[2,32,3072]{2,1,0:T(8,128)(2,1)S(1)}, u32[]{:S(2)}, u32[]{:S(2)}) collective-permute-start(bf16[2,32,3072]{2,1,0:T(8,128)(2,1)} %refs_0_.2), channel_id=1, source_target_pairs={{0,2},{1,3},{2,0},{3,1},{4,6},{5,7},{6,4},{7,5},{8,10},{9,11},{10,... | collective-permute-start | bytes 1179656 | tf_op jit(solution)/shard_map/ppermute | solution.py:309
  4.2 0.5 collective-permute-start.3
  4.7 0.9 %constant_dynamic-slice_fusion = bf16[16,3072]{1,0:T(8,128)(2,1)S(1)} fusion(bf16[64,3072]{1,0:T(8,128)(2,1)} %refs_0_.3, s32[]{:T(128)S(6)} %select_n.16), kind=kLoop, calls=%fused_computation.2 | loop fusion | bytes 196612 | tf_op jit(solution)/shard_map/dynamic_slice | solution.py:368
  5.6 0.2 collective-permute-start.4
  5.8 17.9 %collective-permute-done.4 = bf16[16,3072]{1,0:T(8,128)(2,1)S(1)} collective-permute-done((bf16[16,3072]{1,0:T(8,128)(2,1)S(1)}, bf16[16,3072]{1,0:T(8,128)(2,1)S(1)}, u32[]{:S(2)}, u32[]{:S(2)}) %collective-permute-start.4) | collective-permute-done | bytes 98336 | tf_op jit(solution)/shard_map/ppermute | solution.py:309
  23.7 0.1 collective-permute-start.7
  23.8 0.5 collective-permute-start.6
  24.3 1.6 %collective-permute-start.5 = (bf16[2,32,3072]{2,1,0:T(8,128)(2,1)S(1)}, bf16[2,32,3072]{2,1,0:T(8,128)(2,1)S(1)}, u32[]{:S(2)}, u32[]{:S(2)}) collective-permute-start(bf16[2,32,3072]{2,1,0:T(8,128)(2,1)S(1)} %collective-permute-done.refs_4_), channel_id=1, source_target_pairs={{0,2},{1,3},{2,0},{3,1},{4,6},{5,7},{6,4},{7,5},{8,10},{9,11},{10,... | collective-permute-start | bytes 1179656 | tf_op jit(solution)/shard_map/ppermute | solution.py:309
  25.9 0.5 collective-permute-start.10
  26.4 1.5 %collective-permute-start.8 = (bf16[16,3072]{1,0:T(8,128)(2,1)S(1)}, bf16[16,3072]{1,0:T(8,128)(2,1)S(1)}, u32[]{:S(2)}, u32[]{:S(2)}) collective-permute-start(bf16[16,3072]{1,0:T(8,128)(2,1)S(1)} %collective-permute-done.4), channel_id=1, source_target_pairs={{0,8},{8,0},{16,24},{24,16},{1,9},{9,1},{17,25},{25,17},{2,10},{10... | collective-permute-start | bytes 294920 | tf_op jit(solution)/shard_map/ppermute | solution.py:309
  27.8 1.5 %collective-permute-start.9 = (bf16[16,3072]{1,0:T(8,128)(2,1)S(1)}, bf16[16,3072]{1,0:T(8,128)(2,1)S(1)}, u32[]{:S(2)}, u32[]{:S(2)}) collective-permute-start(bf16[16,3072]{1,0:T(8,128)(2,1)S(1)} %collective-permute-done.4), channel_id=1, source_target_pairs={{0,16},{8,24},{16,0},{24,8},{1,17},{9,25},{17,1},{25,9},{2,18},{10... | collective-permute-start | bytes 294920 | tf_op jit(solution)/shard_map/ppermute | solution.py:309
  29.4 0.1 pad_add_fusion.ids_ref
  30.1 0.0 copy-start
  30.1 1.3 %copy-done = bf16[192,3072]{1,0:T(8,128)(2,1)S(1)} copy-done((bf16[192,3072]{1,0:T(8,128)(2,1)S(1)}, bf16[192,3072]{1,0:T(8,128)(2,1)}, u32[]{:S(2)}) %copy-start) | copy-done | bytes 1179672
  31.4 1.0 %copy-done.2 = bf16[2,32,3072]{2,1,0:T(8,128)(2,1)S(1)} copy-done((bf16[2,32,3072]{2,1,0:T(8,128)(2,1)S(1)}, bf16[2,32,3072]{2,1,0:T(8,128)(2,1)}, u32[]{:S(2)}) %copy-start.2) | copy-done | bytes 393240
  32.4 0.7 copy-done.5
  33.1 1.5 %project.1 = (bf16[432,128]{1,0:T(8,128)(2,1)S(1)}, bf16[192,128]{1,0:T(8,128)(2,1)S(1)}, bf16[256,3072]{1,0:T(8,128)(2,1)S(1)}) custom-call(s32[3]{0:T(128)S(1)} %pad_add_fusion.ids_ref, bf16[2,32,3072]{2,1,0:T(8,128)(2,1)S(1)} %copy-done.2, bf16[2,32,3072]{2,1,0:T(8,128)(2,1)S(1)} %collective-permute-done.2.refs_1_, ...), custom_call_target="tpu_custom_call" | custom-call | flops 603979776 | bytes 4000000 | tf_op jit(solution)/shard_map/project/pallas_call | solution.py:350
  34.6 0.7 collective-permute-done.5.refs_0_
  35.4 1.6 %collective-permute-start.12 = (bf16[64,3072]{1,0:T(8,128)(2,1)S(1)}, bf16[64,3072]{1,0:T(8,128)(2,1)S(1)}, u32[]{:S(2)}, u32[]{:S(2)}) collective-permute-start(bf16[64,3072]{1,0:T(8,128)(2,1)S(1)} %copy-done.1), channel_id=1, source_target_pairs={{0,2},{1,3},{2,0},{3,1},{4,6},{5,7},{6,4},{7,5},{8,10},{9,11},{10,... | collective-permute-start | bytes 1179656 | tf_op jit(solution)/shard_map/ppermute | solution.py:309
  37.0 2.2 %collective-permute-start.13 = (bf16[64,3072]{1,0:T(8,128)(2,1)S(1)}, bf16[64,3072]{1,0:T(8,128)(2,1)S(1)}, u32[]{:S(2)}, u32[]{:S(2)}) collective-permute-start(bf16[64,3072]{1,0:T(8,128)(2,1)S(1)} %copy-done.1), channel_id=1, source_target_pairs={{0,4},{1,5},{2,6},{3,7},{4,0},{5,1},{6,2},{7,3},{8,12},{9,13},{10,... | collective-permute-start | bytes 1179656 | tf_op jit(solution)/shard_map/ppermute | solution.py:309
  39.2 0.0 copy-start.6
  39.3 0.0 copy-start.7
  39.3 0.0 copy-start.9
  39.3 1.3 %finish.1 = (bf16[576,128]{1,0:T(8,128)(2,1)S(1)}, bf16[64,128]{1,0:T(8,128)(2,1)S(1)}) custom-call(s32[3]{0:T(128)S(1)} %pad_add_fusion.ids_ref, bf16[2,32,3072]{2,1,0:T(8,128)(2,1)S(1)} %collective-permute-done.5.refs_0_, bf16[2,32,3072]{2,1,0:T(8,128)(2,1)S(1)} %collective-permute-done.11.refs_1_, bf16[256,3072]{1,0:T(8,128)(2,1)S(1)} %get-tuple-element.31.refs_2_, ...), custom_call_target="tpu_custom_call" | custom-call | flops 201326592 | bytes 4000000 | tf_op jit(solution)/shard_map/finish/pallas_call | solution.py:350
  40.6 9.3 %all-gather = bf16[2304,128]{1,0:T(8,128)(2,1)S(1)} all-gather(bf16[576,128]{1,0:T(8,128)(2,1)S(1)} %get-tuple-element.33), channel_id=2, replica_groups=mesh['seq'=4,'row'=8] {'seq'}, dimensions={0}, use_global_device_ids=true | all-gather | bytes 737280 | tf_op jit(solution)/shard_map/all_gather | solution.py:391
  50.0 13.0 %chain.1 = bf16[256,128]{1,0:T(8,128)(2,1)S(1)} custom-call(s32[3]{0:T(128)S(1)} %pad_add_fusion.ids_ref, bf16[4,576,128]{2,1,0:T(8,128)(2,1)S(1)} %bitcast.9, bf16[192,128]{1,0:T(8,128)(2,1)S(1)} %get-tuple-element.34.refs_1_, bf16[64,128]{1,0:T(8,128)(2,1)S(1)} %get-tuple-element.35.refs_2_, f32[1,64]{1,0:T(1,128)S(1)} %copy-done.7, ...), custom_call_target="tpu_custom_call" | custom-call | tf_op jit(solution)/shard_map/chain/pallas_call | solution.py:394
  63.0 0.1 collective-permute-start.14
  63.1 0.5 collective-permute-start.15
  63.6 0.1 collective-permute-start.16
  63.7 8.8 %all_to_all.5.heads_ref = bf16[8,32,128]{2,1,0:T(8,128)(2,1)S(1)} all-to-all(bf16[8,32,128]{2,1,0:T(8,128)(2,1)S(1)} %bitcast.10), channel_id=1, replica_groups=mesh['seq'=4,'row'=8] {'row'}, dimensions={0} | all-to-all | bytes 131072 | tf_op jit(solution)/shard_map/all_to_all | solution.py:415
  72.5 1.9 %mix.1 = bf16[2,32,3072]{2,1,0:T(8,128)(2,1)} custom-call(s32[3]{0:T(128)S(1)} %pad_add_fusion.ids_ref, bf16[8,32,128]{2,1,0:T(8,128)(2,1)S(1)} %all_to_all.5.heads_ref, bf16[64,3072]{1,0:T(8,128)(2,1)S(1)} %copy-done.1, bf16[64,3072]{1,0:T(8,128)(2,1)S(1)} %collective-permute-done.3.refs_1_, bf16[64,3072]{1,0:T(8,128)(2,1)S(1)} %collective-permute-done.12.refs_2_, ...), custom_call_target="tpu_custom_call" | custom-call | tf_op jit(solution)/shard_map/mix/pallas_call | solution.py:416
  (31 shorter events, 0.1 us)
Async XLA Ops:
  0.0 23.7 %collective-permute-start = (bf16[2,32,3072]{2,1,0:T(8,128)(2,1)}, bf16[2,32,3072]{2,1,0:T(8,128)(2,1)S(1)}, u32[]{:S(2)}, u32[]{:S(2)}) collective-permute-start(bf16[2,32,3072]{2,1,0:T(8,128)(2,1)} %refs_0_.2), channel_id=1, source_target_pairs={{0,4},{1,5},{2,6},{3,7},{4,0},{5,1},{6,2},{7,3},{8,12},{9,13},{10,... | collective-permute-start | bytes 1179656 | tf_op jit(solution)/shard_map/ppermute | solution.py:309
  2.6 21.1 %collective-permute-start.1 = (bf16[2,32,3072]{2,1,0:T(8,128)(2,1)}, bf16[2,32,3072]{2,1,0:T(8,128)(2,1)S(1)}, u32[]{:S(2)}, u32[]{:S(2)}) collective-permute-start(bf16[2,32,3072]{2,1,0:T(8,128)(2,1)} %refs_0_.2), channel_id=1, source_target_pairs={{0,2},{1,3},{2,0},{3,1},{4,6},{5,7},{6,4},{7,5},{8,10},{9,11},{10,... | collective-permute-start | bytes 1179656 | tf_op jit(solution)/shard_map/ppermute | solution.py:309
  4.2 19.5 %collective-permute-start.2 = (bf16[2,32,3072]{2,1,0:T(8,128)(2,1)}, bf16[2,32,3072]{2,1,0:T(8,128)(2,1)S(1)}, u32[]{:S(2)}, u32[]{:S(2)}) collective-permute-start(bf16[2,32,3072]{2,1,0:T(8,128)(2,1)} %refs_0_.2), channel_id=1, source_target_pairs={{0,1},{1,0},{2,3},{3,2},{4,5},{5,4},{6,7},{7,6},{8,9},{9,8},{10,11... | collective-permute-start | bytes 1179656 | tf_op jit(solution)/shard_map/ppermute | solution.py:309
  4.2 19.5 %collective-permute-start.3 = (bf16[64,3072]{1,0:T(8,128)(2,1)}, bf16[64,3072]{1,0:T(8,128)(2,1)S(1)}, u32[]{:S(2)}, u32[]{:S(2)}) collective-permute-start(bf16[64,3072]{1,0:T(8,128)(2,1)} %refs_0_.3), channel_id=1, source_target_pairs={{0,1},{1,0},{2,3},{3,2},{4,5},{5,4},{6,7},{7,6},{8,9},{9,8},{10,11... | collective-permute-start | bytes 1179656 | tf_op jit(solution)/shard_map/ppermute | solution.py:309
  5.6 18.1 %collective-permute-start.4 = (bf16[16,3072]{1,0:T(8,128)(2,1)S(1)}, bf16[16,3072]{1,0:T(8,128)(2,1)S(1)}, u32[]{:S(2)}, u32[]{:S(2)}) collective-permute-start(bf16[16,3072]{1,0:T(8,128)(2,1)S(1)} %constant_dynamic-slice_fusion), channel_id=1, source_target_pairs={{0,6},{1,7},{2,4},{3,5},{4,2},{5,3},{6,0},{7,1},{8,14},{9,15},{10,... | collective-permute-start | bytes 294920 | tf_op jit(solution)/shard_map/ppermute | solution.py:309
  23.7 4.2 %collective-permute-start.7 = (bf16[2,32,3072]{2,1,0:T(8,128)(2,1)S(1)}, bf16[2,32,3072]{2,1,0:T(8,128)(2,1)S(1)}, u32[]{:S(2)}, u32[]{:S(2)}) collective-permute-start(bf16[2,32,3072]{2,1,0:T(8,128)(2,1)S(1)} %collective-permute-done.refs_4_), channel_id=1, source_target_pairs={{0,1},{1,0},{2,3},{3,2},{4,5},{5,4},{6,7},{7,6},{8,9},{9,8},{10,11... | collective-permute-start | bytes 1179656 | tf_op jit(solution)/shard_map/ppermute | solution.py:309
  23.8 6.3 %collective-permute-start.6 = (bf16[2,32,3072]{2,1,0:T(8,128)(2,1)S(1)}, bf16[2,32,3072]{2,1,0:T(8,128)(2,1)S(1)}, u32[]{:S(2)}, u32[]{:S(2)}) collective-permute-start(bf16[2,32,3072]{2,1,0:T(8,128)(2,1)S(1)} %collective-permute-done.1.refs_2_), channel_id=1, source_target_pairs={{0,1},{1,0},{2,3},{3,2},{4,5},{5,4},{6,7},{7,6},{8,9},{9,8},{10,11... | collective-permute-start | bytes 1179656 | tf_op jit(solution)/shard_map/ppermute | solution.py:309
  24.3 11.1 %collective-permute-start.5 = (bf16[2,32,3072]{2,1,0:T(8,128)(2,1)S(1)}, bf16[2,32,3072]{2,1,0:T(8,128)(2,1)S(1)}, u32[]{:S(2)}, u32[]{:S(2)}) collective-permute-start(bf16[2,32,3072]{2,1,0:T(8,128)(2,1)S(1)} %collective-permute-done.refs_4_), channel_id=1, source_target_pairs={{0,2},{1,3},{2,0},{3,1},{4,6},{5,7},{6,4},{7,5},{8,10},{9,11},{10,... | collective-permute-start | bytes 1179656 | tf_op jit(solution)/shard_map/ppermute | solution.py:309
  25.9 8.7 %collective-permute-start.10 = (bf16[16,3072]{1,0:T(8,128)(2,1)S(1)}, bf16[16,3072]{1,0:T(8,128)(2,1)S(1)}, u32[]{:S(2)}, u32[]{:S(2)}) collective-permute-start(bf16[16,3072]{1,0:T(8,128)(2,1)S(1)} %collective-permute-done.4), channel_id=1, source_target_pairs={{0,24},{8,16},{16,8},{24,0},{1,25},{9,17},{17,9},{25,1},{2,26},{10... | collective-permute-start | bytes 294920 | tf_op jit(solution)/shard_map/ppermute | solution.py:309
  26.4 8.3 %collective-permute-start.8 = (bf16[16,3072]{1,0:T(8,128)(2,1)S(1)}, bf16[16,3072]{1,0:T(8,128)(2,1)S(1)}, u32[]{:S(2)}, u32[]{:S(2)}) collective-permute-start(bf16[16,3072]{1,0:T(8,128)(2,1)S(1)} %collective-permute-done.4), channel_id=1, source_target_pairs={{0,8},{8,0},{16,24},{24,16},{1,9},{9,1},{17,25},{25,17},{2,10},{10... | collective-permute-start | bytes 294920 | tf_op jit(solution)/shard_map/ppermute | solution.py:309
  27.8 6.8 %collective-permute-start.9 = (bf16[16,3072]{1,0:T(8,128)(2,1)S(1)}, bf16[16,3072]{1,0:T(8,128)(2,1)S(1)}, u32[]{:S(2)}, u32[]{:S(2)}) collective-permute-start(bf16[16,3072]{1,0:T(8,128)(2,1)S(1)} %collective-permute-done.4), channel_id=1, source_target_pairs={{0,16},{8,24},{16,0},{24,8},{1,17},{9,25},{17,1},{25,9},{2,18},{10... | collective-permute-start | bytes 294920 | tf_op jit(solution)/shard_map/ppermute | solution.py:309
  30.1 1.3 %copy-start = (bf16[192,3072]{1,0:T(8,128)(2,1)S(1)}, bf16[192,3072]{1,0:T(8,128)(2,1)}, u32[]{:S(2)}) copy-start(bf16[192,3072]{1,0:T(8,128)(2,1)} %refs_6_.2) | copy-start | bytes 3538948
  31.4 1.0 %copy-start.2 = (bf16[2,32,3072]{2,1,0:T(8,128)(2,1)S(1)}, bf16[2,32,3072]{2,1,0:T(8,128)(2,1)}, u32[]{:S(2)}) copy-start(bf16[2,32,3072]{2,1,0:T(8,128)(2,1)} %refs_0_.2) | copy-start | bytes 1179652
  32.4 0.7 copy-start.5
  33.1 2.3 %copy-start.1 = (bf16[64,3072]{1,0:T(8,128)(2,1)S(1)}, bf16[64,3072]{1,0:T(8,128)(2,1)}, u32[]{:S(2)}) copy-start(bf16[64,3072]{1,0:T(8,128)(2,1)} %refs_0_.3) | copy-start | bytes 1179652
  35.4 3.9 %collective-permute-start.11 = (bf16[2,32,3072]{2,1,0:T(8,128)(2,1)S(1)}, bf16[2,32,3072]{2,1,0:T(8,128)(2,1)S(1)}, u32[]{:S(2)}, u32[]{:S(2)}) collective-permute-start(bf16[2,32,3072]{2,1,0:T(8,128)(2,1)S(1)} %collective-permute-done.5.refs_0_), channel_id=1, source_target_pairs={{0,1},{1,0},{2,3},{3,2},{4,5},{5,4},{6,7},{7,6},{8,9},{9,8},{10,11... | collective-permute-start | bytes 1179656 | tf_op jit(solution)/shard_map/ppermute | solution.py:309
  35.4 27.6 %collective-permute-start.12 = (bf16[64,3072]{1,0:T(8,128)(2,1)S(1)}, bf16[64,3072]{1,0:T(8,128)(2,1)S(1)}, u32[]{:S(2)}, u32[]{:S(2)}) collective-permute-start(bf16[64,3072]{1,0:T(8,128)(2,1)S(1)} %copy-done.1), channel_id=1, source_target_pairs={{0,2},{1,3},{2,0},{3,1},{4,6},{5,7},{6,4},{7,5},{8,10},{9,11},{10,... | collective-permute-start | bytes 1179656 | tf_op jit(solution)/shard_map/ppermute | solution.py:309
  37.0 26.0 %collective-permute-start.13 = (bf16[64,3072]{1,0:T(8,128)(2,1)S(1)}, bf16[64,3072]{1,0:T(8,128)(2,1)S(1)}, u32[]{:S(2)}, u32[]{:S(2)}) collective-permute-start(bf16[64,3072]{1,0:T(8,128)(2,1)S(1)} %copy-done.1), channel_id=1, source_target_pairs={{0,4},{1,5},{2,6},{3,7},{4,0},{5,1},{6,2},{7,3},{8,12},{9,13},{10,... | collective-permute-start | bytes 1179656 | tf_op jit(solution)/shard_map/ppermute | solution.py:309
  39.2 10.7 %copy-start.3 = (f32[1,64,256]{2,1,0:T(8,128)S(1)}, f32[1,64,256]{2,1,0:T(8,128)}, u32[]{:S(2)}) copy-start(f32[1,64,256]{2,1,0:T(8,128)} %refs_5_.1) | copy-start | bytes 196612
  39.2 10.7 %copy-start.4 = (f32[1,256,64]{1,2,0:T(8,128)S(1)}, f32[1,256,64]{1,2,0:T(8,128)}, u32[]{:S(2)}) copy-start(f32[1,256,64]{1,2,0:T(8,128)} %param.18) | copy-start | bytes 196612
  39.2 10.7 %copy-start.6 = (f32[1,256]{1,0:T(1,128)S(1)}, f32[1,256]{1,0:T(1,128)}, u32[]{:S(2)}) copy-start(f32[1,256]{1,0:T(1,128)} %refs_6_.3) | copy-start | bytes 3076
  39.3 10.7 %copy-start.7 = (f32[1,64]{1,0:T(1,128)S(1)}, f32[1,64]{1,0:T(1,128)}, u32[]{:S(2)}) copy-start(f32[1,64]{1,0:T(1,128)} %refs_3_.1) | copy-start | bytes 772
  39.3 10.7 %copy-start.8 = (f32[1,64]{1,0:T(1,128)S(1)}, f32[1,64]{1,0:T(1,128)}, u32[]{:S(2)}) copy-start(f32[1,64]{1,0:T(1,128)} %refs_4_.1) | copy-start | bytes 772
  39.3 10.7 %copy-start.9 = (f32[1,64]{1,0:T(1,128)S(1)}, f32[1,64]{1,0:T(1,128)}, u32[]{:S(2)}) copy-start(f32[1,64]{1,0:T(1,128)} %refs_8_.1) | copy-start | bytes 772
  63.0 9.5 %collective-permute-start.14 = (bf16[64,3072]{1,0:T(8,128)(2,1)S(1)}, bf16[64,3072]{1,0:T(8,128)(2,1)S(1)}, u32[]{:S(2)}, u32[]{:S(2)}) collective-permute-start(bf16[64,3072]{1,0:T(8,128)(2,1)S(1)} %collective-permute-done.12.refs_2_), channel_id=1, source_target_pairs={{0,1},{1,0},{2,3},{3,2},{4,5},{5,4},{6,7},{7,6},{8,9},{9,8},{10,11... | collective-permute-start | bytes 1179656 | tf_op jit(solution)/shard_map/ppermute | solution.py:309
  63.1 9.4 %collective-permute-start.15 = (bf16[64,3072]{1,0:T(8,128)(2,1)S(1)}, bf16[64,3072]{1,0:T(8,128)(2,1)S(1)}, u32[]{:S(2)}, u32[]{:S(2)}) collective-permute-start(bf16[64,3072]{1,0:T(8,128)(2,1)S(1)} %collective-permute-done.13.refs_4_), channel_id=1, source_target_pairs={{0,1},{1,0},{2,3},{3,2},{4,5},{5,4},{6,7},{7,6},{8,9},{9,8},{10,11... | collective-permute-start | bytes 1179656 | tf_op jit(solution)/shard_map/ppermute | solution.py:309
  63.6 8.9 %collective-permute-start.16 = (bf16[64,3072]{1,0:T(8,128)(2,1)S(1)}, bf16[64,3072]{1,0:T(8,128)(2,1)S(1)}, u32[]{:S(2)}, u32[]{:S(2)}) collective-permute-start(bf16[64,3072]{1,0:T(8,128)(2,1)S(1)} %pad_maximum_fusion.refs_6_), channel_id=1, source_target_pairs={{0,1},{1,0},{2,3},{3,2},{4,5},{5,4},{6,7},{7,6},{8,9},{9,8},{10,11... | collective-permute-start | bytes 1179656 | tf_op jit(solution)/shard_map/ppermute | solution.py:309

commit v7 on v6

--- a/solution.py
+++ b/solution.py
@@ -29,6 +29,13 @@
 def halved(x):
     high = x.astype(bf16)
     return high, (x - high.astype(f32)).astype(bf16)
+
+
+def thirds(x):
+    high = x.astype(bf16)
+    rest = x - high.astype(f32)
+    middle = rest.astype(bf16)
+    return high, middle, (rest - middle.astype(f32)).astype(bf16)
 
 
 def lane_low(shape):
@@ -165,7 +172,7 @@
 
     def step(j, m, state, z1, kb, key_cat, nxt, query):
         w1, b1, w2, b2 = state
-        w1h, (w2h, w2l) = w1.astype(bf16), halved(w2)
+        w1h, (w2h, w2m, w2l) = w1.astype(bf16), thirds(w2)
         value_cat = kv_s[j, m, pl.ds(mini, mini), :].astype(f32)
         rate_rows = kv_s[j, m, pl.ds(both, PACK), :].astype(f32)
         e = halves(pick * (rate_rows[:1] + rate_rows[1:2]))
@@ -173,9 +180,13 @@
         u_mean = halves(u) * (1.0 / d)
 
         x2, slope = gelu_both(z1)
-        x2h, x2l = halved(x2)
-        pieces = dot(x2h, jnp.concatenate([w2h, w2l], axis=1))
-        z = lane_cat(pieces[:, :both] + (pieces[:, both:] + dot(x2l, w2h))) + b2
+        x2h, x2m, x2l = thirds(x2)
+        pieces = dot(
+            jnp.concatenate([x2h, x2m, x2l], axis=0), jnp.concatenate([w2h, w2m], axis=1)
+        )
+        small = dot(x2h, w2l) + pieces[both : 2 * both, both:] + pieces[2 * both :, :both]
+        medium = pieces[:both, both:] + pieces[both : 2 * both, :both]
+        z = lane_cat(pieces[:both, :both] + (medium + small)) + b2
         scaled = gain_sq * z
         rs = lax.rsqrt(halves(z * z) * (1.0 / d) + ln_eps)
         mean_g = rs * halves(scaled) * (1.0 / d) + u_mean
@@ -187,7 +198,7 @@
         h1h = (d1 * slope).astype(bf16)
         h1 = h1h.astype(f32)
         h2 = spread(alpha) * ((gain_sq - spread(mean_gn)) * (spread(rs) * z) + (u - spread(mean_g)))
-        h2h, h2l = (blocks(x) for x in halved(h2))
+        h2h, h2m, h2l = (blocks(x) for x in thirds(h2))
 
         z1_next, kb_next, result = None, None, None
         streams = [] if nxt is None else [blocks(nxt)]
@@ -224,7 +235,9 @@
             axis=0,
         )
         w2 = w2 - dot(
-            jnp.concatenate([x2h, x2l, x2h], axis=0), jnp.concatenate([h2h, h2h, h2l], axis=0), TN
+            jnp.concatenate([x2h, x2m, x2h, x2l, x2m, x2h], axis=0),
+            jnp.concatenate([h2h, h2h, h2m, h2h, h2m, h2l], axis=0),
+            TN,
         )
         b2 = b2 - jnp.sum(h2, axis=0, keepdims=True)
         return (w1, b1, w2, b2), z1_next, kb_next, result

time: 74.7 us -> 76.4 us (1.023)
  Pallas kernels: 17.7 us -> 19.4 us
    pallas_call x1, Pallas kernels: 13 us -> 14.7 us  [on_device(): pl.pallas_call(partial(chain_kernel, seq_count), out_shape=jax.ShapeDtype...]
  transfers between devices with their start and end apart: 17 -> 17, of which waited for: 2 -> 2; matrix products, arithmetic and copies ran while one was open for 1% -> 1% of each run, Pallas kernels for 21% -> 23%
where the time goes in v7:
time: 76.4 us; the launch traced here: 76.1 us
  Pallas kernels  19.4 us (25%)
  waiting for transfers between devices  18.6 us (24%)
  blocking collectives  18.1 us (24%)
  starting transfers between devices  15 us (20%)
  local copies, waits for them, and re-layouts  3.91 us (5%)
  between operations  0.88 us (1%)
    ppermute x17, waiting for transfers between devices, swapped(): lax.ppermute(array, axis, [(i, i ^ flip) for i in range(lax.axis_size(axi...  18.6 us
    ppermute x17, starting transfers between devices, swapped(): lax.ppermute(array, axis, [(i, i ^ flip) for i in range(lax.axis_size(axi...  15 us
    pallas_call x1, Pallas kernels, on_device(): pl.pallas_call(partial(chain_kernel, seq_count), out_shape=jax.ShapeDtype...  14.7 us
    all_gather x1, blocking collectives, on_device(): operands = [lax.all_gather(kv, 'seq'), q_early, q_late, ln_gain, ln_bias]  9.33 us
    all_to_all x1, blocking collectives, on_device(): lax.all_to_all(heads, 'row', split_axis=0, concat_axis=0, tiled=True)  8.77 us
    unnamed x20, local copies, waits for them, and re-layouts  3.01 us
    pallas_call x2, Pallas kernels, project(): pl.pallas_call(partial(project_kernel, count, pieces, first), out_shape=o...  2.81 us
    pallas_call x1, Pallas kernels, on_device(): pl.pallas_call(partial(out_kernel, len(w_parts)), out_shape=jax.ShapeDtyp...  1.94 us
  transfers between devices with their start and end apart: 17, of which 2 were waited for; matrix products, arithmetic and copies ran while one was open for 1% of the time, Pallas kernels for 23%

profile of v7, /device:TPU:6, one launch (start us, length us, event | category | flops | bytes accessed | tf_op | source)
XLA Modules:
  0.0 76.1 jit_solution(6912977549095254761)
XLA Ops:
  0.0 2.6 %collective-permute-start = (bf16[2,32,3072]{2,1,0:T(8,128)(2,1)}, bf16[2,32,3072]{2,1,0:T(8,128)(2,1)S(1)}, u32[]{:S(2)}, u32[]{:S(2)}) collective-permute-start(bf16[2,32,3072]{2,1,0:T(8,128)(2,1)} %refs_0_.2), channel_id=1, source_target_pairs={{0,4},{1,5},{2,6},{3,7},{4,0},{5,1},{6,2},{7,3},{8,12},{9,13},{10,... | collective-permute-start | bytes 1179656 | tf_op jit(solution)/shard_map/ppermute | solution.py:322
  2.6 1.6 %collective-permute-start.1 = (bf16[2,32,3072]{2,1,0:T(8,128)(2,1)}, bf16[2,32,3072]{2,1,0:T(8,128)(2,1)S(1)}, u32[]{:S(2)}, u32[]{:S(2)}) collective-permute-start(bf16[2,32,3072]{2,1,0:T(8,128)(2,1)} %refs_0_.2), channel_id=1, source_target_pairs={{0,2},{1,3},{2,0},{3,1},{4,6},{5,7},{6,4},{7,5},{8,10},{9,11},{10,... | collective-permute-start | bytes 1179656 | tf_op jit(solution)/shard_map/ppermute | solution.py:322
  4.2 0.5 collective-permute-start.3
  4.7 0.9 %constant_dynamic-slice_fusion = bf16[16,3072]{1,0:T(8,128)(2,1)S(1)} fusion(bf16[64,3072]{1,0:T(8,128)(2,1)} %refs_0_.3, s32[]{:T(128)S(6)} %select_n.16), kind=kLoop, calls=%fused_computation.2 | loop fusion | bytes 196612 | tf_op jit(solution)/shard_map/dynamic_slice | solution.py:381
  5.6 0.2 collective-permute-start.4
  5.8 17.9 %collective-permute-done.4 = bf16[16,3072]{1,0:T(8,128)(2,1)S(1)} collective-permute-done((bf16[16,3072]{1,0:T(8,128)(2,1)S(1)}, bf16[16,3072]{1,0:T(8,128)(2,1)S(1)}, u32[]{:S(2)}, u32[]{:S(2)}) %collective-permute-start.4) | collective-permute-done | bytes 98336 | tf_op jit(solution)/shard_map/ppermute | solution.py:322
  23.7 0.1 collective-permute-start.7
  23.8 0.5 collective-permute-start.6
  24.3 1.6 %collective-permute-start.5 = (bf16[2,32,3072]{2,1,0:T(8,128)(2,1)S(1)}, bf16[2,32,3072]{2,1,0:T(8,128)(2,1)S(1)}, u32[]{:S(2)}, u32[]{:S(2)}) collective-permute-start(bf16[2,32,3072]{2,1,0:T(8,128)(2,1)S(1)} %collective-permute-done.refs_4_), channel_id=1, source_target_pairs={{0,2},{1,3},{2,0},{3,1},{4,6},{5,7},{6,4},{7,5},{8,10},{9,11},{10,... | collective-permute-start | bytes 1179656 | tf_op jit(solution)/shard_map/ppermute | solution.py:322
  25.9 0.5 collective-permute-start.10
  26.4 1.5 %collective-permute-start.8 = (bf16[16,3072]{1,0:T(8,128)(2,1)S(1)}, bf16[16,3072]{1,0:T(8,128)(2,1)S(1)}, u32[]{:S(2)}, u32[]{:S(2)}) collective-permute-start(bf16[16,3072]{1,0:T(8,128)(2,1)S(1)} %collective-permute-done.4), channel_id=1, source_target_pairs={{0,8},{8,0},{16,24},{24,16},{1,9},{9,1},{17,25},{25,17},{2,10},{10... | collective-permute-start | bytes 294920 | tf_op jit(solution)/shard_map/ppermute | solution.py:322
  27.8 1.5 %collective-permute-start.9 = (bf16[16,3072]{1,0:T(8,128)(2,1)S(1)}, bf16[16,3072]{1,0:T(8,128)(2,1)S(1)}, u32[]{:S(2)}, u32[]{:S(2)}) collective-permute-start(bf16[16,3072]{1,0:T(8,128)(2,1)S(1)} %collective-permute-done.4), channel_id=1, source_target_pairs={{0,16},{8,24},{16,0},{24,8},{1,17},{9,25},{17,1},{25,9},{2,18},{10... | collective-permute-start | bytes 294920 | tf_op jit(solution)/shard_map/ppermute | solution.py:322
  29.4 0.1 pad_add_fusion.ids_ref
  30.1 0.0 copy-start
  30.1 1.3 %copy-done = bf16[192,3072]{1,0:T(8,128)(2,1)S(1)} copy-done((bf16[192,3072]{1,0:T(8,128)(2,1)S(1)}, bf16[192,3072]{1,0:T(8,128)(2,1)}, u32[]{:S(2)}) %copy-start) | copy-done | bytes 1179672
  31.4 1.0 %copy-done.2 = bf16[2,32,3072]{2,1,0:T(8,128)(2,1)S(1)} copy-done((bf16[2,32,3072]{2,1,0:T(8,128)(2,1)S(1)}, bf16[2,32,3072]{2,1,0:T(8,128)(2,1)}, u32[]{:S(2)}) %copy-start.2) | copy-done | bytes 393240
  32.4 0.7 copy-done.5
  33.1 1.5 %project.1 = (bf16[432,128]{1,0:T(8,128)(2,1)S(1)}, bf16[192,128]{1,0:T(8,128)(2,1)S(1)}, bf16[256,3072]{1,0:T(8,128)(2,1)S(1)}) custom-call(s32[3]{0:T(128)S(1)} %pad_add_fusion.ids_ref, bf16[2,32,3072]{2,1,0:T(8,128)(2,1)S(1)} %copy-done.2, bf16[2,32,3072]{2,1,0:T(8,128)(2,1)S(1)} %collective-permute-done.2.refs_1_, ...), custom_call_target="tpu_custom_call" | custom-call | flops 603979776 | bytes 4000000 | tf_op jit(solution)/shard_map/project/pallas_call | solution.py:363
  34.6 0.7 collective-permute-done.5.refs_0_
  35.4 1.6 %collective-permute-start.12 = (bf16[64,3072]{1,0:T(8,128)(2,1)S(1)}, bf16[64,3072]{1,0:T(8,128)(2,1)S(1)}, u32[]{:S(2)}, u32[]{:S(2)}) collective-permute-start(bf16[64,3072]{1,0:T(8,128)(2,1)S(1)} %copy-done.1), channel_id=1, source_target_pairs={{0,2},{1,3},{2,0},{3,1},{4,6},{5,7},{6,4},{7,5},{8,10},{9,11},{10,... | collective-permute-start | bytes 1179656 | tf_op jit(solution)/shard_map/ppermute | solution.py:322
  37.0 2.2 %collective-permute-start.13 = (bf16[64,3072]{1,0:T(8,128)(2,1)S(1)}, bf16[64,3072]{1,0:T(8,128)(2,1)S(1)}, u32[]{:S(2)}, u32[]{:S(2)}) collective-permute-start(bf16[64,3072]{1,0:T(8,128)(2,1)S(1)} %copy-done.1), channel_id=1, source_target_pairs={{0,4},{1,5},{2,6},{3,7},{4,0},{5,1},{6,2},{7,3},{8,12},{9,13},{10,... | collective-permute-start | bytes 1179656 | tf_op jit(solution)/shard_map/ppermute | solution.py:322
  39.2 0.0 copy-start.6
  39.3 0.0 copy-start.7
  39.3 0.0 copy-start.9
  39.3 1.3 %finish.1 = (bf16[576,128]{1,0:T(8,128)(2,1)S(1)}, bf16[64,128]{1,0:T(8,128)(2,1)S(1)}) custom-call(s32[3]{0:T(128)S(1)} %pad_add_fusion.ids_ref, bf16[2,32,3072]{2,1,0:T(8,128)(2,1)S(1)} %collective-permute-done.5.refs_0_, bf16[2,32,3072]{2,1,0:T(8,128)(2,1)S(1)} %collective-permute-done.11.refs_1_, bf16[256,3072]{1,0:T(8,128)(2,1)S(1)} %get-tuple-element.31.refs_2_, ...), custom_call_target="tpu_custom_call" | custom-call | flops 201326592 | bytes 4000000 | tf_op jit(solution)/shard_map/finish/pallas_call | solution.py:363
  40.6 9.3 %all-gather = bf16[2304,128]{1,0:T(8,128)(2,1)S(1)} all-gather(bf16[576,128]{1,0:T(8,128)(2,1)S(1)} %get-tuple-element.33), channel_id=2, replica_groups=mesh['seq'=4,'row'=8] {'seq'}, dimensions={0}, use_global_device_ids=true | all-gather | bytes 737280 | tf_op jit(solution)/shard_map/all_gather | solution.py:404
  50.0 14.7 %chain.1 = bf16[256,128]{1,0:T(8,128)(2,1)S(1)} custom-call(s32[3]{0:T(128)S(1)} %pad_add_fusion.ids_ref, bf16[4,576,128]{2,1,0:T(8,128)(2,1)S(1)} %bitcast.9, bf16[192,128]{1,0:T(8,128)(2,1)S(1)} %get-tuple-element.34.refs_1_, bf16[64,128]{1,0:T(8,128)(2,1)S(1)} %get-tuple-element.35.refs_2_, f32[1,64]{1,0:T(1,128)S(1)} %copy-done.7, ...), custom_call_target="tpu_custom_call" | custom-call | tf_op jit(solution)/shard_map/chain/pallas_call | solution.py:407
  64.7 0.1 collective-permute-start.14
  64.8 0.5 collective-permute-start.15
  65.3 0.1 collective-permute-start.16
  65.4 8.8 %all_to_all.5.heads_ref = bf16[8,32,128]{2,1,0:T(8,128)(2,1)S(1)} all-to-all(bf16[8,32,128]{2,1,0:T(8,128)(2,1)S(1)} %bitcast.10), channel_id=1, replica_groups=mesh['seq'=4,'row'=8] {'row'}, dimensions={0} | all-to-all | bytes 131072 | tf_op jit(solution)/shard_map/all_to_all | solution.py:428
  74.2 1.9 %mix.1 = bf16[2,32,3072]{2,1,0:T(8,128)(2,1)} custom-call(s32[3]{0:T(128)S(1)} %pad_add_fusion.ids_ref, bf16[8,32,128]{2,1,0:T(8,128)(2,1)S(1)} %all_to_all.5.heads_ref, bf16[64,3072]{1,0:T(8,128)(2,1)S(1)} %copy-done.1, bf16[64,3072]{1,0:T(8,128)(2,1)S(1)} %collective-permute-done.3.refs_1_, bf16[64,3072]{1,0:T(8,128)(2,1)S(1)} %collective-permute-done.12.refs_2_, ...), custom_call_target="tpu_custom_call" | custom-call | tf_op jit(solution)/shard_map/mix/pallas_call | solution.py:429
  (31 shorter events, 0.1 us)
Async XLA Ops:
  0.0 23.7 %collective-permute-start = (bf16[2,32,3072]{2,1,0:T(8,128)(2,1)}, bf16[2,32,3072]{2,1,0:T(8,128)(2,1)S(1)}, u32[]{:S(2)}, u32[]{:S(2)}) collective-permute-start(bf16[2,32,3072]{2,1,0:T(8,128)(2,1)} %refs_0_.2), channel_id=1, source_target_pairs={{0,4},{1,5},{2,6},{3,7},{4,0},{5,1},{6,2},{7,3},{8,12},{9,13},{10,... | collective-permute-start | bytes 1179656 | tf_op jit(solution)/shard_map/ppermute | solution.py:322
  2.6 21.1 %collective-permute-start.1 = (bf16[2,32,3072]{2,1,0:T(8,128)(2,1)}, bf16[2,32,3072]{2,1,0:T(8,128)(2,1)S(1)}, u32[]{:S(2)}, u32[]{:S(2)}) collective-permute-start(bf16[2,32,3072]{2,1,0:T(8,128)(2,1)} %refs_0_.2), channel_id=1, source_target_pairs={{0,2},{1,3},{2,0},{3,1},{4,6},{5,7},{6,4},{7,5},{8,10},{9,11},{10,... | collective-permute-start | bytes 1179656 | tf_op jit(solution)/shard_map/ppermute | solution.py:322
  4.2 19.5 %collective-permute-start.2 = (bf16[2,32,3072]{2,1,0:T(8,128)(2,1)}, bf16[2,32,3072]{2,1,0:T(8,128)(2,1)S(1)}, u32[]{:S(2)}, u32[]{:S(2)}) collective-permute-start(bf16[2,32,3072]{2,1,0:T(8,128)(2,1)} %refs_0_.2), channel_id=1, source_target_pairs={{0,1},{1,0},{2,3},{3,2},{4,5},{5,4},{6,7},{7,6},{8,9},{9,8},{10,11... | collective-permute-start | bytes 1179656 | tf_op jit(solution)/shard_map/ppermute | solution.py:322
  4.2 19.5 %collective-permute-start.3 = (bf16[64,3072]{1,0:T(8,128)(2,1)}, bf16[64,3072]{1,0:T(8,128)(2,1)S(1)}, u32[]{:S(2)}, u32[]{:S(2)}) collective-permute-start(bf16[64,3072]{1,0:T(8,128)(2,1)} %refs_0_.3), channel_id=1, source_target_pairs={{0,1},{1,0},{2,3},{3,2},{4,5},{5,4},{6,7},{7,6},{8,9},{9,8},{10,11... | collective-permute-start | bytes 1179656 | tf_op jit(solution)/shard_map/ppermute | solution.py:322
  5.6 18.1 %collective-permute-start.4 = (bf16[16,3072]{1,0:T(8,128)(2,1)S(1)}, bf16[16,3072]{1,0:T(8,128)(2,1)S(1)}, u32[]{:S(2)}, u32[]{:S(2)}) collective-permute-start(bf16[16,3072]{1,0:T(8,128)(2,1)S(1)} %constant_dynamic-slice_fusion), channel_id=1, source_target_pairs={{0,6},{1,7},{2,4},{3,5},{4,2},{5,3},{6,0},{7,1},{8,14},{9,15},{10,... | collective-permute-start | bytes 294920 | tf_op jit(solution)/shard_map/ppermute | solution.py:322
  23.7 4.2 %collective-permute-start.7 = (bf16[2,32,3072]{2,1,0:T(8,128)(2,1)S(1)}, bf16[2,32,3072]{2,1,0:T(8,128)(2,1)S(1)}, u32[]{:S(2)}, u32[]{:S(2)}) collective-permute-start(bf16[2,32,3072]{2,1,0:T(8,128)(2,1)S(1)} %collective-permute-done.refs_4_), channel_id=1, source_target_pairs={{0,1},{1,0},{2,3},{3,2},{4,5},{5,4},{6,7},{7,6},{8,9},{9,8},{10,11... | collective-permute-start | bytes 1179656 | tf_op jit(solution)/shard_map/ppermute | solution.py:322
  23.8 6.3 %collective-permute-start.6 = (bf16[2,32,3072]{2,1,0:T(8,128)(2,1)S(1)}, bf16[2,32,3072]{2,1,0:T(8,128)(2,1)S(1)}, u32[]{:S(2)}, u32[]{:S(2)}) collective-permute-start(bf16[2,32,3072]{2,1,0:T(8,128)(2,1)S(1)} %collective-permute-done.1.refs_2_), channel_id=1, source_target_pairs={{0,1},{1,0},{2,3},{3,2},{4,5},{5,4},{6,7},{7,6},{8,9},{9,8},{10,11... | collective-permute-start | bytes 1179656 | tf_op jit(solution)/shard_map/ppermute | solution.py:322
  24.3 11.1 %collective-permute-start.5 = (bf16[2,32,3072]{2,1,0:T(8,128)(2,1)S(1)}, bf16[2,32,3072]{2,1,0:T(8,128)(2,1)S(1)}, u32[]{:S(2)}, u32[]{:S(2)}) collective-permute-start(bf16[2,32,3072]{2,1,0:T(8,128)(2,1)S(1)} %collective-permute-done.refs_4_), channel_id=1, source_target_pairs={{0,2},{1,3},{2,0},{3,1},{4,6},{5,7},{6,4},{7,5},{8,10},{9,11},{10,... | collective-permute-start | bytes 1179656 | tf_op jit(solution)/shard_map/ppermute | solution.py:322
  25.9 8.7 %collective-permute-start.10 = (bf16[16,3072]{1,0:T(8,128)(2,1)S(1)}, bf16[16,3072]{1,0:T(8,128)(2,1)S(1)}, u32[]{:S(2)}, u32[]{:S(2)}) collective-permute-start(bf16[16,3072]{1,0:T(8,128)(2,1)S(1)} %collective-permute-done.4), channel_id=1, source_target_pairs={{0,24},{8,16},{16,8},{24,0},{1,25},{9,17},{17,9},{25,1},{2,26},{10... | collective-permute-start | bytes 294920 | tf_op jit(solution)/shard_map/ppermute | solution.py:322
  26.4 8.3 %collective-permute-start.8 = (bf16[16,3072]{1,0:T(8,128)(2,1)S(1)}, bf16[16,3072]{1,0:T(8,128)(2,1)S(1)}, u32[]{:S(2)}, u32[]{:S(2)}) collective-permute-start(bf16[16,3072]{1,0:T(8,128)(2,1)S(1)} %collective-permute-done.4), channel_id=1, source_target_pairs={{0,8},{8,0},{16,24},{24,16},{1,9},{9,1},{17,25},{25,17},{2,10},{10... | collective-permute-start | bytes 294920 | tf_op jit(solution)/shard_map/ppermute | solution.py:322
  27.8 6.8 %collective-permute-start.9 = (bf16[16,3072]{1,0:T(8,128)(2,1)S(1)}, bf16[16,3072]{1,0:T(8,128)(2,1)S(1)}, u32[]{:S(2)}, u32[]{:S(2)}) collective-permute-start(bf16[16,3072]{1,0:T(8,128)(2,1)S(1)} %collective-permute-done.4), channel_id=1, source_target_pairs={{0,16},{8,24},{16,0},{24,8},{1,17},{9,25},{17,1},{25,9},{2,18},{10... | collective-permute-start | bytes 294920 | tf_op jit(solution)/shard_map/ppermute | solution.py:322
  30.1 1.3 %copy-start = (bf16[192,3072]{1,0:T(8,128)(2,1)S(1)}, bf16[192,3072]{1,0:T(8,128)(2,1)}, u32[]{:S(2)}) copy-start(bf16[192,3072]{1,0:T(8,128)(2,1)} %refs_6_.2) | copy-start | bytes 3538948
  31.4 1.0 %copy-start.2 = (bf16[2,32,3072]{2,1,0:T(8,128)(2,1)S(1)}, bf16[2,32,3072]{2,1,0:T(8,128)(2,1)}, u32[]{:S(2)}) copy-start(bf16[2,32,3072]{2,1,0:T(8,128)(2,1)} %refs_0_.2) | copy-start | bytes 1179652
  32.4 0.7 copy-start.5
  33.1 2.3 %copy-start.1 = (bf16[64,3072]{1,0:T(8,128)(2,1)S(1)}, bf16[64,3072]{1,0:T(8,128)(2,1)}, u32[]{:S(2)}) copy-start(bf16[64,3072]{1,0:T(8,128)(2,1)} %refs_0_.3) | copy-start | bytes 1179652
  35.4 3.9 %collective-permute-start.11 = (bf16[2,32,3072]{2,1,0:T(8,128)(2,1)S(1)}, bf16[2,32,3072]{2,1,0:T(8,128)(2,1)S(1)}, u32[]{:S(2)}, u32[]{:S(2)}) collective-permute-start(bf16[2,32,3072]{2,1,0:T(8,128)(2,1)S(1)} %collective-permute-done.5.refs_0_), channel_id=1, source_target_pairs={{0,1},{1,0},{2,3},{3,2},{4,5},{5,4},{6,7},{7,6},{8,9},{9,8},{10,11... | collective-permute-start | bytes 1179656 | tf_op jit(solution)/shard_map/ppermute | solution.py:322
  35.4 29.3 %collective-permute-start.12 = (bf16[64,3072]{1,0:T(8,128)(2,1)S(1)}, bf16[64,3072]{1,0:T(8,128)(2,1)S(1)}, u32[]{:S(2)}, u32[]{:S(2)}) collective-permute-start(bf16[64,3072]{1,0:T(8,128)(2,1)S(1)} %copy-done.1), channel_id=1, source_target_pairs={{0,2},{1,3},{2,0},{3,1},{4,6},{5,7},{6,4},{7,5},{8,10},{9,11},{10,... | collective-permute-start | bytes 1179656 | tf_op jit(solution)/shard_map/ppermute | solution.py:322
  37.0 27.7 %collective-permute-start.13 = (bf16[64,3072]{1,0:T(8,128)(2,1)S(1)}, bf16[64,3072]{1,0:T(8,128)(2,1)S(1)}, u32[]{:S(2)}, u32[]{:S(2)}) collective-permute-start(bf16[64,3072]{1,0:T(8,128)(2,1)S(1)} %copy-done.1), channel_id=1, source_target_pairs={{0,4},{1,5},{2,6},{3,7},{4,0},{5,1},{6,2},{7,3},{8,12},{9,13},{10,... | collective-permute-start | bytes 1179656 | tf_op jit(solution)/shard_map/ppermute | solution.py:322
  39.2 10.7 %copy-start.3 = (f32[1,64,256]{2,1,0:T(8,128)S(1)}, f32[1,64,256]{2,1,0:T(8,128)}, u32[]{:S(2)}) copy-start(f32[1,64,256]{2,1,0:T(8,128)} %refs_5_.1) | copy-start | bytes 196612
  39.2 10.7 %copy-start.4 = (f32[1,256,64]{1,2,0:T(8,128)S(1)}, f32[1,256,64]{1,2,0:T(8,128)}, u32[]{:S(2)}) copy-start(f32[1,256,64]{1,2,0:T(8,128)} %param.18) | copy-start | bytes 196612
  39.2 10.7 %copy-start.6 = (f32[1,256]{1,0:T(1,128)S(1)}, f32[1,256]{1,0:T(1,128)}, u32[]{:S(2)}) copy-start(f32[1,256]{1,0:T(1,128)} %refs_6_.3) | copy-start | bytes 3076
  39.3 10.7 %copy-start.7 = (f32[1,64]{1,0:T(1,128)S(1)}, f32[1,64]{1,0:T(1,128)}, u32[]{:S(2)}) copy-start(f32[1,64]{1,0:T(1,128)} %refs_3_.1) | copy-start | bytes 772
  39.3 10.7 %copy-start.8 = (f32[1,64]{1,0:T(1,128)S(1)}, f32[1,64]{1,0:T(1,128)}, u32[]{:S(2)}) copy-start(f32[1,64]{1,0:T(1,128)} %refs_4_.1) | copy-start | bytes 772
  39.3 10.7 %copy-start.9 = (f32[1,64]{1,0:T(1,128)S(1)}, f32[1,64]{1,0:T(1,128)}, u32[]{:S(2)}) copy-start(f32[1,64]{1,0:T(1,128)} %refs_8_.1) | copy-start | bytes 772
  64.7 9.4 %collective-permute-start.14 = (bf16[64,3072]{1,0:T(8,128)(2,1)S(1)}, bf16[64,3072]{1,0:T(8,128)(2,1)S(1)}, u32[]{:S(2)}, u32[]{:S(2)}) collective-permute-start(bf16[64,3072]{1,0:T(8,128)(2,1)S(1)} %collective-permute-done.12.refs_2_), channel_id=1, source_target_pairs={{0,1},{1,0},{2,3},{3,2},{4,5},{5,4},{6,7},{7,6},{8,9},{9,8},{10,11... | collective-permute-start | bytes 1179656 | tf_op jit(solution)/shard_map/ppermute | solution.py:322
  64.8 9.4 %collective-permute-start.15 = (bf16[64,3072]{1,0:T(8,128)(2,1)S(1)}, bf16[64,3072]{1,0:T(8,128)(2,1)S(1)}, u32[]{:S(2)}, u32[]{:S(2)}) collective-permute-start(bf16[64,3072]{1,0:T(8,128)(2,1)S(1)} %collective-permute-done.13.refs_4_), channel_id=1, source_target_pairs={{0,1},{1,0},{2,3},{3,2},{4,5},{5,4},{6,7},{7,6},{8,9},{9,8},{10,11... | collective-permute-start | bytes 1179656 | tf_op jit(solution)/shard_map/ppermute | solution.py:322
  65.3 8.9 %collective-permute-start.16 = (bf16[64,3072]{1,0:T(8,128)(2,1)S(1)}, bf16[64,3072]{1,0:T(8,128)(2,1)S(1)}, u32[]{:S(2)}, u32[]{:S(2)}) collective-permute-start(bf16[64,3072]{1,0:T(8,128)(2,1)S(1)} %pad_maximum_fusion.refs_6_), channel_id=1, source_target_pairs={{0,1},{1,0},{2,3},{3,2},{4,5},{5,4},{6,7},{7,6},{8,9},{9,8},{10,11... | collective-permute-start | bytes 1179656 | tf_op jit(solution)/shard_map/ppermute | solution.py:322

commit v8 on v7

--- a/solution.py
+++ b/solution.py
@@ -181,11 +181,9 @@
 
         x2, slope = gelu_both(z1)
         x2h, x2m, x2l = thirds(x2)
-        pieces = dot(
-            jnp.concatenate([x2h, x2m, x2l], axis=0), jnp.concatenate([w2h, w2m], axis=1)
-        )
-        small = dot(x2h, w2l) + pieces[both : 2 * both, both:] + pieces[2 * both :, :both]
-        medium = pieces[:both, both:] + pieces[both : 2 * both, :both]
+        pieces = dot(jnp.concatenate([x2h, x2m], axis=0), jnp.concatenate([w2h, w2m], axis=1))
+        small = dot(x2h, w2l) + (dot(x2l, w2h) + pieces[both:, both:])
+        medium = pieces[:both, both:] + pieces[both:, :both]
         z = lane_cat(pieces[:both, :both] + (medium + small)) + b2
         scaled = gain_sq * z
         rs = lax.rsqrt(halves(z * z) * (1.0 / d) + ln_eps)
@@ -198,7 +196,7 @@
         h1h = (d1 * slope).astype(bf16)
         h1 = h1h.astype(f32)
         h2 = spread(alpha) * ((gain_sq - spread(mean_gn)) * (spread(rs) * z) + (u - spread(mean_g)))
-        h2h, h2m, h2l = (blocks(x) for x in thirds(h2))
+        h2h, h2m = (blocks(x) for x in halved(h2))
 
         z1_next, kb_next, result = None, None, None
         streams = [] if nxt is None else [blocks(nxt)]
@@ -235,9 +233,7 @@
             axis=0,
         )
         w2 = w2 - dot(
-            jnp.concatenate([x2h, x2m, x2h, x2l, x2m, x2h], axis=0),
-            jnp.concatenate([h2h, h2h, h2m, h2h, h2m, h2l], axis=0),
-            TN,
+            jnp.concatenate([x2h, x2m, x2h], axis=0), jnp.concatenate([h2h, h2h, h2m], axis=0), TN
         )
         b2 = b2 - jnp.sum(h2, axis=0, keepdims=True)
         return (w1, b1, w2, b2), z1_next, kb_next, result
@@ -390,7 +386,7 @@
         w_end = jnp.concatenate(w_end, axis=0)
         late = [last, swapped(last, 1)]
         w_after, _ = lax.optimization_barrier((w_out, last))
-        w_far, w_near = swapped(w_after, 4), swapped(w_after, 2)
+        w_near, w_far = swapped(w_after, 2), swapped(w_after, 4)
         kv, q_late = project(1, 2, False, late, (stack,), kv_early)
     else:
         whole = lax.all_gather(tokens, "row", axis=1, tiled=True)

time: 76.4 us -> 75.6 us (0.990)
  Pallas kernels: 19.4 us -> 18.6 us
    pallas_call x1, Pallas kernels: 14.7 us -> 13.8 us  [on_device(): pl.pallas_call(partial(chain_kernel, seq_count), out_shape=jax.ShapeDtype...]
  transfers between devices with their start and end apart: 17 -> 17, of which waited for: 2 -> 2; matrix products, arithmetic and copies ran while one was open for 1% -> 1% of each run, Pallas kernels for 23% -> 22%
where the time goes in v8:
time: 75.6 us; the launch traced here: 75.3 us
  waiting for transfers between devices  18.6 us (25%)
  Pallas kernels  18.6 us (25%)
  blocking collectives  18.1 us (24%)
  starting transfers between devices  15 us (20%)
  local copies, waits for them, and re-layouts  3.91 us (5%)
  between operations  0.88 us (1%)
    ppermute x17, waiting for transfers between devices, swapped(): lax.ppermute(array, axis, [(i, i ^ flip) for i in range(lax.axis_size(axi...  18.6 us
    ppermute x17, starting transfers between devices, swapped(): lax.ppermute(array, axis, [(i, i ^ flip) for i in range(lax.axis_size(axi...  15 us
    pallas_call x1, Pallas kernels, on_device(): pl.pallas_call(partial(chain_kernel, seq_count), out_shape=jax.ShapeDtype...  13.8 us
    all_gather x1, blocking collectives, on_device(): operands = [lax.all_gather(kv, 'seq'), q_early, q_late, ln_gain, ln_bias]  9.33 us
    all_to_all x1, blocking collectives, on_device(): lax.all_to_all(heads, 'row', split_axis=0, concat_axis=0, tiled=True)  8.77 us
    unnamed x20, local copies, waits for them, and re-layouts  3.01 us
    pallas_call x2, Pallas kernels, project(): pl.pallas_call(partial(project_kernel, count, pieces, first), out_shape=o...  2.81 us
    pallas_call x1, Pallas kernels, on_device(): pl.pallas_call(partial(out_kernel, len(w_parts)), out_shape=jax.ShapeDtyp...  1.94 us
  transfers between devices with their start and end apart: 17, of which 2 were waited for; matrix products, arithmetic and copies ran while one was open for 1% of the time, Pallas kernels for 22%

profile of v8, /device:TPU:6, one launch (start us, length us, event | category | flops | bytes accessed | tf_op | source)
XLA Modules:
  0.0 75.3 jit_solution(10618451688529391956)
XLA Ops:
  0.0 2.6 %collective-permute-start = (bf16[2,32,3072]{2,1,0:T(8,128)(2,1)}, bf16[2,32,3072]{2,1,0:T(8,128)(2,1)S(1)}, u32[]{:S(2)}, u32[]{:S(2)}) collective-permute-start(bf16[2,32,3072]{2,1,0:T(8,128)(2,1)} %refs_0_.2), channel_id=1, source_target_pairs={{0,4},{1,5},{2,6},{3,7},{4,0},{5,1},{6,2},{7,3},{8,12},{9,13},{10,... | collective-permute-start | bytes 1179656 | tf_op jit(solution)/shard_map/ppermute | solution.py:318
  2.6 1.6 %collective-permute-start.1 = (bf16[2,32,3072]{2,1,0:T(8,128)(2,1)}, bf16[2,32,3072]{2,1,0:T(8,128)(2,1)S(1)}, u32[]{:S(2)}, u32[]{:S(2)}) collective-permute-start(bf16[2,32,3072]{2,1,0:T(8,128)(2,1)} %refs_0_.2), channel_id=1, source_target_pairs={{0,2},{1,3},{2,0},{3,1},{4,6},{5,7},{6,4},{7,5},{8,10},{9,11},{10,... | collective-permute-start | bytes 1179656 | tf_op jit(solution)/shard_map/ppermute | solution.py:318
  4.2 0.5 collective-permute-start.3
  4.7 0.9 %constant_dynamic-slice_fusion = bf16[16,3072]{1,0:T(8,128)(2,1)S(1)} fusion(bf16[64,3072]{1,0:T(8,128)(2,1)} %refs_0_.3, s32[]{:T(128)S(6)} %select_n.16), kind=kLoop, calls=%fused_computation.2 | loop fusion | bytes 196612 | tf_op jit(solution)/shard_map/dynamic_slice | solution.py:377
  5.6 0.2 collective-permute-start.4
  5.8 17.9 %collective-permute-done.4 = bf16[16,3072]{1,0:T(8,128)(2,1)S(1)} collective-permute-done((bf16[16,3072]{1,0:T(8,128)(2,1)S(1)}, bf16[16,3072]{1,0:T(8,128)(2,1)S(1)}, u32[]{:S(2)}, u32[]{:S(2)}) %collective-permute-start.4) | collective-permute-done | bytes 98336 | tf_op jit(solution)/shard_map/ppermute | solution.py:318
  23.7 0.1 collective-permute-start.7
  23.8 0.5 collective-permute-start.6
  24.3 1.6 %collective-permute-start.5 = (bf16[2,32,3072]{2,1,0:T(8,128)(2,1)S(1)}, bf16[2,32,3072]{2,1,0:T(8,128)(2,1)S(1)}, u32[]{:S(2)}, u32[]{:S(2)}) collective-permute-start(bf16[2,32,3072]{2,1,0:T(8,128)(2,1)S(1)} %collective-permute-done.refs_4_), channel_id=1, source_target_pairs={{0,2},{1,3},{2,0},{3,1},{4,6},{5,7},{6,4},{7,5},{8,10},{9,11},{10,... | collective-permute-start | bytes 1179656 | tf_op jit(solution)/shard_map/ppermute | solution.py:318
  25.9 0.5 collective-permute-start.10
  26.4 1.5 %collective-permute-start.8 = (bf16[16,3072]{1,0:T(8,128)(2,1)S(1)}, bf16[16,3072]{1,0:T(8,128)(2,1)S(1)}, u32[]{:S(2)}, u32[]{:S(2)}) collective-permute-start(bf16[16,3072]{1,0:T(8,128)(2,1)S(1)} %collective-permute-done.4), channel_id=1, source_target_pairs={{0,8},{8,0},{16,24},{24,16},{1,9},{9,1},{17,25},{25,17},{2,10},{10... | collective-permute-start | bytes 294920 | tf_op jit(solution)/shard_map/ppermute | solution.py:318
  27.8 1.5 %collective-permute-start.9 = (bf16[16,3072]{1,0:T(8,128)(2,1)S(1)}, bf16[16,3072]{1,0:T(8,128)(2,1)S(1)}, u32[]{:S(2)}, u32[]{:S(2)}) collective-permute-start(bf16[16,3072]{1,0:T(8,128)(2,1)S(1)} %collective-permute-done.4), channel_id=1, source_target_pairs={{0,16},{8,24},{16,0},{24,8},{1,17},{9,25},{17,1},{25,9},{2,18},{10... | collective-permute-start | bytes 294920 | tf_op jit(solution)/shard_map/ppermute | solution.py:318
  29.4 0.1 pad_add_fusion.ids_ref
  30.1 0.0 copy-start
  30.1 1.3 %copy-done = bf16[192,3072]{1,0:T(8,128)(2,1)S(1)} copy-done((bf16[192,3072]{1,0:T(8,128)(2,1)S(1)}, bf16[192,3072]{1,0:T(8,128)(2,1)}, u32[]{:S(2)}) %copy-start) | copy-done | bytes 1179672
  31.4 1.0 %copy-done.2 = bf16[2,32,3072]{2,1,0:T(8,128)(2,1)S(1)} copy-done((bf16[2,32,3072]{2,1,0:T(8,128)(2,1)S(1)}, bf16[2,32,3072]{2,1,0:T(8,128)(2,1)}, u32[]{:S(2)}) %copy-start.2) | copy-done | bytes 393240
  32.4 0.7 copy-done.5
  33.1 1.5 %project.1 = (bf16[432,128]{1,0:T(8,128)(2,1)S(1)}, bf16[192,128]{1,0:T(8,128)(2,1)S(1)}, bf16[256,3072]{1,0:T(8,128)(2,1)S(1)}) custom-call(s32[3]{0:T(128)S(1)} %pad_add_fusion.ids_ref, bf16[2,32,3072]{2,1,0:T(8,128)(2,1)S(1)} %copy-done.2, bf16[2,32,3072]{2,1,0:T(8,128)(2,1)S(1)} %collective-permute-done.2.refs_1_, ...), custom_call_target="tpu_custom_call" | custom-call | flops 603979776 | bytes 4000000 | tf_op jit(solution)/shard_map/project/pallas_call | solution.py:359
  34.6 0.7 collective-permute-done.5.refs_0_
  35.4 1.6 %collective-permute-start.12 = (bf16[64,3072]{1,0:T(8,128)(2,1)S(1)}, bf16[64,3072]{1,0:T(8,128)(2,1)S(1)}, u32[]{:S(2)}, u32[]{:S(2)}) collective-permute-start(bf16[64,3072]{1,0:T(8,128)(2,1)S(1)} %copy-done.1), channel_id=1, source_target_pairs={{0,2},{1,3},{2,0},{3,1},{4,6},{5,7},{6,4},{7,5},{8,10},{9,11},{10,... | collective-permute-start | bytes 1179656 | tf_op jit(solution)/shard_map/ppermute | solution.py:318
  37.0 2.2 %collective-permute-start.13 = (bf16[64,3072]{1,0:T(8,128)(2,1)S(1)}, bf16[64,3072]{1,0:T(8,128)(2,1)S(1)}, u32[]{:S(2)}, u32[]{:S(2)}) collective-permute-start(bf16[64,3072]{1,0:T(8,128)(2,1)S(1)} %copy-done.1), channel_id=1, source_target_pairs={{0,4},{1,5},{2,6},{3,7},{4,0},{5,1},{6,2},{7,3},{8,12},{9,13},{10,... | collective-permute-start | bytes 1179656 | tf_op jit(solution)/shard_map/ppermute | solution.py:318
  39.2 0.0 copy-start.6
  39.3 0.0 copy-start.7
  39.3 0.0 copy-start.9
  39.3 1.3 %finish.1 = (bf16[576,128]{1,0:T(8,128)(2,1)S(1)}, bf16[64,128]{1,0:T(8,128)(2,1)S(1)}) custom-call(s32[3]{0:T(128)S(1)} %pad_add_fusion.ids_ref, bf16[2,32,3072]{2,1,0:T(8,128)(2,1)S(1)} %collective-permute-done.5.refs_0_, bf16[2,32,3072]{2,1,0:T(8,128)(2,1)S(1)} %collective-permute-done.11.refs_1_, bf16[256,3072]{1,0:T(8,128)(2,1)S(1)} %get-tuple-element.31.refs_2_, ...), custom_call_target="tpu_custom_call" | custom-call | flops 201326592 | bytes 4000000 | tf_op jit(solution)/shard_map/finish/pallas_call | solution.py:359
  40.6 9.3 %all-gather = bf16[2304,128]{1,0:T(8,128)(2,1)S(1)} all-gather(bf16[576,128]{1,0:T(8,128)(2,1)S(1)} %get-tuple-element.33), channel_id=2, replica_groups=mesh['seq'=4,'row'=8] {'seq'}, dimensions={0}, use_global_device_ids=true | all-gather | bytes 737280 | tf_op jit(solution)/shard_map/all_gather | solution.py:400
  50.0 13.8 %chain.1 = bf16[256,128]{1,0:T(8,128)(2,1)S(1)} custom-call(s32[3]{0:T(128)S(1)} %pad_add_fusion.ids_ref, bf16[4,576,128]{2,1,0:T(8,128)(2,1)S(1)} %bitcast.9, bf16[192,128]{1,0:T(8,128)(2,1)S(1)} %get-tuple-element.34.refs_1_, bf16[64,128]{1,0:T(8,128)(2,1)S(1)} %get-tuple-element.35.refs_2_, f32[1,64]{1,0:T(1,128)S(1)} %copy-done.7, ...), custom_call_target="tpu_custom_call" | custom-call | tf_op jit(solution)/shard_map/chain/pallas_call | solution.py:403
  63.9 0.1 collective-permute-start.14
  64.0 0.5 collective-permute-start.15
  64.4 0.1 collective-permute-start.16
  64.5 8.8 %all_to_all.5.heads_ref = bf16[8,32,128]{2,1,0:T(8,128)(2,1)S(1)} all-to-all(bf16[8,32,128]{2,1,0:T(8,128)(2,1)S(1)} %bitcast.10), channel_id=1, replica_groups=mesh['seq'=4,'row'=8] {'row'}, dimensions={0} | all-to-all | bytes 131072 | tf_op jit(solution)/shard_map/all_to_all | solution.py:424
  73.3 1.9 %mix.1 = bf16[2,32,3072]{2,1,0:T(8,128)(2,1)} custom-call(s32[3]{0:T(128)S(1)} %pad_add_fusion.ids_ref, bf16[8,32,128]{2,1,0:T(8,128)(2,1)S(1)} %all_to_all.5.heads_ref, bf16[64,3072]{1,0:T(8,128)(2,1)S(1)} %copy-done.1, bf16[64,3072]{1,0:T(8,128)(2,1)S(1)} %collective-permute-done.3.refs_1_, bf16[64,3072]{1,0:T(8,128)(2,1)S(1)} %collective-permute-done.12.refs_2_, ...), custom_call_target="tpu_custom_call" | custom-call | tf_op jit(solution)/shard_map/mix/pallas_call | solution.py:425
  (31 shorter events, 0.1 us)
Async XLA Ops:
  0.0 23.7 %collective-permute-start = (bf16[2,32,3072]{2,1,0:T(8,128)(2,1)}, bf16[2,32,3072]{2,1,0:T(8,128)(2,1)S(1)}, u32[]{:S(2)}, u32[]{:S(2)}) collective-permute-start(bf16[2,32,3072]{2,1,0:T(8,128)(2,1)} %refs_0_.2), channel_id=1, source_target_pairs={{0,4},{1,5},{2,6},{3,7},{4,0},{5,1},{6,2},{7,3},{8,12},{9,13},{10,... | collective-permute-start | bytes 1179656 | tf_op jit(solution)/shard_map/ppermute | solution.py:318
  2.6 21.1 %collective-permute-start.1 = (bf16[2,32,3072]{2,1,0:T(8,128)(2,1)}, bf16[2,32,3072]{2,1,0:T(8,128)(2,1)S(1)}, u32[]{:S(2)}, u32[]{:S(2)}) collective-permute-start(bf16[2,32,3072]{2,1,0:T(8,128)(2,1)} %refs_0_.2), channel_id=1, source_target_pairs={{0,2},{1,3},{2,0},{3,1},{4,6},{5,7},{6,4},{7,5},{8,10},{9,11},{10,... | collective-permute-start | bytes 1179656 | tf_op jit(solution)/shard_map/ppermute | solution.py:318
  4.2 19.5 %collective-permute-start.2 = (bf16[2,32,3072]{2,1,0:T(8,128)(2,1)}, bf16[2,32,3072]{2,1,0:T(8,128)(2,1)S(1)}, u32[]{:S(2)}, u32[]{:S(2)}) collective-permute-start(bf16[2,32,3072]{2,1,0:T(8,128)(2,1)} %refs_0_.2), channel_id=1, source_target_pairs={{0,1},{1,0},{2,3},{3,2},{4,5},{5,4},{6,7},{7,6},{8,9},{9,8},{10,11... | collective-permute-start | bytes 1179656 | tf_op jit(solution)/shard_map/ppermute | solution.py:318
  4.2 19.5 %collective-permute-start.3 = (bf16[64,3072]{1,0:T(8,128)(2,1)}, bf16[64,3072]{1,0:T(8,128)(2,1)S(1)}, u32[]{:S(2)}, u32[]{:S(2)}) collective-permute-start(bf16[64,3072]{1,0:T(8,128)(2,1)} %refs_0_.3), channel_id=1, source_target_pairs={{0,1},{1,0},{2,3},{3,2},{4,5},{5,4},{6,7},{7,6},{8,9},{9,8},{10,11... | collective-permute-start | bytes 1179656 | tf_op jit(solution)/shard_map/ppermute | solution.py:318
  5.6 18.1 %collective-permute-start.4 = (bf16[16,3072]{1,0:T(8,128)(2,1)S(1)}, bf16[16,3072]{1,0:T(8,128)(2,1)S(1)}, u32[]{:S(2)}, u32[]{:S(2)}) collective-permute-start(bf16[16,3072]{1,0:T(8,128)(2,1)S(1)} %constant_dynamic-slice_fusion), channel_id=1, source_target_pairs={{0,6},{1,7},{2,4},{3,5},{4,2},{5,3},{6,0},{7,1},{8,14},{9,15},{10,... | collective-permute-start | bytes 294920 | tf_op jit(solution)/shard_map/ppermute | solution.py:318
  23.7 4.2 %collective-permute-start.7 = (bf16[2,32,3072]{2,1,0:T(8,128)(2,1)S(1)}, bf16[2,32,3072]{2,1,0:T(8,128)(2,1)S(1)}, u32[]{:S(2)}, u32[]{:S(2)}) collective-permute-start(bf16[2,32,3072]{2,1,0:T(8,128)(2,1)S(1)} %collective-permute-done.refs_4_), channel_id=1, source_target_pairs={{0,1},{1,0},{2,3},{3,2},{4,5},{5,4},{6,7},{7,6},{8,9},{9,8},{10,11... | collective-permute-start | bytes 1179656 | tf_op jit(solution)/shard_map/ppermute | solution.py:318
  23.8 6.3 %collective-permute-start.6 = (bf16[2,32,3072]{2,1,0:T(8,128)(2,1)S(1)}, bf16[2,32,3072]{2,1,0:T(8,128)(2,1)S(1)}, u32[]{:S(2)}, u32[]{:S(2)}) collective-permute-start(bf16[2,32,3072]{2,1,0:T(8,128)(2,1)S(1)} %collective-permute-done.1.refs_2_), channel_id=1, source_target_pairs={{0,1},{1,0},{2,3},{3,2},{4,5},{5,4},{6,7},{7,6},{8,9},{9,8},{10,11... | collective-permute-start | bytes 1179656 | tf_op jit(solution)/shard_map/ppermute | solution.py:318
  24.3 11.1 %collective-permute-start.5 = (bf16[2,32,3072]{2,1,0:T(8,128)(2,1)S(1)}, bf16[2,32,3072]{2,1,0:T(8,128)(2,1)S(1)}, u32[]{:S(2)}, u32[]{:S(2)}) collective-permute-start(bf16[2,32,3072]{2,1,0:T(8,128)(2,1)S(1)} %collective-permute-done.refs_4_), channel_id=1, source_target_pairs={{0,2},{1,3},{2,0},{3,1},{4,6},{5,7},{6,4},{7,5},{8,10},{9,11},{10,... | collective-permute-start | bytes 1179656 | tf_op jit(solution)/shard_map/ppermute | solution.py:318
  25.9 8.7 %collective-permute-start.10 = (bf16[16,3072]{1,0:T(8,128)(2,1)S(1)}, bf16[16,3072]{1,0:T(8,128)(2,1)S(1)}, u32[]{:S(2)}, u32[]{:S(2)}) collective-permute-start(bf16[16,3072]{1,0:T(8,128)(2,1)S(1)} %collective-permute-done.4), channel_id=1, source_target_pairs={{0,24},{8,16},{16,8},{24,0},{1,25},{9,17},{17,9},{25,1},{2,26},{10... | collective-permute-start | bytes 294920 | tf_op jit(solution)/shard_map/ppermute | solution.py:318
  26.4 8.3 %collective-permute-start.8 = (bf16[16,3072]{1,0:T(8,128)(2,1)S(1)}, bf16[16,3072]{1,0:T(8,128)(2,1)S(1)}, u32[]{:S(2)}, u32[]{:S(2)}) collective-permute-start(bf16[16,3072]{1,0:T(8,128)(2,1)S(1)} %collective-permute-done.4), channel_id=1, source_target_pairs={{0,8},{8,0},{16,24},{24,16},{1,9},{9,1},{17,25},{25,17},{2,10},{10... | collective-permute-start | bytes 294920 | tf_op jit(solution)/shard_map/ppermute | solution.py:318
  27.8 6.8 %collective-permute-start.9 = (bf16[16,3072]{1,0:T(8,128)(2,1)S(1)}, bf16[16,3072]{1,0:T(8,128)(2,1)S(1)}, u32[]{:S(2)}, u32[]{:S(2)}) collective-permute-start(bf16[16,3072]{1,0:T(8,128)(2,1)S(1)} %collective-permute-done.4), channel_id=1, source_target_pairs={{0,16},{8,24},{16,0},{24,8},{1,17},{9,25},{17,1},{25,9},{2,18},{10... | collective-permute-start | bytes 294920 | tf_op jit(solution)/shard_map/ppermute | solution.py:318
  30.1 1.3 %copy-start = (bf16[192,3072]{1,0:T(8,128)(2,1)S(1)}, bf16[192,3072]{1,0:T(8,128)(2,1)}, u32[]{:S(2)}) copy-start(bf16[192,3072]{1,0:T(8,128)(2,1)} %refs_6_.2) | copy-start | bytes 3538948
  31.4 1.0 %copy-start.2 = (bf16[2,32,3072]{2,1,0:T(8,128)(2,1)S(1)}, bf16[2,32,3072]{2,1,0:T(8,128)(2,1)}, u32[]{:S(2)}) copy-start(bf16[2,32,3072]{2,1,0:T(8,128)(2,1)} %refs_0_.2) | copy-start | bytes 1179652
  32.4 0.7 copy-start.5
  33.1 2.3 %copy-start.1 = (bf16[64,3072]{1,0:T(8,128)(2,1)S(1)}, bf16[64,3072]{1,0:T(8,128)(2,1)}, u32[]{:S(2)}) copy-start(bf16[64,3072]{1,0:T(8,128)(2,1)} %refs_0_.3) | copy-start | bytes 1179652
  35.4 3.9 %collective-permute-start.11 = (bf16[2,32,3072]{2,1,0:T(8,128)(2,1)S(1)}, bf16[2,32,3072]{2,1,0:T(8,128)(2,1)S(1)}, u32[]{:S(2)}, u32[]{:S(2)}) collective-permute-start(bf16[2,32,3072]{2,1,0:T(8,128)(2,1)S(1)} %collective-permute-done.5.refs_0_), channel_id=1, source_target_pairs={{0,1},{1,0},{2,3},{3,2},{4,5},{5,4},{6,7},{7,6},{8,9},{9,8},{10,11... | collective-permute-start | bytes 1179656 | tf_op jit(solution)/shard_map/ppermute | solution.py:318
  35.4 28.5 %collective-permute-start.12 = (bf16[64,3072]{1,0:T(8,128)(2,1)S(1)}, bf16[64,3072]{1,0:T(8,128)(2,1)S(1)}, u32[]{:S(2)}, u32[]{:S(2)}) collective-permute-start(bf16[64,3072]{1,0:T(8,128)(2,1)S(1)} %copy-done.1), channel_id=1, source_target_pairs={{0,2},{1,3},{2,0},{3,1},{4,6},{5,7},{6,4},{7,5},{8,10},{9,11},{10,... | collective-permute-start | bytes 1179656 | tf_op jit(solution)/shard_map/ppermute | solution.py:318
  37.0 26.9 %collective-permute-start.13 = (bf16[64,3072]{1,0:T(8,128)(2,1)S(1)}, bf16[64,3072]{1,0:T(8,128)(2,1)S(1)}, u32[]{:S(2)}, u32[]{:S(2)}) collective-permute-start(bf16[64,3072]{1,0:T(8,128)(2,1)S(1)} %copy-done.1), channel_id=1, source_target_pairs={{0,4},{1,5},{2,6},{3,7},{4,0},{5,1},{6,2},{7,3},{8,12},{9,13},{10,... | collective-permute-start | bytes 1179656 | tf_op jit(solution)/shard_map/ppermute | solution.py:318
  39.2 10.7 %copy-start.3 = (f32[1,64,256]{2,1,0:T(8,128)S(1)}, f32[1,64,256]{2,1,0:T(8,128)}, u32[]{:S(2)}) copy-start(f32[1,64,256]{2,1,0:T(8,128)} %refs_5_.1) | copy-start | bytes 196612
  39.2 10.7 %copy-start.4 = (f32[1,256,64]{1,2,0:T(8,128)S(1)}, f32[1,256,64]{1,2,0:T(8,128)}, u32[]{:S(2)}) copy-start(f32[1,256,64]{1,2,0:T(8,128)} %param.18) | copy-start | bytes 196612
  39.2 10.7 %copy-start.6 = (f32[1,256]{1,0:T(1,128)S(1)}, f32[1,256]{1,0:T(1,128)}, u32[]{:S(2)}) copy-start(f32[1,256]{1,0:T(1,128)} %refs_6_.3) | copy-start | bytes 3076
  39.3 10.7 %copy-start.7 = (f32[1,64]{1,0:T(1,128)S(1)}, f32[1,64]{1,0:T(1,128)}, u32[]{:S(2)}) copy-start(f32[1,64]{1,0:T(1,128)} %refs_3_.1) | copy-start | bytes 772
  39.3 10.7 %copy-start.8 = (f32[1,64]{1,0:T(1,128)S(1)}, f32[1,64]{1,0:T(1,128)}, u32[]{:S(2)}) copy-start(f32[1,64]{1,0:T(1,128)} %refs_4_.1) | copy-start | bytes 772
  39.3 10.7 %copy-start.9 = (f32[1,64]{1,0:T(1,128)S(1)}, f32[1,64]{1,0:T(1,128)}, u32[]{:S(2)}) copy-start(f32[1,64]{1,0:T(1,128)} %refs_8_.1) | copy-start | bytes 772
  63.9 9.4 %collective-permute-start.14 = (bf16[64,3072]{1,0:T(8,128)(2,1)S(1)}, bf16[64,3072]{1,0:T(8,128)(2,1)S(1)}, u32[]{:S(2)}, u32[]{:S(2)}) collective-permute-start(bf16[64,3072]{1,0:T(8,128)(2,1)S(1)} %collective-permute-done.12.refs_2_), channel_id=1, source_target_pairs={{0,1},{1,0},{2,3},{3,2},{4,5},{5,4},{6,7},{7,6},{8,9},{9,8},{10,11... | collective-permute-start | bytes 1179656 | tf_op jit(solution)/shard_map/ppermute | solution.py:318
  64.0 9.4 %collective-permute-start.15 = (bf16[64,3072]{1,0:T(8,128)(2,1)S(1)}, bf16[64,3072]{1,0:T(8,128)(2,1)S(1)}, u32[]{:S(2)}, u32[]{:S(2)}) collective-permute-start(bf16[64,3072]{1,0:T(8,128)(2,1)S(1)} %collective-permute-done.13.refs_4_), channel_id=1, source_target_pairs={{0,1},{1,0},{2,3},{3,2},{4,5},{5,4},{6,7},{7,6},{8,9},{9,8},{10,11... | collective-permute-start | bytes 1179656 | tf_op jit(solution)/shard_map/ppermute | solution.py:318
  64.4 8.9 %collective-permute-start.16 = (bf16[64,3072]{1,0:T(8,128)(2,1)S(1)}, bf16[64,3072]{1,0:T(8,128)(2,1)S(1)}, u32[]{:S(2)}, u32[]{:S(2)}) collective-permute-start(bf16[64,3072]{1,0:T(8,128)(2,1)S(1)} %pad_maximum_fusion.refs_6_), channel_id=1, source_target_pairs={{0,1},{1,0},{2,3},{3,2},{4,5},{5,4},{6,7},{7,6},{8,9},{9,8},{10,11... | collective-permute-start | bytes 1179656 | tf_op jit(solution)/shard_map/ppermute | solution.py:318

commit v9 on v8

--- a/solution.py
+++ b/solution.py
@@ -182,9 +182,9 @@
         x2, slope = gelu_both(z1)
         x2h, x2m, x2l = thirds(x2)
         pieces = dot(jnp.concatenate([x2h, x2m], axis=0), jnp.concatenate([w2h, w2m], axis=1))
-        small = dot(x2h, w2l) + (dot(x2l, w2h) + pieces[both:, both:])
-        medium = pieces[:both, both:] + pieces[both:, :both]
-        z = lane_cat(pieces[:both, :both] + (medium + small)) + b2
+        small = lane_cat(dot(x2h, w2l)) + (lane_cat(dot(x2l, w2h)) + lane_cat(pieces[both:, both:]))
+        medium = lane_cat(pieces[:both, both:]) + lane_cat(pieces[both:, :both])
+        z = lane_cat(pieces[:both, :both]) + (medium + (small + b2))
         scaled = gain_sq * z
         rs = lax.rsqrt(halves(z * z) * (1.0 / d) + ln_eps)
         mean_g = rs * halves(scaled) * (1.0 / d) + u_mean

time: 75.6 us -> 75.6 us (level)
  no operation moved by 1% of the time
where the time goes in v9:
time: 75.6 us; the launch traced here: 75.3 us
  Pallas kernels  18.7 us (25%)
  waiting for transfers between devices  18.6 us (25%)
  blocking collectives  18.1 us (24%)
  starting transfers between devices  15 us (20%)
  local copies, waits for them, and re-layouts  3.91 us (5%)
  between operations  0.88 us (1%)
    ppermute x17, waiting for transfers between devices, swapped(): lax.ppermute(array, axis, [(i, i ^ flip) for i in range(lax.axis_size(axi...  18.6 us
    ppermute x17, starting transfers between devices, swapped(): lax.ppermute(array, axis, [(i, i ^ flip) for i in range(lax.axis_size(axi...  15 us
    pallas_call x1, Pallas kernels, on_device(): pl.pallas_call(partial(chain_kernel, seq_count), out_shape=jax.ShapeDtype...  13.9 us
    all_gather x1, blocking collectives, on_device(): operands = [lax.all_gather(kv, 'seq'), q_early, q_late, ln_gain, ln_bias]  9.33 us
    all_to_all x1, blocking collectives, on_device(): lax.all_to_all(heads, 'row', split_axis=0, concat_axis=0, tiled=True)  8.77 us
    unnamed x20, local copies, waits for them, and re-layouts  3.01 us
    pallas_call x2, Pallas kernels, project(): pl.pallas_call(partial(project_kernel, count, pieces, first), out_shape=o...  2.81 us
    pallas_call x1, Pallas kernels, on_device(): pl.pallas_call(partial(out_kernel, len(w_parts)), out_shape=jax.ShapeDtyp...  1.94 us
  transfers between devices with their start and end apart: 17, of which 2 were waited for; matrix products, arithmetic and copies ran while one was open for 1% of the time, Pallas kernels for 22%

profile of v9, /device:TPU:6, one launch (start us, length us, event | category | flops | bytes accessed | tf_op | source)
XLA Modules:
  0.0 75.3 jit_solution(4798996801704173438)
XLA Ops:
  0.0 2.6 %collective-permute-start = (bf16[2,32,3072]{2,1,0:T(8,128)(2,1)}, bf16[2,32,3072]{2,1,0:T(8,128)(2,1)S(1)}, u32[]{:S(2)}, u32[]{:S(2)}) collective-permute-start(bf16[2,32,3072]{2,1,0:T(8,128)(2,1)} %refs_0_.2), channel_id=1, source_target_pairs={{0,4},{1,5},{2,6},{3,7},{4,0},{5,1},{6,2},{7,3},{8,12},{9,13},{10,... | collective-permute-start | bytes 1179656 | tf_op jit(solution)/shard_map/ppermute | solution.py:318
  2.6 1.6 %collective-permute-start.1 = (bf16[2,32,3072]{2,1,0:T(8,128)(2,1)}, bf16[2,32,3072]{2,1,0:T(8,128)(2,1)S(1)}, u32[]{:S(2)}, u32[]{:S(2)}) collective-permute-start(bf16[2,32,3072]{2,1,0:T(8,128)(2,1)} %refs_0_.2), channel_id=1, source_target_pairs={{0,2},{1,3},{2,0},{3,1},{4,6},{5,7},{6,4},{7,5},{8,10},{9,11},{10,... | collective-permute-start | bytes 1179656 | tf_op jit(solution)/shard_map/ppermute | solution.py:318
  4.2 0.5 collective-permute-start.3
  4.7 0.9 %constant_dynamic-slice_fusion = bf16[16,3072]{1,0:T(8,128)(2,1)S(1)} fusion(bf16[64,3072]{1,0:T(8,128)(2,1)} %refs_0_.3, s32[]{:T(128)S(6)} %select_n.16), kind=kLoop, calls=%fused_computation.2 | loop fusion | bytes 196612 | tf_op jit(solution)/shard_map/dynamic_slice | solution.py:377
  5.6 0.2 collective-permute-start.4
  5.8 17.9 %collective-permute-done.4 = bf16[16,3072]{1,0:T(8,128)(2,1)S(1)} collective-permute-done((bf16[16,3072]{1,0:T(8,128)(2,1)S(1)}, bf16[16,3072]{1,0:T(8,128)(2,1)S(1)}, u32[]{:S(2)}, u32[]{:S(2)}) %collective-permute-start.4) | collective-permute-done | bytes 98336 | tf_op jit(solution)/shard_map/ppermute | solution.py:318
  23.7 0.1 collective-permute-start.7
  23.8 0.5 collective-permute-start.6
  24.3 1.6 %collective-permute-start.5 = (bf16[2,32,3072]{2,1,0:T(8,128)(2,1)S(1)}, bf16[2,32,3072]{2,1,0:T(8,128)(2,1)S(1)}, u32[]{:S(2)}, u32[]{:S(2)}) collective-permute-start(bf16[2,32,3072]{2,1,0:T(8,128)(2,1)S(1)} %collective-permute-done.refs_4_), channel_id=1, source_target_pairs={{0,2},{1,3},{2,0},{3,1},{4,6},{5,7},{6,4},{7,5},{8,10},{9,11},{10,... | collective-permute-start | bytes 1179656 | tf_op jit(solution)/shard_map/ppermute | solution.py:318
  25.9 0.5 collective-permute-start.10
  26.4 1.5 %collective-permute-start.8 = (bf16[16,3072]{1,0:T(8,128)(2,1)S(1)}, bf16[16,3072]{1,0:T(8,128)(2,1)S(1)}, u32[]{:S(2)}, u32[]{:S(2)}) collective-permute-start(bf16[16,3072]{1,0:T(8,128)(2,1)S(1)} %collective-permute-done.4), channel_id=1, source_target_pairs={{0,8},{8,0},{16,24},{24,16},{1,9},{9,1},{17,25},{25,17},{2,10},{10... | collective-permute-start | bytes 294920 | tf_op jit(solution)/shard_map/ppermute | solution.py:318
  27.8 1.5 %collective-permute-start.9 = (bf16[16,3072]{1,0:T(8,128)(2,1)S(1)}, bf16[16,3072]{1,0:T(8,128)(2,1)S(1)}, u32[]{:S(2)}, u32[]{:S(2)}) collective-permute-start(bf16[16,3072]{1,0:T(8,128)(2,1)S(1)} %collective-permute-done.4), channel_id=1, source_target_pairs={{0,16},{8,24},{16,0},{24,8},{1,17},{9,25},{17,1},{25,9},{2,18},{10... | collective-permute-start | bytes 294920 | tf_op jit(solution)/shard_map/ppermute | solution.py:318
  29.4 0.1 pad_add_fusion.ids_ref
  30.1 0.0 copy-start
  30.1 1.3 %copy-done = bf16[192,3072]{1,0:T(8,128)(2,1)S(1)} copy-done((bf16[192,3072]{1,0:T(8,128)(2,1)S(1)}, bf16[192,3072]{1,0:T(8,128)(2,1)}, u32[]{:S(2)}) %copy-start) | copy-done | bytes 1179672
  31.4 1.0 %copy-done.2 = bf16[2,32,3072]{2,1,0:T(8,128)(2,1)S(1)} copy-done((bf16[2,32,3072]{2,1,0:T(8,128)(2,1)S(1)}, bf16[2,32,3072]{2,1,0:T(8,128)(2,1)}, u32[]{:S(2)}) %copy-start.2) | copy-done | bytes 393240
  32.4 0.7 copy-done.5
  33.1 1.5 %project.1 = (bf16[432,128]{1,0:T(8,128)(2,1)S(1)}, bf16[192,128]{1,0:T(8,128)(2,1)S(1)}, bf16[256,3072]{1,0:T(8,128)(2,1)S(1)}) custom-call(s32[3]{0:T(128)S(1)} %pad_add_fusion.ids_ref, bf16[2,32,3072]{2,1,0:T(8,128)(2,1)S(1)} %copy-done.2, bf16[2,32,3072]{2,1,0:T(8,128)(2,1)S(1)} %collective-permute-done.2.refs_1_, ...), custom_call_target="tpu_custom_call" | custom-call | flops 603979776 | bytes 4000000 | tf_op jit(solution)/shard_map/project/pallas_call | solution.py:359
  34.6 0.7 collective-permute-done.5.refs_0_
  35.4 1.6 %collective-permute-start.12 = (bf16[64,3072]{1,0:T(8,128)(2,1)S(1)}, bf16[64,3072]{1,0:T(8,128)(2,1)S(1)}, u32[]{:S(2)}, u32[]{:S(2)}) collective-permute-start(bf16[64,3072]{1,0:T(8,128)(2,1)S(1)} %copy-done.1), channel_id=1, source_target_pairs={{0,2},{1,3},{2,0},{3,1},{4,6},{5,7},{6,4},{7,5},{8,10},{9,11},{10,... | collective-permute-start | bytes 1179656 | tf_op jit(solution)/shard_map/ppermute | solution.py:318
  37.0 2.2 %collective-permute-start.13 = (bf16[64,3072]{1,0:T(8,128)(2,1)S(1)}, bf16[64,3072]{1,0:T(8,128)(2,1)S(1)}, u32[]{:S(2)}, u32[]{:S(2)}) collective-permute-start(bf16[64,3072]{1,0:T(8,128)(2,1)S(1)} %copy-done.1), channel_id=1, source_target_pairs={{0,4},{1,5},{2,6},{3,7},{4,0},{5,1},{6,2},{7,3},{8,12},{9,13},{10,... | collective-permute-start | bytes 1179656 | tf_op jit(solution)/shard_map/ppermute | solution.py:318
  39.2 0.0 copy-start.6
  39.3 0.0 copy-start.7
  39.3 0.0 copy-start.9
  39.3 1.3 %finish.1 = (bf16[576,128]{1,0:T(8,128)(2,1)S(1)}, bf16[64,128]{1,0:T(8,128)(2,1)S(1)}) custom-call(s32[3]{0:T(128)S(1)} %pad_add_fusion.ids_ref, bf16[2,32,3072]{2,1,0:T(8,128)(2,1)S(1)} %collective-permute-done.5.refs_0_, bf16[2,32,3072]{2,1,0:T(8,128)(2,1)S(1)} %collective-permute-done.11.refs_1_, bf16[256,3072]{1,0:T(8,128)(2,1)S(1)} %get-tuple-element.31.refs_2_, ...), custom_call_target="tpu_custom_call" | custom-call | flops 201326592 | bytes 4000000 | tf_op jit(solution)/shard_map/finish/pallas_call | solution.py:359
  40.6 9.3 %all-gather = bf16[2304,128]{1,0:T(8,128)(2,1)S(1)} all-gather(bf16[576,128]{1,0:T(8,128)(2,1)S(1)} %get-tuple-element.33), channel_id=2, replica_groups=mesh['seq'=4,'row'=8] {'seq'}, dimensions={0}, use_global_device_ids=true | all-gather | bytes 737280 | tf_op jit(solution)/shard_map/all_gather | solution.py:400
  50.0 13.9 %chain.1 = bf16[256,128]{1,0:T(8,128)(2,1)S(1)} custom-call(s32[3]{0:T(128)S(1)} %pad_add_fusion.ids_ref, bf16[4,576,128]{2,1,0:T(8,128)(2,1)S(1)} %bitcast.9, bf16[192,128]{1,0:T(8,128)(2,1)S(1)} %get-tuple-element.34.refs_1_, bf16[64,128]{1,0:T(8,128)(2,1)S(1)} %get-tuple-element.35.refs_2_, f32[1,64]{1,0:T(1,128)S(1)} %copy-done.7, ...), custom_call_target="tpu_custom_call" | custom-call | tf_op jit(solution)/shard_map/chain/pallas_call | solution.py:403
  63.9 0.1 collective-permute-start.14
  64.0 0.5 collective-permute-start.15
  64.5 0.1 collective-permute-start.16
  64.6 8.8 %all_to_all.5.heads_ref = bf16[8,32,128]{2,1,0:T(8,128)(2,1)S(1)} all-to-all(bf16[8,32,128]{2,1,0:T(8,128)(2,1)S(1)} %bitcast.10), channel_id=1, replica_groups=mesh['seq'=4,'row'=8] {'row'}, dimensions={0} | all-to-all | bytes 131072 | tf_op jit(solution)/shard_map/all_to_all | solution.py:424
  73.4 1.9 %mix.1 = bf16[2,32,3072]{2,1,0:T(8,128)(2,1)} custom-call(s32[3]{0:T(128)S(1)} %pad_add_fusion.ids_ref, bf16[8,32,128]{2,1,0:T(8,128)(2,1)S(1)} %all_to_all.5.heads_ref, bf16[64,3072]{1,0:T(8,128)(2,1)S(1)} %copy-done.1, bf16[64,3072]{1,0:T(8,128)(2,1)S(1)} %collective-permute-done.3.refs_1_, bf16[64,3072]{1,0:T(8,128)(2,1)S(1)} %collective-permute-done.12.refs_2_, ...), custom_call_target="tpu_custom_call" | custom-call | tf_op jit(solution)/shard_map/mix/pallas_call | solution.py:425
  (31 shorter events, 0.1 us)
Async XLA Ops:
  0.0 23.7 %collective-permute-start = (bf16[2,32,3072]{2,1,0:T(8,128)(2,1)}, bf16[2,32,3072]{2,1,0:T(8,128)(2,1)S(1)}, u32[]{:S(2)}, u32[]{:S(2)}) collective-permute-start(bf16[2,32,3072]{2,1,0:T(8,128)(2,1)} %refs_0_.2), channel_id=1, source_target_pairs={{0,4},{1,5},{2,6},{3,7},{4,0},{5,1},{6,2},{7,3},{8,12},{9,13},{10,... | collective-permute-start | bytes 1179656 | tf_op jit(solution)/shard_map/ppermute | solution.py:318
  2.6 21.1 %collective-permute-start.1 = (bf16[2,32,3072]{2,1,0:T(8,128)(2,1)}, bf16[2,32,3072]{2,1,0:T(8,128)(2,1)S(1)}, u32[]{:S(2)}, u32[]{:S(2)}) collective-permute-start(bf16[2,32,3072]{2,1,0:T(8,128)(2,1)} %refs_0_.2), channel_id=1, source_target_pairs={{0,2},{1,3},{2,0},{3,1},{4,6},{5,7},{6,4},{7,5},{8,10},{9,11},{10,... | collective-permute-start | bytes 1179656 | tf_op jit(solution)/shard_map/ppermute | solution.py:318
  4.2 19.5 %collective-permute-start.2 = (bf16[2,32,3072]{2,1,0:T(8,128)(2,1)}, bf16[2,32,3072]{2,1,0:T(8,128)(2,1)S(1)}, u32[]{:S(2)}, u32[]{:S(2)}) collective-permute-start(bf16[2,32,3072]{2,1,0:T(8,128)(2,1)} %refs_0_.2), channel_id=1, source_target_pairs={{0,1},{1,0},{2,3},{3,2},{4,5},{5,4},{6,7},{7,6},{8,9},{9,8},{10,11... | collective-permute-start | bytes 1179656 | tf_op jit(solution)/shard_map/ppermute | solution.py:318
  4.2 19.5 %collective-permute-start.3 = (bf16[64,3072]{1,0:T(8,128)(2,1)}, bf16[64,3072]{1,0:T(8,128)(2,1)S(1)}, u32[]{:S(2)}, u32[]{:S(2)}) collective-permute-start(bf16[64,3072]{1,0:T(8,128)(2,1)} %refs_0_.3), channel_id=1, source_target_pairs={{0,1},{1,0},{2,3},{3,2},{4,5},{5,4},{6,7},{7,6},{8,9},{9,8},{10,11... | collective-permute-start | bytes 1179656 | tf_op jit(solution)/shard_map/ppermute | solution.py:318
  5.6 18.1 %collective-permute-start.4 = (bf16[16,3072]{1,0:T(8,128)(2,1)S(1)}, bf16[16,3072]{1,0:T(8,128)(2,1)S(1)}, u32[]{:S(2)}, u32[]{:S(2)}) collective-permute-start(bf16[16,3072]{1,0:T(8,128)(2,1)S(1)} %constant_dynamic-slice_fusion), channel_id=1, source_target_pairs={{0,6},{1,7},{2,4},{3,5},{4,2},{5,3},{6,0},{7,1},{8,14},{9,15},{10,... | collective-permute-start | bytes 294920 | tf_op jit(solution)/shard_map/ppermute | solution.py:318
  23.7 4.2 %collective-permute-start.7 = (bf16[2,32,3072]{2,1,0:T(8,128)(2,1)S(1)}, bf16[2,32,3072]{2,1,0:T(8,128)(2,1)S(1)}, u32[]{:S(2)}, u32[]{:S(2)}) collective-permute-start(bf16[2,32,3072]{2,1,0:T(8,128)(2,1)S(1)} %collective-permute-done.refs_4_), channel_id=1, source_target_pairs={{0,1},{1,0},{2,3},{3,2},{4,5},{5,4},{6,7},{7,6},{8,9},{9,8},{10,11... | collective-permute-start | bytes 1179656 | tf_op jit(solution)/shard_map/ppermute | solution.py:318
  23.8 6.3 %collective-permute-start.6 = (bf16[2,32,3072]{2,1,0:T(8,128)(2,1)S(1)}, bf16[2,32,3072]{2,1,0:T(8,128)(2,1)S(1)}, u32[]{:S(2)}, u32[]{:S(2)}) collective-permute-start(bf16[2,32,3072]{2,1,0:T(8,128)(2,1)S(1)} %collective-permute-done.1.refs_2_), channel_id=1, source_target_pairs={{0,1},{1,0},{2,3},{3,2},{4,5},{5,4},{6,7},{7,6},{8,9},{9,8},{10,11... | collective-permute-start | bytes 1179656 | tf_op jit(solution)/shard_map/ppermute | solution.py:318
  24.3 11.1 %collective-permute-start.5 = (bf16[2,32,3072]{2,1,0:T(8,128)(2,1)S(1)}, bf16[2,32,3072]{2,1,0:T(8,128)(2,1)S(1)}, u32[]{:S(2)}, u32[]{:S(2)}) collective-permute-start(bf16[2,32,3072]{2,1,0:T(8,128)(2,1)S(1)} %collective-permute-done.refs_4_), channel_id=1, source_target_pairs={{0,2},{1,3},{2,0},{3,1},{4,6},{5,7},{6,4},{7,5},{8,10},{9,11},{10,... | collective-permute-start | bytes 1179656 | tf_op jit(solution)/shard_map/ppermute | solution.py:318
  25.9 8.7 %collective-permute-start.10 = (bf16[16,3072]{1,0:T(8,128)(2,1)S(1)}, bf16[16,3072]{1,0:T(8,128)(2,1)S(1)}, u32[]{:S(2)}, u32[]{:S(2)}) collective-permute-start(bf16[16,3072]{1,0:T(8,128)(2,1)S(1)} %collective-permute-done.4), channel_id=1, source_target_pairs={{0,24},{8,16},{16,8},{24,0},{1,25},{9,17},{17,9},{25,1},{2,26},{10... | collective-permute-start | bytes 294920 | tf_op jit(solution)/shard_map/ppermute | solution.py:318
  26.4 8.3 %collective-permute-start.8 = (bf16[16,3072]{1,0:T(8,128)(2,1)S(1)}, bf16[16,3072]{1,0:T(8,128)(2,1)S(1)}, u32[]{:S(2)}, u32[]{:S(2)}) collective-permute-start(bf16[16,3072]{1,0:T(8,128)(2,1)S(1)} %collective-permute-done.4), channel_id=1, source_target_pairs={{0,8},{8,0},{16,24},{24,16},{1,9},{9,1},{17,25},{25,17},{2,10},{10... | collective-permute-start | bytes 294920 | tf_op jit(solution)/shard_map/ppermute | solution.py:318
  27.8 6.8 %collective-permute-start.9 = (bf16[16,3072]{1,0:T(8,128)(2,1)S(1)}, bf16[16,3072]{1,0:T(8,128)(2,1)S(1)}, u32[]{:S(2)}, u32[]{:S(2)}) collective-permute-start(bf16[16,3072]{1,0:T(8,128)(2,1)S(1)} %collective-permute-done.4), channel_id=1, source_target_pairs={{0,16},{8,24},{16,0},{24,8},{1,17},{9,25},{17,1},{25,9},{2,18},{10... | collective-permute-start | bytes 294920 | tf_op jit(solution)/shard_map/ppermute | solution.py:318
  30.1 1.3 %copy-start = (bf16[192,3072]{1,0:T(8,128)(2,1)S(1)}, bf16[192,3072]{1,0:T(8,128)(2,1)}, u32[]{:S(2)}) copy-start(bf16[192,3072]{1,0:T(8,128)(2,1)} %refs_6_.2) | copy-start | bytes 3538948
  31.4 1.0 %copy-start.2 = (bf16[2,32,3072]{2,1,0:T(8,128)(2,1)S(1)}, bf16[2,32,3072]{2,1,0:T(8,128)(2,1)}, u32[]{:S(2)}) copy-start(bf16[2,32,3072]{2,1,0:T(8,128)(2,1)} %refs_0_.2) | copy-start | bytes 1179652
  32.4 0.7 copy-start.5
  33.1 2.3 %copy-start.1 = (bf16[64,3072]{1,0:T(8,128)(2,1)S(1)}, bf16[64,3072]{1,0:T(8,128)(2,1)}, u32[]{:S(2)}) copy-start(bf16[64,3072]{1,0:T(8,128)(2,1)} %refs_0_.3) | copy-start | bytes 1179652
  35.4 3.9 %collective-permute-start.11 = (bf16[2,32,3072]{2,1,0:T(8,128)(2,1)S(1)}, bf16[2,32,3072]{2,1,0:T(8,128)(2,1)S(1)}, u32[]{:S(2)}, u32[]{:S(2)}) collective-permute-start(bf16[2,32,3072]{2,1,0:T(8,128)(2,1)S(1)} %collective-permute-done.5.refs_0_), channel_id=1, source_target_pairs={{0,1},{1,0},{2,3},{3,2},{4,5},{5,4},{6,7},{7,6},{8,9},{9,8},{10,11... | collective-permute-start | bytes 1179656 | tf_op jit(solution)/shard_map/ppermute | solution.py:318
  35.4 28.5 %collective-permute-start.12 = (bf16[64,3072]{1,0:T(8,128)(2,1)S(1)}, bf16[64,3072]{1,0:T(8,128)(2,1)S(1)}, u32[]{:S(2)}, u32[]{:S(2)}) collective-permute-start(bf16[64,3072]{1,0:T(8,128)(2,1)S(1)} %copy-done.1), channel_id=1, source_target_pairs={{0,2},{1,3},{2,0},{3,1},{4,6},{5,7},{6,4},{7,5},{8,10},{9,11},{10,... | collective-permute-start | bytes 1179656 | tf_op jit(solution)/shard_map/ppermute | solution.py:318
  37.0 26.9 %collective-permute-start.13 = (bf16[64,3072]{1,0:T(8,128)(2,1)S(1)}, bf16[64,3072]{1,0:T(8,128)(2,1)S(1)}, u32[]{:S(2)}, u32[]{:S(2)}) collective-permute-start(bf16[64,3072]{1,0:T(8,128)(2,1)S(1)} %copy-done.1), channel_id=1, source_target_pairs={{0,4},{1,5},{2,6},{3,7},{4,0},{5,1},{6,2},{7,3},{8,12},{9,13},{10,... | collective-permute-start | bytes 1179656 | tf_op jit(solution)/shard_map/ppermute | solution.py:318
  39.2 10.7 %copy-start.3 = (f32[1,64,256]{2,1,0:T(8,128)S(1)}, f32[1,64,256]{2,1,0:T(8,128)}, u32[]{:S(2)}) copy-start(f32[1,64,256]{2,1,0:T(8,128)} %refs_5_.1) | copy-start | bytes 196612
  39.2 10.7 %copy-start.4 = (f32[1,256,64]{1,2,0:T(8,128)S(1)}, f32[1,256,64]{1,2,0:T(8,128)}, u32[]{:S(2)}) copy-start(f32[1,256,64]{1,2,0:T(8,128)} %param.18) | copy-start | bytes 196612
  39.2 10.7 %copy-start.6 = (f32[1,256]{1,0:T(1,128)S(1)}, f32[1,256]{1,0:T(1,128)}, u32[]{:S(2)}) copy-start(f32[1,256]{1,0:T(1,128)} %refs_6_.3) | copy-start | bytes 3076
  39.3 10.7 %copy-start.7 = (f32[1,64]{1,0:T(1,128)S(1)}, f32[1,64]{1,0:T(1,128)}, u32[]{:S(2)}) copy-start(f32[1,64]{1,0:T(1,128)} %refs_3_.1) | copy-start | bytes 772
  39.3 10.7 %copy-start.8 = (f32[1,64]{1,0:T(1,128)S(1)}, f32[1,64]{1,0:T(1,128)}, u32[]{:S(2)}) copy-start(f32[1,64]{1,0:T(1,128)} %refs_4_.1) | copy-start | bytes 772
  39.3 10.7 %copy-start.9 = (f32[1,64]{1,0:T(1,128)S(1)}, f32[1,64]{1,0:T(1,128)}, u32[]{:S(2)}) copy-start(f32[1,64]{1,0:T(1,128)} %refs_8_.1) | copy-start | bytes 772
  63.9 9.4 %collective-permute-start.14 = (bf16[64,3072]{1,0:T(8,128)(2,1)S(1)}, bf16[64,3072]{1,0:T(8,128)(2,1)S(1)}, u32[]{:S(2)}, u32[]{:S(2)}) collective-permute-start(bf16[64,3072]{1,0:T(8,128)(2,1)S(1)} %collective-permute-done.12.refs_2_), channel_id=1, source_target_pairs={{0,1},{1,0},{2,3},{3,2},{4,5},{5,4},{6,7},{7,6},{8,9},{9,8},{10,11... | collective-permute-start | bytes 1179656 | tf_op jit(solution)/shard_map/ppermute | solution.py:318
  64.0 9.4 %collective-permute-start.15 = (bf16[64,3072]{1,0:T(8,128)(2,1)S(1)}, bf16[64,3072]{1,0:T(8,128)(2,1)S(1)}, u32[]{:S(2)}, u32[]{:S(2)}) collective-permute-start(bf16[64,3072]{1,0:T(8,128)(2,1)S(1)} %collective-permute-done.13.refs_4_), channel_id=1, source_target_pairs={{0,1},{1,0},{2,3},{3,2},{4,5},{5,4},{6,7},{7,6},{8,9},{9,8},{10,11... | collective-permute-start | bytes 1179656 | tf_op jit(solution)/shard_map/ppermute | solution.py:318
  64.5 8.9 %collective-permute-start.16 = (bf16[64,3072]{1,0:T(8,128)(2,1)S(1)}, bf16[64,3072]{1,0:T(8,128)(2,1)S(1)}, u32[]{:S(2)}, u32[]{:S(2)}) collective-permute-start(bf16[64,3072]{1,0:T(8,128)(2,1)S(1)} %pad_maximum_fusion.refs_6_), channel_id=1, source_target_pairs={{0,1},{1,0},{2,3},{3,2},{4,5},{5,4},{6,7},{7,6},{8,9},{9,8},{10,11... | collective-permute-start | bytes 1179656 | tf_op jit(solution)/shard_map/ppermute | solution.py:318
